TPU v7x, 32 devices: a whole 2x2x4 slice. The times are simulated.
32 devices in a mesh: dp: 8 (over z, y), sp: 4 (over x, core).
Axes of the slice: x: 2, y: 2, z: 4, core: 2. Of those that a mesh axis runs over, the one named last changes fastest.
Arguments:
- normed: bfloat16 [4096, 2560], P(('dp', 'sp')), may hold values from -6 to 6
- w_query: bfloat16 [2560, 4096], P(None, 'sp'), may hold values from -0.125 to 0.125
- key_weight: bfloat16 [2560, 512], P(None, 'sp'), may hold values from -0.125 to 0.125
- value_weight: bfloat16 [2560, 512], P(None, 'sp'), may hold values from -0.125 to 0.125
- q_gain: float32 [128], replicated, may hold values from 0.25 to 1.75
- key_norm_gain: float32 [128], replicated, may hold values from 0.25 to 1.75
- ctx_grad: bfloat16 [4096, 4096], P(('dp', 'sp')), may hold values from -6 to 6
- lengths: int32 [8], P('dp'), may hold values from 64 to 512, as said below
Outputs:
- normed_input_gradient: bfloat16 [4096, 2560], P(('dp', 'sp'))
- grad_w_query: float32 [2560, 4096], P('dp', 'sp')
- grad_w_key: float32 [2560, 512], P('dp', 'sp')
- grad_w_value: float32 [2560, 512], P('dp', 'sp')
Inputs may be any that keep to these rules, and one draw needn't show every extreme that they name: `lengths`: in every draw some response has its whole span valid and some only one eighth of 512.
All inputs are finite; a program needn't handle non-finite values.
Results may differ from a plain program's by a relative error of at most 0.008.
Values may be sent and summed in bfloat16 or wider, within the bound.
No kernel may reach another device: no remote copies, remote signals or barrier semaphores. Data moves between devices by JAX's collectives and lax.ppermute only.
A program may use at most 128 MiB of HBM per device.

v0:
```python
import math

import jax
import jax.numpy as jnp
from jax import lax
from jax.sharding import PartitionSpec as P

epsilon = 1e-06
log_base = math.log(1000000.0)


def angle_tables(length, width):
    position = jnp.arange(length, dtype=jnp.int32).astype(jnp.float32)
    freqs = jnp.exp(jnp.arange(width // 2, dtype=jnp.float32) * (-2.0 * log_base / width))
    angles = position[:, None] * freqs[None, :]
    cosine_table = jnp.cos(angles)
    sine_values = jnp.sin(angles)
    return (
        jnp.concatenate([cosine_table, cosine_table], 1),
        jnp.concatenate([sine_values, sine_values], 1),
    )


def turned(values):
    half = values.shape[-1] // 2
    return jnp.concatenate([-values[..., half:], values[..., :half]], -1)


def rotate_pairs(values, cosine_table, sine_values):
    return values * cosine_table + turned(values) * sine_values


def inverse_rotation(grads, cosine_table, sine_values):
    return grads * cosine_table - turned(grads) * sine_values


def normalize(values, gain):
    inverse = lax.rsqrt(jnp.mean(values * values, -1, keepdims=True) + epsilon)
    return (values * inverse * gain, inverse)


def head_norm_gradient(values, inverse, gain, grads):
    weighted = gain * grads
    return inverse * weighted - values * (inverse * inverse * inverse) * jnp.mean(
        values * weighted, -1, keepdims=True
    )


def column_product(span, grads):
    return lax.dot_general(
        span, grads, (((0,), (0,)), ((), ())), preferred_element_type=jnp.float32
    )


def local(normed, w_query, key_weight, value_weight, q_gain, key_norm_gain, ctx_grad, lengths):
    span = lax.all_gather(normed, "sp", axis=0, tiled=True)
    length = span.shape[0]
    head_dim = q_gain.shape[0]
    query_heads = w_query.shape[1] // head_dim
    pair_heads = key_weight.shape[1] // head_dim
    group_size = query_heads // pair_heads
    scale_factor = head_dim ** (-0.5)
    cosine_table, sine_values = angle_tables(length, head_dim)
    q_proj = jnp.dot(span, w_query, preferred_element_type=jnp.float32).reshape(
        length, query_heads, head_dim
    )
    key_projected = jnp.dot(span, key_weight, preferred_element_type=jnp.float32).reshape(
        length, pair_heads, head_dim
    )
    value_row_block = (
        jnp.dot(span, value_weight, preferred_element_type=jnp.float32)
        .astype(jnp.bfloat16)
        .reshape(length, pair_heads, head_dim)
    )
    q_normed, q_inverse = normalize(q_proj, q_gain)
    k_normed, key_inverse_norm = normalize(key_projected, key_norm_gain)
    query_matrix = rotate_pairs(q_normed, cosine_table[:, None, :], sine_values[:, None, :]).astype(
        jnp.bfloat16
    )
    key_rows = rotate_pairs(k_normed, cosine_table[:, None, :], sine_values[:, None, :]).astype(
        jnp.bfloat16
    )
    output_gradient = lax.all_to_all(ctx_grad, "sp", split_axis=1, concat_axis=0, tiled=True)
    positions = jnp.arange(length, dtype=jnp.int32)
    unmasked_rows = positions < lengths[0]
    output_gradient = jnp.where(
        unmasked_rows[:, None], output_gradient, jnp.zeros((), jnp.bfloat16)
    ).reshape(length, query_heads, head_dim)
    allowed = (positions[None, :] <= positions[:, None]) & unmasked_rows[None, :]
    key_sums = [jnp.zeros((length, head_dim), jnp.float32)]
    value_sums = [jnp.zeros((length, head_dim), jnp.float32)]
    query_parts = []
    for head_index in range(query_heads):
        pair_index = head_index // group_size
        q_head = query_matrix[:, head_index]
        k_head = key_rows[:, pair_index]
        v_head = value_row_block[:, pair_index]
        o_grad = output_gradient[:, head_index]
        scores = (
            lax.dot_general(
                q_head, k_head, (((1,), (1,)), ((), ())), preferred_element_type=jnp.float32
            )
            * scale_factor
        )
        weights = jnp.where(allowed, jnp.exp(scores), jnp.zeros((), jnp.float32))
        probs = weights / jnp.sum(weights, -1, keepdims=True)
        probabilities_reduced = probs.astype(jnp.bfloat16)
        context = jnp.dot(probabilities_reduced, v_head, preferred_element_type=jnp.float32)
        delta = jnp.sum(o_grad.astype(jnp.float32) * context, -1, keepdims=True)
        dprob = lax.dot_general(
            o_grad, v_head, (((1,), (1,)), ((), ())), preferred_element_type=jnp.float32
        )
        dscore = (probs * (dprob - delta)).astype(jnp.bfloat16)
        dq_rot = jnp.dot(dscore, k_head, preferred_element_type=jnp.float32) * scale_factor
        key_sums[pair_index] = (
            key_sums[pair_index]
            + lax.dot_general(
                dscore, q_head, (((0,), (0,)), ((), ())), preferred_element_type=jnp.float32
            )
            * scale_factor
        )
        value_sums[pair_index] = value_sums[pair_index] + lax.dot_general(
            probabilities_reduced,
            o_grad,
            (((0,), (0,)), ((), ())),
            preferred_element_type=jnp.float32,
        )
        head_grad = head_norm_gradient(
            q_proj[:, head_index],
            q_inverse[:, head_index],
            q_gain,
            inverse_rotation(dq_rot, cosine_table, sine_values),
        ).astype(jnp.bfloat16)
        query_parts.append(head_grad)
    query_grad = jnp.stack(query_parts, 1).reshape(length, query_heads * head_dim)
    rotated_key_gradient = jnp.stack(key_sums, 1)
    key_gradient = (
        head_norm_gradient(
            key_projected,
            key_inverse_norm,
            key_norm_gain,
            inverse_rotation(
                rotated_key_gradient, cosine_table[:, None, :], sine_values[:, None, :]
            ),
        )
        .astype(jnp.bfloat16)
        .reshape(length, pair_heads * head_dim)
    )
    value_gradient = (
        jnp.stack(value_sums, 1).astype(jnp.bfloat16).reshape(length, pair_heads * head_dim)
    )
    total = lax.dot_general(
        query_grad, w_query, (((1,), (1,)), ((), ())), preferred_element_type=jnp.float32
    )
    total = total + lax.dot_general(
        key_gradient, key_weight, (((1,), (1,)), ((), ())), preferred_element_type=jnp.float32
    )
    normed_input_gradient = lax.psum_scatter(
        total
        + lax.dot_general(
            value_gradient,
            value_weight,
            (((1,), (1,)), ((), ())),
            preferred_element_type=jnp.float32,
        ),
        "sp",
        scatter_dimension=0,
        tiled=True,
    ).astype(jnp.bfloat16)
    pair_width = pair_heads * head_dim
    all_grads = jnp.concatenate([query_grad, key_gradient, value_gradient], 1)
    everything = lax.psum_scatter(
        column_product(span, all_grads), "dp", scatter_dimension=0, tiled=True
    )
    query_width = query_heads * head_dim
    grad_w_query = everything[:, :query_width]
    grad_w_key = everything[:, query_width : query_width + pair_width]
    grad_w_value = everything[:, query_width + pair_width :]
    return (normed_input_gradient, grad_w_query, grad_w_key, grad_w_value)


def solution(mesh):
    in_specs = (
        P(("dp", "sp"), None),
        P(None, "sp"),
        P(None, "sp"),
        P(None, "sp"),
        P(),
        P(),
        P(("dp", "sp"), None),
        P("dp"),
    )
    out_specs = (P(("dp", "sp"), None), P("dp", "sp"), P("dp", "sp"), P("dp", "sp"))
    return jax.shard_map(local, mesh=mesh, in_specs=in_specs, out_specs=out_specs, check_vma=False)
```

profile of v0, /device:TPU:0, one launch (start us, length us, event | category | flops | bytes accessed | tf_op | source)
XLA Modules:
  0.0 396.0 jit_solution(14019135251379671178)
XLA Ops:
  7.2 0.7 all-gather.2.cloned.1.call-update
  7.9 2.3 copy.86
  10.2 4.2 %all-to-all-start = ((bf16[128,4,1024]{0,2,1:T(8,128)(2,1)}), bf16[128,4,1024]{0,2,1:T(8,128)(2,1)S(1)}, u32[]{:S(2)}, u32[]{:S(2)}) async-start(bf16[128,4,1024]{0,2,1:T(8,128)(2,1)} %bitcast.7), calls=%async_computation | async-start | bytes 2097152 | tf_op jit(solution)/shard_map/all_to_all | solution.py:83
  15.6 20.4 %all-to-all-done = bf16[128,4,1024]{0,2,1:T(8,128)(2,1)S(1)} async-done(((bf16[128,4,1024]{0,2,1:T(8,128)(2,1)}), bf16[128,4,1024]{0,2,1:T(8,128)(2,1)S(1)}, u32[]{:S(2)}, u32[]{:S(2)}) %all-to-all-start) | async-done | bytes 1048608 | tf_op jit(solution)/shard_map/all_to_all | solution.py:83
  36.0 0.8 copy.87
  37.3 1.0 broadcast_select_fusion
  38.3 6.1 %all-gather.2.cloned.1.call-done = bf16[512,2560]{1,0:T(8,128)(2,1)} async-done(((bf16[128,2560]{1,0:T(8,128)(2,1)}), bf16[512,2560]{1,0:T(8,128)(2,1)}) %all-gather.2.cloned.1.call-update) | async-done | bytes 2621456 | tf_op jit(solution)/shard_map/all_gather | solution.py:56
  44.4 5.6 %fusion.168 = f32[512,1024]{1,0:T(8,128)S(1)} fusion(bf16[512,2560]{1,0:T(8,128)(2,1)} %all-gather.2.cloned.1.call-done, bf16[2560,1024]{1,0:T(8,128)(2,1)} %param.9), kind=kOutput, calls=%fused_computation.293 | convolution fusion | flops 2684354560 | bytes 9961472 | tf_op jit(solution)/shard_map/dot_general | solution.py:64
  50.5 1.3 multiply_reduce_fusion
  51.8 2.5 fusion.157
  54.4 1.0 multiply_reduce_fusion.2
  55.6 0.9 pad_maximum_fusion
  56.4 1.8 copy.84
  58.2 1.8 copy.85
  60.0 1.0 copy.82
  61.1 0.7 fusion
  61.8 0.7 slice_negate_fusion
  62.8 1.4 fusion.2
  64.3 1.4 fusion.160
  65.7 1.4 fusion.162
  67.1 1.4 fusion.164
  68.5 1.4 fusion.166
  69.9 1.4 fusion.167
  71.3 1.5 fusion.165
  72.8 1.4 fusion.163
  74.7 2.2 fusion.131
  76.9 0.8 convolution_convert_fusion
  77.8 1.2 fusion.42
  79.0 1.2 fusion.39
  80.6 1.0 fusion.130
  82.4 1.1 copy.118
  83.5 0.8 copy.117
  84.4 1.1 copy.123
  85.5 1.7 fusion.49
  88.0 0.7 copy-done.26
  91.1 0.7 copy-done.28
  99.8 0.9 copy-done.2
  106.1 3.0 fusion.169
  109.2 0.9 fusion.170
  110.3 3.3 add_add_fusion
  113.6 1.1 copy-done.21
  114.8 10.7 %convolution_bitcast_fusion = f32[2560,1280]{0,1:T(8,128)} fusion(bf16[512,2560]{1,0:T(8,128)(2,1)} %all-gather.2.cloned.1.call-done, bf16[512,128]{0,1:T(8,128)(2,1)S(1)} %fusion.41, bf16[512,128]{0,1:T(8,128)(2,1)S(1)} %subtract_convert_fusion, bf16[512,1024]{0,1:T(8,128)(2,1)S(1)} %bitcast.377), kind=kOutput, calls=%fused_computation | convolution fusion | flops 3359375360 | bytes 17039360 | tf_op jit(solution)/shard_map/dot_general | solution.py:50
  125.5 14.2 %copy.115 = f32[2560,1280]{1,0:T(8,128)} copy(f32[2560,1280]{0,1:T(8,128)} %convolution_bitcast_fusion) | data formatting | bytes 26214400
  139.7 26.5 %reduce-scatter.5.cloned.1.call-done = f32[128,2560]{1,0:T(8,128)} async-done(((f32[512,2560]{1,0:T(8,128)}), f32[128,2560]{1,0:T(8,128)}) %reduce-scatter.5.cloned.1.call-update) | async-done | bytes 1310736 | tf_op jit(solution)/shard_map/reduce_scatter | solution.py:158
  166.2 2.2 convert_element_type.168
  168.4 216.8 %reduce-scatter.7.cloned.1.call-done = f32[320,1280]{1,0:T(8,128)} async-done(((f32[2560,1280]{1,0:T(8,128)}), f32[320,1280]{1,0:T(8,128)}) %reduce-scatter.7.cloned.1.call-update) | async-done | bytes 1638416
  385.2 1.7 fusion.158
  387.0 2.5 slice.282
  (159 shorter events, 20.0 us)
Async XLA Ops:
  7.2 47.2 %copy-start = (bf16[2560,128]{1,0:T(8,128)(2,1)S(1)}, bf16[2560,128]{1,0:T(8,128)(2,1)}, u32[]{:S(2)}) copy-start(bf16[2560,128]{1,0:T(8,128)(2,1)} %param.10) | copy-start | bytes 1966084
  7.2 37.3 %all-gather.2.cloned.1.call-start = ((), (), s32[]{:S(2)}) async-start(), calls=%async_computation.3 | async-start | bytes 3276800 | tf_op jit(solution)/shard_map/all_gather | solution.py:56
  10.2 25.8 %all-to-all-start = ((bf16[128,4,1024]{0,2,1:T(8,128)(2,1)}), bf16[128,4,1024]{0,2,1:T(8,128)(2,1)S(1)}, u32[]{:S(2)}, u32[]{:S(2)}) async-start(bf16[128,4,1024]{0,2,1:T(8,128)(2,1)} %bitcast.7), calls=%async_computation | async-start | bytes 2097152 | tf_op jit(solution)/shard_map/all_to_all | solution.py:83
  14.4 151.8 %reduce-scatter.5.cloned.1.call-start = ((), (), s32[]{:S(2)}) async-start(), calls=%async_computation.4 | async-start | bytes 6553600 | tf_op jit(solution)/shard_map/reduce_scatter | solution.py:158
  51.8 2.5 copy-start.3
  54.4 1.1 copy-start.22
  55.4 5.7 %copy-start.19 = (f32[128]{0:T(128)S(1)}, f32[128]{0:T(128)}, u32[]{:S(2)}) copy-start(f32[128]{0:T(128)} %param.12) | copy-start | bytes 1540
  61.8 1.0 copy-start.13
  61.8 1.0 copy-start.14
  64.3 16.3 %copy-start.1 = (bf16[512,8,128]{2,0,1:T(8,128)(2,1)}, bf16[512,8,128]{2,0,1:T(8,128)(2,1)S(1)}, u32[]{:S(2)}) copy-start(bf16[512,8,128]{2,0,1:T(8,128)(2,1)S(1)} %fusion.2) | copy-start | bytes 3145732
  74.2 2.7 copy-start.4
  74.2 2.7 copy-start.16
  77.8 1.3 copy-start.23
  79.0 2.6 copy-start.12
  80.3 1.6 copy-start.11
  80.3 1.7 copy-start.10
  80.3 1.9 copy-start.9
  80.3 2.0 copy-start.8
  80.6 3.0 copy-start.7
  85.5 1.8 copy-start.6
  85.5 1.8 copy-start.24
  85.5 2.0 copy-start.25
  87.5 1.2 copy-start.26
  89.0 1.2 copy-start.27
  90.5 1.2 copy-start.28
  92.0 1.2 copy-start.29
  93.5 1.2 copy-start.30
  95.0 1.2 copy-start.31
  96.6 1.0 copy-start.18
  99.4 1.2 copy-start.2
  99.4 1.3 copy-start.15
  103.3 1.0 copy-start.5
  103.3 2.3 slice-start
  104.3 1.8 slice-start.1
  105.3 3.8 copy-start.20
  109.2 1.1 copy-start.17
  113.6 1.2 copy-start.21
  113.6 271.6 %reduce-scatter.7.cloned.1.call-start = ((), (), s32[]{:S(2)}) async-start(), calls=%async_computation.5 | async-start | bytes 14745600
Sparse Core Ops, SparseCore 0:
  9.6 34.8 all-gather.1
  113.7 52.4 reduce-scatter.4
  170.3 214.9 reduce-scatter.6
where the time goes:
time: 397 us; the launch traced here: 396 us
  waiting for transfers between devices  271 us (68%)
  matrix products  52.9 us (13%)
  local copies, waits for them, and re-layouts  41.8 us (11%)
  between operations  15.3 us (4%)
  other arithmetic  11.1 us (3%)
  starting transfers between devices  4.29 us (1%)
    unnamed x4, waiting for transfers between devices  218 us
    unnamed x79, local copies, waits for them, and re-layouts  29.1 us
    reduce_scatter x1, waiting for transfers between devices, local(): lax.psum_scatter(total + lax.dot_general(value_gradient, value_weight, ((...  26.5 us
    all_to_all x1, waiting for transfers between devices, local(): lax.all_to_all(ctx_grad, 'sp', split_axis=1, concat_axis=0, tiled=True)  20.4 us
    dot_general x1, matrix products, column_product(): lax.dot_general(span, grads, (((0,), (0,)), ((), ())), preferred_element_...  10.7 us
    dot_general x8, matrix products, local(): lax.dot_general(q_head, k_head, (((1,), (1,)), ((), ())), preferred_eleme...  10.3 us
  transfers between devices with their start and end apart: 4, of which 4 were waited for; matrix products, arithmetic and copies ran while one was open for 8% of the time, Pallas kernels for 0%

commit v1 on v0

v1 whole, which is shorter than its diff:
```python
import functools
import math

import jax
import jax.numpy as jnp
from jax import lax
from jax.experimental import pallas as pl
from jax.experimental.pallas import tpu as pltpu
from jax.sharding import PartitionSpec as P

epsilon = 1e-06
log_base = math.log(1000000.0)
bf16 = jnp.bfloat16
f32 = jnp.float32
MIB = 1024 * 1024


def cost(flops):
    return pl.CostEstimate(flops=int(flops), bytes_accessed=1024, transcendentals=0)


def waiting(deps, kernel, first=0):
    def body(*refs):
        return kernel(*refs[:first], *refs[first + len(deps) :])

    return body


ANY = pl.BlockSpec(memory_space=pl.ANY)


def angle_tables(length, width):
    position = jnp.arange(length, dtype=jnp.int32).astype(f32)
    freqs = jnp.exp(jnp.arange(width // 2, dtype=f32) * (-2.0 * log_base / width))
    angles = position[:, None] * freqs[None, :]
    cosine = jnp.cos(angles)
    sine = jnp.sin(angles)
    return jnp.concatenate([cosine, cosine], 1), jnp.concatenate([-sine, sine], 1)


def exchange(value, axis, size, bit):
    return lax.ppermute(value, axis, [(d, d ^ bit) for d in range(size)])


def roll_half(a):
    return pltpu.roll(a, a.shape[-1] // 2, a.ndim - 1)


def norm_gradient(values, gain, grads):
    inverse = lax.rsqrt(jnp.mean(values * values, -1, keepdims=True) + epsilon)
    weighted = gain * grads
    mean = jnp.mean(values * weighted, -1, keepdims=True)
    return inverse * weighted - values * (inverse * inverse * inverse * mean)


def projection_kernel(me, s0, s1, wq, wk, wv, q_gain, k_gain, cosine, signed, *rest):
    q_out, u_out, k_out, kp_out, v_out, span = rest[-6:]
    step = pl.program_id(0)
    rows = s0.shape[0]
    width = q_gain.shape[1]

    def normed_rotated(u, gain):
        inverse = lax.rsqrt(jnp.mean(u * u, -1, keepdims=True) + epsilon)
        a = u * inverse * gain
        return (a * cosine[...] + roll_half(a) * signed[...]).astype(bf16)

    @pl.when(step == 0)
    def _():
        for m, s in enumerate((s0, s1)):
            at = pl.multiple_of(((me[0] & 1) ^ m) * rows, rows)
            span[pl.ds(at, rows), :] = s[...]
        both = jnp.concatenate([wk[...], wv[...]], 1)
        kv = jnp.dot(span[...], both, preferred_element_type=f32)
        kp_out[...] = kv[:, :width]
        k_out[...] = normed_rotated(kv[:, :width], k_gain[...])
        v_out[...] = kv[:, width:].astype(bf16)

    @pl.when(step > 0)
    def _():
        u = jnp.dot(span[...], wq[...], preferred_element_type=f32)
        u_out[...] = u
        for h in range(u.shape[1] // width):
            part = slice(h * width, (h + 1) * width)
            q_out[:, part] = normed_rotated(u[:, part], q_gain[...])


def projections(me, flip, pair, wq, wk, wv, q_gain, k_gain, cosine, signed, block, previous):
    rows, features = pair[0].shape
    length = cosine.shape[0]
    half = 2 * rows
    columns, width = wq.shape[1], wk.shape[1]
    steps = columns // block + 1

    def whole(a):
        return pl.BlockSpec(a.shape, lambda i, me: (0, 0))

    def rows_of(me):
        return (me[0] >> 1) ^ flip

    def column_of(i):
        return jnp.maximum(i - 1, 0)

    table = pl.BlockSpec((half, width), lambda i, me: (rows_of(me), 0))
    wide = pl.BlockSpec((half, block), lambda i, me: (rows_of(me), column_of(i)))
    shape = jax.ShapeDtypeStruct
    inputs = (me, *pair, wq, wk, wv, q_gain, k_gain, cosine, signed)
    return pl.pallas_call(
        projection_kernel,
        grid_spec=pltpu.PrefetchScalarGridSpec(
            num_scalar_prefetch=1,
            grid=(steps,),
            in_specs=[whole(s) for s in pair]
            + [pl.BlockSpec((features, block), lambda i, me: (0, column_of(i)))]
            + [whole(a) for a in (wk, wv, q_gain, k_gain)]
            + [table, table]
            + [pl.BlockSpec(memory_space=pl.ANY)] * len(previous),
            out_specs=[wide, wide, table, table, table],
            scratch_shapes=[pltpu.VMEM((half, features), bf16)],
        ),
        out_shape=[
            shape((length, columns), bf16),
            shape((length, columns), f32),
            shape((length, width), bf16),
            shape((length, width), f32),
            shape((length, width), bf16),
        ],
        input_output_aliases={len(inputs) + n: n for n in range(len(previous))},
        compiler_params=pltpu.CompilerParams(vmem_limit_bytes=40 * MIB),
        cost_estimate=cost(2 * half * features * (columns + 2 * width)),
        name="projections",
    )(*inputs, *previous)


def transpose_kernel(me, s0, s1, out):
    rows = s0.shape[0]
    for m, s in enumerate((s0, s1)):
        at = pl.multiple_of(((me[0] & 1) ^ m) * rows, rows)
        out[:, pl.ds(at, rows)] = s[...].T


def transposed(me, pair, deps=()):
    rows, features = pair[0].shape
    block = features
    for size in (256, 128):
        if features % size == 0:
            block = size
            break
    return pl.pallas_call(
        waiting(deps, transpose_kernel),
        grid=(features // block,),
        in_specs=[ANY] * len(deps)
        + [pl.BlockSpec(memory_space=pltpu.SMEM)]
        + [pl.BlockSpec((rows, block), lambda i: (0, i))] * 2,
        out_specs=pl.BlockSpec((block, 2 * rows), lambda i: (i, 0)),
        out_shape=jax.ShapeDtypeStruct((features, 2 * rows), bf16),
        compiler_params=pltpu.CompilerParams(vmem_limit_bytes=32 * MIB),
        cost_estimate=cost(2 * rows * features * 512),
        name="transposed",
    )(*deps, me, *pair)


def attention_kernel(
    tile, me, lengths, q, u, k, v, c0, c1, c2, c3, q_gain, cosine, signed,
    dk_in, dv_in, kp, k_gain, qg_out, dk_out, dv_out, d_out,
):
    length, width = k.shape
    heads = q.shape[1] // width
    rows = c0.shape[0]
    scale = width ** (-0.5)
    constant = scale * math.log2(math.e)
    valid = lengths[0]
    for m, c in enumerate((c0, c1, c2, c3)):
        at = pl.multiple_of((me[0] ^ m) * rows, rows)
        position = lax.broadcasted_iota(jnp.int32, c.shape, 0) + at
        kept = jnp.where(position < valid, c[...].astype(f32), 0.0)
        d_out[pl.ds(at, rows), :] = kept.astype(bf16)
    dk_out[...] = dk_in[...]
    dv_out[...] = dv_in[...]
    for block in range(length // tile):
        here = slice(block * tile, (block + 1) * tile)
        seen = slice(0, (block + 1) * tile)
        keys = lax.broadcasted_iota(jnp.int32, ((block + 1) * tile, tile), 0)
        queries = lax.broadcasted_iota(jnp.int32, ((block + 1) * tile, tile), 1) + block * tile
        allowed = (keys <= queries) & (keys < valid)
        for h in range(heads):
            part = slice(h * width, (h + 1) * width)
            q_head = q[here, part]
            o_grad = d_out[here, part]
            scores = lax.dot_general(
                k[seen, :], q_head, (((1,), (1,)), ((), ())), preferred_element_type=f32
            )
            weights = jnp.where(allowed, jnp.exp2(scores * constant), 0.0)
            probs = weights * (1.0 / jnp.sum(weights, 0, keepdims=True))
            low = probs.astype(bf16)
            dprob = lax.dot_general(
                v[seen, :], o_grad, (((1,), (1,)), ((), ())), preferred_element_type=f32
            )
            delta = jnp.sum(low.astype(f32) * dprob, 0, keepdims=True)
            dscore = (probs * (dprob - delta)).astype(bf16)
            dq = lax.dot_general(
                dscore, k[seen, :], (((0,), (0,)), ((), ())), preferred_element_type=f32
            ) * scale
            dk_out[seen, :] += jnp.dot(dscore, q_head, preferred_element_type=f32)
            dv_out[seen, :] += jnp.dot(low, o_grad, preferred_element_type=f32)
            back = dq * cosine[here, :] - roll_half(dq) * signed[here, :]
            qg_out[here, part] = norm_gradient(u[here, part], q_gain[...], back).astype(bf16)


def attention_last_kernel(tile, *refs):
    *inputs, qg_out, kv_out, d_out, dk_out, dv_out = refs
    attention_kernel(tile, *inputs, qg_out, dk_out, dv_out, d_out)
    cosine, signed, _, _, kp, k_gain = inputs[-6:]
    width = kp.shape[1]
    scale = width ** (-0.5)
    dk = dk_out[...] * scale
    back = dk * cosine[...] - roll_half(dk) * signed[...]
    kv_out[:, :width] = norm_gradient(kp[...], k_gain[...], back).astype(bf16)
    kv_out[:, width:] = dv_out[...].astype(bf16)


def attention(group, last, block, me, lengths, q, u, k, v, cs, q_gain, cosine, signed, dk, dv, kp, k_gain, deps):
    length, width = k.shape
    rows = cs[0].shape[0]
    tile = min(256, length)

    def whole(a):
        return pl.BlockSpec(a.shape, lambda i: (0, 0))

    part = pl.BlockSpec((length, block), lambda i: (0, group))
    out = pl.BlockSpec((length, block), lambda i: (0, 0))
    sums = pl.BlockSpec((length, width), lambda i: (0, 0))
    shape = jax.ShapeDtypeStruct
    if last:
        kernel = functools.partial(attention_last_kernel, tile)
        out_specs = [out, pl.BlockSpec((length, 2 * width), lambda i: (0, 0))]
        out_shape = [shape((length, block), bf16), shape((length, 2 * width), bf16)]
        scratch = [pltpu.VMEM((length, block), bf16)] + [pltpu.VMEM((length, width), f32)] * 2
    else:
        kernel = functools.partial(attention_kernel, tile)
        out_specs = [out, sums, sums]
        out_shape = [shape((length, block), bf16)] + [shape((length, width), f32)] * 2
        scratch = [pltpu.VMEM((length, block), bf16)]
    heads = block // width
    return pl.pallas_call(
        waiting(deps, kernel),
        grid=(1,),
        in_specs=[ANY] * len(deps)
        + [pl.BlockSpec(memory_space=pltpu.SMEM)] * 2
        + [part, part, whole(k), whole(v)]
        + [pl.BlockSpec((rows, block), lambda i: (0, group))] * len(cs)
        + [whole(a) for a in (q_gain, cosine, signed, dk, dv, kp, k_gain)],
        out_specs=out_specs,
        out_shape=out_shape,
        scratch_shapes=scratch,
        compiler_params=pltpu.CompilerParams(vmem_limit_bytes=48 * MIB),
        cost_estimate=cost(1.3e9),
        name="attention",
    )(*deps, me, lengths, q, u, k, v, *cs, q_gain, cosine, signed, dk, dv, kp, k_gain)


def weight_kernel(me, own_a, own_b, other_a, other_b, own_g, other_g, send, keep):
    step = pl.program_id(0)
    half = own_a.shape[1]
    first = pl.multiple_of((me[0] >> 1) * half, half)
    second = pl.multiple_of(((me[0] >> 1) ^ 1) * half, half)

    lhs = jnp.concatenate([own_a[...], own_b[...], other_a[...], other_b[...]], 1)
    rhs = [g[pl.ds(at, half), :] for g in (own_g, other_g) for at in (first, second)]
    total = jnp.dot(lhs, jnp.concatenate(rhs, 0), preferred_element_type=f32)

    @pl.when(step == 0)
    def _():
        send[...] = total.astype(bf16)

    @pl.when(step == 1)
    def _():
        keep[...] = total


def weight_products(me, transposes, own_g, other_g, deps, last):
    features, half = transposes[0].shape
    length, columns = own_g.shape
    out = pl.BlockSpec((features // 2, columns), lambda i: (0, 0))
    return pl.pallas_call(
        waiting(deps, weight_kernel),
        grid=(2,),
        in_specs=[ANY] * len(deps)
        + [pl.BlockSpec(memory_space=pltpu.SMEM)]
        + [pl.BlockSpec((features // 2, half), lambda i: (i, 0))] * 4
        + [pl.BlockSpec((length, columns), lambda i: (0, 0))] * 2,
        out_specs=[out, out],
        out_shape=[
            jax.ShapeDtypeStruct((features // 2, columns), bf16),
            jax.ShapeDtypeStruct((features // 2, columns), f32),
        ],
        compiler_params=pltpu.CompilerParams(vmem_limit_bytes=32 * MIB),
        cost_estimate=cost(3e10 if last else 1.2e9),
        name="weight_products",
    )(*deps, me, *transposes, own_g, other_g)


def input_kernel(me, *refs):
    *parts, kv, wq, wk, wv, send, keep, grads = refs
    half = send.shape[0]
    rows = half // 2
    block = parts[0].shape[1]

    @pl.when(pl.program_id(0) == 0)
    def _():
        for other in range(2):
            for chip in range(2):
                at = pl.multiple_of((2 * chip + (1 - other) * (1 - me[0]) + other * me[0]) * rows, rows)
                here = slice((2 * other + chip) * rows, (2 * other + chip + 1) * rows)
                for g, ref in enumerate((*parts, kv)):
                    grads[here, g * block : (g + 1) * block] = ref[pl.ds(at, rows), :]

    weights = jnp.concatenate([wq[...], wk[...], wv[...]], 1)
    total = lax.dot_general(
        grads[...], weights, (((1,), (1,)), ((), ())), preferred_element_type=f32
    )
    send[...] = total[:half].astype(bf16)
    keep[...] = total[half:]


def input_products(core, parts, kv, wq, wk, wv, deps):
    length = kv.shape[0]
    features, columns = wq.shape
    width = wk.shape[1]
    tile = 512 if features % 512 == 0 else features
    out = pl.BlockSpec((length // 2, tile), lambda i: (0, i))
    return pl.pallas_call(
        waiting(deps, input_kernel),
        grid=(features // tile,),
        in_specs=[ANY] * len(deps)
        + [pl.BlockSpec(memory_space=pltpu.SMEM)]
        + [pl.BlockSpec(a.shape, lambda i: (0, 0)) for a in (*parts, kv)]
        + [pl.BlockSpec((tile, a.shape[1]), lambda i: (i, 0)) for a in (wq, wk, wv)],
        out_specs=[out, out],
        out_shape=[
            jax.ShapeDtypeStruct((length // 2, features), bf16),
            jax.ShapeDtypeStruct((length // 2, features), f32),
        ],
        scratch_shapes=[pltpu.VMEM((length, columns + 2 * width), bf16)],
        compiler_params=pltpu.CompilerParams(vmem_limit_bytes=32 * MIB),
        cost_estimate=cost(1e6),
        name="input_products",
    )(*deps, core.astype(jnp.int32).reshape(1), *parts, kv, wq, wk, wv)


def final_kernel(*refs):
    *inputs, query_out, key_out, value_out = refs
    width = key_out.shape[1]
    count = len(inputs) // 2
    for n in range(count):
        total = inputs[n][...] + inputs[count + n][...].astype(f32)
        columns = total.shape[1]
        if n < count - 1:
            query_out[:, n * columns : (n + 1) * columns] = total
        else:
            key_out[...] = total[:, :width]
            value_out[...] = total[:, width:]


def final_sums(ends, width):
    share, columns = ends[0][1].shape
    kept = [end[0] for end in ends]
    received = [end[1] for end in ends]

    def spec(columns, block=0):
        return pl.BlockSpec((share, columns), lambda i: (block, 0))

    widths = ((len(ends) - 1) * columns, width, width)
    return pl.pallas_call(
        final_kernel,
        grid=(1,),
        in_specs=[spec(columns, 1)] * len(ends) + [spec(columns)] * len(ends),
        out_specs=[spec(w) for w in widths],
        out_shape=[jax.ShapeDtypeStruct((share, w), f32) for w in widths],
        compiler_params=pltpu.CompilerParams(vmem_limit_bytes=32 * MIB),
        cost_estimate=cost(1024),
        name="final_sums",
    )(*kept, *received)


def local(dp, sp, normed, wq, wk, wv, q_gain, k_gain, ctx_grad, lengths):
    rows, features = normed.shape
    width = q_gain.shape[0]
    columns = wq.shape[1]
    length = rows * sp
    block = 2 * width
    me_sp = lax.axis_index("sp")
    me_dp = lax.axis_index("dp")
    core, chip = me_sp % 2, me_sp // 2
    me = me_sp.astype(jnp.int32).reshape(1)
    q_gain = q_gain.reshape(1, width)
    k_gain = k_gain.reshape(1, width)
    cosine, signed = angle_tables(length, width)
    over_sp = functools.partial(exchange, axis="sp", size=sp)
    over_dp = functools.partial(exchange, axis="dp", size=dp)
    pair_bit = 2 if dp > 2 else 1
    halving = [b for b in (1 << i for i in range(dp.bit_length() - 1)) if b != pair_bit]
    share = features // dp
    mine = (me_dp // pair_bit) % 2

    def theirs(rows_of):
        size = pair_bit * share
        return jnp.concatenate(
            [
                lax.dynamic_slice_in_dim(rows_of, (2 * i + 1 - mine) * size, size, 1)
                for i in range(features // (2 * size))
            ],
            1,
        )

    def cotangent(m):
        return lax.dynamic_slice_in_dim(ctx_grad, (me_sp ^ m) * columns, columns, 1)

    far = over_sp(normed, bit=2)
    near = over_sp(normed, bit=1)
    pair0 = over_dp(theirs(normed), bit=pair_bit)

    previous = projections(
        me, 0, (normed, near), wq, wk, wv, q_gain, k_gain, cosine, signed, block, ()
    )
    own_a = transposed(me, (normed, near))
    cots = [cotangent(m) for m in range(4)]
    far, pair0, own_a, *rest = lax.optimization_barrier((far, pair0, own_a, *previous, *cots))
    previous, cots = rest[: len(previous)], rest[len(previous) :]

    diagonal = over_sp(far, bit=1)
    cs = (cots[0],) + tuple(over_sp(cots[m], bit=m) for m in (1, 2, 3))
    pair2 = over_dp(theirs(far), bit=pair_bit)
    q, u, k, kp, v = projections(
        me, 1, (far, diagonal), wq, wk, wv, q_gain, k_gain, cosine, signed, block, previous
    )
    own_b = transposed(me, (far, diagonal), (k,))
    pair0, k = lax.optimization_barrier((pair0, k))
    pair1 = over_sp(pair0, bit=1)

    def wanted(i):
        target = me_dp & pair_bit
        for n, bit in enumerate(halving):
            same = (i >> (len(halving) - 1 - n)) & 1
            target = target | ((me_dp if same else ~me_dp) & bit)
        return target

    def compact(d):
        return (d // (2 * pair_bit)) * pair_bit + d % pair_bit

    def ordered(t, place):
        t = t.reshape(t.shape[0] // share, share, t.shape[1])
        return jnp.concatenate(
            [lax.dynamic_index_in_dim(t, place(wanted(i)), 0, False) for i in range(dp // 2)], 0
        )

    own_a = ordered(own_a, lambda d: d)
    own_b = ordered(own_b, lambda d: d)

    groups = columns // block
    dk = jnp.zeros((length, width), f32)
    dv = dk
    parts, received, firsts = [], [], []

    def heads(g, deps):
        result = attention(
            g, g == groups - 1, block, me, lengths, q, u, k, v, cs,
            q_gain, cosine, signed, dk, dv, kp, k_gain, deps,
        )
        parts.append(result[0])
        received.append(over_dp(result[0], bit=pair_bit))
        return result[1:]

    def product(n, deps):
        send, keep = weight_products(
            me, (own_a, own_b, other_a, other_b), parts[n], received[n], deps, n == groups
        )
        firsts.append(keep + over_dp(send, bit=halving[0]).astype(f32))
        return keep

    def last_steps(keep):
        for bit in halving[1:-1]:
            half = keep.shape[0] // 2
            send, keep = keep[:half].astype(bf16), keep[half:]
            keep = keep + over_dp(send, bit=bit).astype(f32)
        return keep, over_dp(keep[:share].astype(bf16), bit=halving[-1])

    dk, dv = heads(0, (own_b,))
    other_a = transposed(me, (pair0, pair1), (dk,))
    pair2, dk = lax.optimization_barrier((pair2, dk))
    pair3 = over_sp(pair2, bit=1)
    dk, dv = heads(1, (other_a,))
    other_b = transposed(me, (pair2, pair3), (dk,))
    dk, dv = heads(2, (other_b,))
    other_a, other_b = ordered(other_a, compact), ordered(other_b, compact)
    keep = product(0, (dk,))
    (kv,) = heads(3, (keep, received[1]))
    parts.append(kv)
    received.append(over_dp(kv, bit=pair_bit))
    keep = product(1, (kv,))
    keep = product(2, (keep, firsts[0]))
    keep = product(3, (keep, firsts[1]))
    sent, kept = input_products(core, parts[:-1], kv, wq, wk, wv, (keep,))
    sent_near = over_sp(sent, bit=1)
    ends = [last_steps(first) for first in firsts]
    product(4, (sent, firsts[2], ends[0][1]))
    kept = (kept + sent_near.astype(f32)).reshape(sp // 2, rows, features)
    sent = lax.dynamic_index_in_dim(kept, 1 - chip, 0, False).astype(bf16)
    sent_far = over_sp(sent, bit=2)
    ends.append(last_steps(firsts[4]))
    kept = lax.dynamic_index_in_dim(kept, chip, 0, False)
    input_gradient = (kept + sent_far.astype(f32)).astype(bf16)
    return (input_gradient, *final_sums(ends, width))


def solution(mesh):
    in_specs = (
        P(("dp", "sp"), None),
        P(None, "sp"),
        P(None, "sp"),
        P(None, "sp"),
        P(),
        P(),
        P(("dp", "sp"), None),
        P("dp"),
    )
    out_specs = (P(("dp", "sp"), None), P("dp", "sp"), P("dp", "sp"), P("dp", "sp"))
    body = functools.partial(local, mesh.shape["dp"], mesh.shape["sp"])
    return jax.shard_map(body, mesh=mesh, in_specs=in_specs, out_specs=out_specs, check_vma=False)
```

time: 397 us -> 138 us (0.35)
  waiting for transfers between devices: 271 us -> 15.9 us
  matrix products: 52.9 us -> 0 us
  Pallas kernels: 0 us -> 52.9 us
  starting transfers between devices: 4.29 us -> 31.3 us
  local copies, waits for them, and re-layouts: 41.8 us -> 28.2 us
  between operations: 15.3 us -> 2.24 us
  other arithmetic: 11.1 us -> 5.83 us
    unnamed x4 -> x0, waiting for transfers between devices: 218 us -> none
    pallas_call x0 -> x17, Pallas kernels: none -> 52.9 us  [the longest x4 16 us: attention(): pl.pallas_call(waiting(deps, kernel), grid=(1,), in_specs=[ANY] * len(dep...]
    dot_general x55 -> x0, matrix products: 52.9 us -> none  [the longest x1 10.7 us: column_product(): lax.dot_general(span, grads, (((0,), (0,)), ((), ())), preferred_element_...]
    ppermute x0 -> x27, starting transfers between devices: none -> 31.3 us  [exchange(): return lax.ppermute(value, axis, [(d, d ^ bit) for d in range(size)])]
    reduce_scatter x1 -> x0, waiting for transfers between devices: 26.5 us -> none  [local(): lax.psum_scatter(total + lax.dot_general(value_gradient, value_weight, ((...]
    all_to_all x1 -> x0, waiting for transfers between devices: 20.4 us -> none  [local(): lax.all_to_all(ctx_grad, 'sp', split_axis=1, concat_axis=0, tiled=True)]
    ppermute x0 -> x27, waiting for transfers between devices: none -> 15.9 us  [exchange(): return lax.ppermute(value, axis, [(d, d ^ bit) for d in range(size)])]
    unnamed x79 -> x116, local copies, waits for them, and re-layouts: 29.1 us -> 18.5 us
  transfers between devices with their start and end apart: 4 -> 27, of which waited for: 4 -> 4; matrix products, arithmetic and copies ran while one was open for 8% -> 10% of each run, Pallas kernels for 0% -> 39%
where the time goes in v1:
time: 138 us; the launch traced here: 136 us
  Pallas kernels  52.9 us (38%)
  starting transfers between devices  31.3 us (23%)
  local copies, waits for them, and re-layouts  28.2 us (20%)
  waiting for transfers between devices  15.9 us (12%)
  other arithmetic  5.83 us (4%)
  between operations  2.24 us (2%)
    ppermute x27, starting transfers between devices, exchange(): return lax.ppermute(value, axis, [(d, d ^ bit) for d in range(size)])  31.3 us
    unnamed x116, local copies, waits for them, and re-layouts  18.5 us
    pallas_call x4, Pallas kernels, attention(): pl.pallas_call(waiting(deps, kernel), grid=(1,), in_specs=[ANY] * len(dep...  16 us
    ppermute x27, waiting for transfers between devices, exchange(): return lax.ppermute(value, axis, [(d, d ^ bit) for d in range(size)])  15.9 us
    pallas_call x2, Pallas kernels, projections(): pl.pallas_call(projection_kernel, grid_spec=pltpu.PrefetchScalarGridSpec(...  10.2 us
    pallas_call x4, Pallas kernels, transposed(): pl.pallas_call(waiting(deps, transpose_kernel), grid=(features // block,)...  9.75 us
    pallas_call x5, Pallas kernels, weight_products(): pl.pallas_call(waiting(deps, weight_kernel), grid=(2,), in_specs=[ANY] *...  8.54 us
    pallas_call x1, Pallas kernels, input_products(): pl.pallas_call(waiting(deps, input_kernel), grid=(features // tile,), in_...  5.79 us
  transfers between devices with their start and end apart: 27, of which 4 were waited for; matrix products, arithmetic and copies ran while one was open for 10% of the time, Pallas kernels for 39%

profile of v1, /device:TPU:0, one launch (start us, length us, event | category | flops | bytes accessed | tf_op | source)
XLA Modules:
  0.0 136.3 jit_solution(285384447261941997)
XLA Ops:
  1.1 2.6 %collective-permute-start = (bf16[128,2560]{1,0:T(8,128)(2,1)}, bf16[128,2560]{1,0:T(8,128)(2,1)}, u32[]{:S(2)}, u32[]{:S(2)}) collective-permute-start(bf16[128,2560]{1,0:T(8,128)(2,1)} %s0.1), channel_id=1, source_target_pairs={{0,2},{1,3},{2,0},{3,1},{4,6},{5,7},{6,4},{7,5},{8,10},{9,11},{10,... | collective-permute-start | bytes 1966088 | tf_op jit(solution)/shard_map/ppermute | solution.py:42
  3.7 1.0 constant_dynamic-slice_fusion.7
  5.5 1.6 %collective-permute-start.1 = (bf16[128,1280]{1,0:T(8,128)(2,1)}, bf16[128,1280]{1,0:T(8,128)(2,1)}, u32[]{:S(2)}, u32[]{:S(2)}) collective-permute-start(bf16[128,1280]{1,0:T(8,128)(2,1)} %pad_maximum_fusion.4), channel_id=1, source_target_pairs={{0,8},{4,12},{8,0},{12,4},{16,24},{20,28},{24,16},{28,20},{1,9},{5... | collective-permute-start | bytes 983048 | tf_op jit(solution)/shard_map/ppermute | solution.py:42
  7.1 1.0 fusion.2
  8.4 2.5 %constant_dynamic-slice_fusion.2 = (bf16[128,1024]{1,0:T(8,128)(2,1)}, bf16[128,1024]{1,0:T(8,128)(2,1)}, bf16[128,1024]{1,0:T(8,128)(2,1)}, bf16[128,1024]{1,0:T(8,128)(2,1)}) fusion(bf16[128,4096]{1,0:T(8,128)(2,1)} %param.14, s32[]{:T(128)S(6)} %select_n.126, s32[]{:T(128)S(6)} %select_n.124, s32[]{:T(128)S(6)} %select_n.123, s32[]{:T(128)S(6)} %select_n.125), kind=kLoop, calls=%fused_computation.44 | loop fusion | bytes 2097168 | tf_op jit(solution)/shard_map/dynamic_slice | solution.py:416
  10.9 1.1 transposed.4
  12.0 1.0 copy-done.35
  13.1 1.1 copy-done.30
  14.2 1.1 copy-done.37
  15.3 4.5 %projections.2 = (bf16[512,1024]{1,0:T(8,128)(2,1)S(1)}, f32[512,1024]{1,0:T(8,128)S(1)}, bf16[512,128]{1,0:T(8,128)(2,1)S(1)}, f32[512,128]{1,0:T(8,128)S(1)}, bf16[512,128]{1,0:T(8,128)(2,1)S(1)}) custom-call(s32[1]{0:T(128)} %bitcast.refs_0_.me.refs_1_.refs_2_.refs_3_, bf16[128,2560]{1,0:T(8,128)(2,1)S(1)} %copy-done.30, ...), custom_call_target="tpu_custom_call" | custom-call | flops 1677721600 | bytes 1024 | tf_op jit(solution)/shard_map/projections/pallas_call | solution.py:107
  22.9 1.0 collective-permute-start.6
  23.9 1.0 constant_dynamic-slice_fusion.1
  25.5 1.2 dynamic-slice_bitcast_fusion.11
  26.7 2.5 %copy-done.2 = bf16[2560,1024]{1,0:T(8,128)(2,1)S(1)} copy-done((bf16[2560,1024]{1,0:T(8,128)(2,1)S(1)}, bf16[2560,1024]{1,0:T(8,128)(2,1)}, u32[]{:S(2)}) %copy-start.2) | copy-done | bytes 5242904
  29.2 5.8 %projections.3 = (bf16[512,1024]{1,0:T(8,128)(2,1)S(1)}, f32[512,1024]{1,0:T(8,128)S(1)}, bf16[512,128]{1,0:T(8,128)(2,1)S(1)}, f32[512,128]{1,0:T(8,128)S(1)}, bf16[512,128]{1,0:T(8,128)(2,1)S(1)}) custom-call(s32[1]{0:T(128)} %bitcast.refs_0_.me.refs_1_.refs_2_.refs_3_, ...), custom_call_target="tpu_custom_call", output_to_operand_aliasing={{0}: (10, {}), {1}: (11, {}), {2}: (12, {}), {3}: (13, {}),... | custom-call | flops 1677721600 | bytes 1024 | tf_op jit(solution)/shard_map/projections/pallas_call | solution.py:107
  35.0 5.3 %transposed.5 = bf16[2560,256]{1,0:T(8,128)(2,1)S(1)} custom-call(bf16[512,128]{1,0:T(8,128)(2,1)S(1)} %get-tuple-element.71.refs_0_.refs_5_.refs_6_, s32[1]{0:T(128)} %bitcast.refs_0_.me.refs_1_.refs_2_.refs_3_, bf16[128,2560]{1,0:T(8,128)(2,1)} %collective-permute-done.s0.refs_2_, bf16[128,2560]{1,0:T(8,128)(2,1)} %collective-permute-done.3.s1.refs_3_), custom_call_target="tpu_custom_call" | custom-call | flops 335544320 | bytes 1024 | tf_op jit(solution)/shard_map/transposed/pallas_call | solution.py:148
  41.3 3.3 %attention.4 = (bf16[512,256]{1,0:T(8,128)(2,1)S(1)}, f32[512,128]{1,0:T(8,128)S(1)}, f32[512,128]{1,0:T(8,128)S(1)}) custom-call(bf16[1280,256]{1,0:T(8,128)(2,1)S(1)} %pad_maximum_fusion.refs_0_.refs_3_.refs_4_.refs_5_, s32[1]{0:T(128)} %bitcast.refs_0_.me.refs_1_.refs_2_.refs_3_, s32[1]{0:T(128)S(6)} %copy.22.refs_2_.refs_3_, ...), custom_call_target="tpu_custom_call" | custom-call | flops 1300000000 | bytes 1024 | tf_op jit(solution)/shard_map/attention/pallas_call | solution.py:244
  45.1 1.6 %collective-permute-start.10 = (bf16[512,256]{1,0:T(8,128)(2,1)S(1)}, bf16[512,256]{1,0:T(8,128)(2,1)S(1)}, u32[]{:S(2)}, u32[]{:S(2)}) collective-permute-start(bf16[512,256]{1,0:T(8,128)(2,1)S(1)} %get-tuple-element.87.refs_6_.refs_2_), channel_id=1, source_target_pairs={{0,8},{4,12},{8,0},{12,4},{16,24},{20,28},{24,16},{28,20},{1,9},{5... | collective-permute-start | bytes 786440 | tf_op jit(solution)/shard_map/ppermute | solution.py:42
  46.8 2.8 %transposed.6.refs_0_ = bf16[1280,256]{1,0:T(8,128)(2,1)S(1)} custom-call(f32[512,128]{1,0:T(8,128)S(1)} %get-tuple-element.80.refs_0_.refs_14_, s32[1]{0:T(128)} %bitcast.refs_0_.me.refs_1_.refs_2_.refs_3_, bf16[128,1280]{1,0:T(8,128)(2,1)} %collective-permute-done.1.refs_2_, bf16[128,1280]{1,0:T(8,128)(2,1)S(1)} %collective-permute-done.7.refs_3_), custom_call_target="tpu_custom_call" | custom-call | flops 167772160 | bytes 1024 | tf_op jit(solution)/shard_map/transposed/pallas_call | solution.py:148
  49.6 4.1 %attention.5 = (bf16[512,256]{1,0:T(8,128)(2,1)}, f32[512,128]{1,0:T(8,128)S(1)}, f32[512,128]{1,0:T(8,128)S(1)}) custom-call(bf16[1280,256]{1,0:T(8,128)(2,1)S(1)} %transposed.6.refs_0_, s32[1]{0:T(128)} %bitcast.refs_0_.me.refs_1_.refs_2_.refs_3_, s32[1]{0:T(128)S(6)} %copy.22.refs_2_.refs_3_, bf16[512,1024]{1,0:T(8,128)(2,1)S(1)} %get-tuple-element.68.refs_3_.refs_4_, ...), custom_call_target="tpu_custom_call" | custom-call | flops 1300000000 | bytes 1024 | tf_op jit(solution)/shard_map/attention/pallas_call | solution.py:244
  54.9 3.7 %attention.6 = (bf16[512,256]{1,0:T(8,128)(2,1)S(1)}, f32[512,128]{1,0:T(8,128)S(1)}, f32[512,128]{1,0:T(8,128)S(1)}) custom-call(bf16[1280,256]{1,0:T(8,128)(2,1)S(1)} %transposed.7.refs_0_, s32[1]{0:T(128)} %bitcast.refs_0_.me.refs_1_.refs_2_.refs_3_, s32[1]{0:T(128)S(6)} %copy.22.refs_2_.refs_3_, bf16[512,1024]{1,0:T(8,128)(2,1)S(1)} %get-tuple-element.68.refs_3_.refs_4_, ...), custom_call_target="tpu_custom_call" | custom-call | flops 1300000000 | bytes 1024 | tf_op jit(solution)/shard_map/attention/pallas_call | solution.py:244
  60.1 1.9 %weight_products.5 = (bf16[640,256]{1,0:T(8,128)(2,1)}, f32[640,256]{1,0:T(8,128)S(1)}) custom-call(f32[512,128]{1,0:T(8,128)S(1)} %get-tuple-element.85.refs_0_.refs_15_, s32[1]{0:T(128)} %bitcast.refs_0_.me.refs_1_.refs_2_.refs_3_, bf16[1280,256]{1,0:T(8,128)(2,1)S(1)} %pad_maximum_fusion.1.refs_2_.refs_3_.refs_4_, ...), custom_call_target="tpu_custom_call" | custom-call | flops 1200000000 | bytes 1024 | tf_op jit(solution)/shard_map/weight_products/pallas_call | solution.py:284
  62.8 1.5 %collective-permute-start.12 = (bf16[640,256]{1,0:T(8,128)(2,1)}, bf16[640,256]{1,0:T(8,128)(2,1)}, u32[]{:S(2)}, u32[]{:S(2)}) collective-permute-start(bf16[640,256]{1,0:T(8,128)(2,1)} %get-tuple-element.93), channel_id=1, source_target_pairs={{0,4},{4,0},{8,12},{12,8},{16,20},{20,16},{24,28},{28,24},{1,5},{5... | collective-permute-start | bytes 983048 | tf_op jit(solution)/shard_map/ppermute | solution.py:42
  64.3 1.6 %collective-permute-start.13 = (bf16[512,256]{1,0:T(8,128)(2,1)}, bf16[512,256]{1,0:T(8,128)(2,1)S(1)}, u32[]{:S(2)}, u32[]{:S(2)}) collective-permute-start(bf16[512,256]{1,0:T(8,128)(2,1)} %copy-done.40), channel_id=1, source_target_pairs={{0,8},{4,12},{8,0},{12,4},{16,24},{20,28},{24,16},{28,20},{1,9},{5... | collective-permute-start | bytes 786440 | tf_op jit(solution)/shard_map/ppermute | solution.py:42
  66.9 0.9 copy-done.26
  69.7 1.1 copy-done.39
  70.8 0.9 copy-done.47
  72.7 5.0 %attention.7 = (bf16[512,256]{1,0:T(8,128)(2,1)S(1)}, bf16[512,256]{1,0:T(8,128)(2,1)}) custom-call(f32[640,256]{1,0:T(8,128)S(1)} %copy-done.39, bf16[512,256]{1,0:T(8,128)(2,1)} %collective-permute-done.11.refs_1_.refs_7_, s32[1]{0:T(128)} %bitcast.refs_0_.me.refs_1_.refs_2_.refs_3_, s32[1]{0:T(128)S(6)} %copy.22.refs_2_.refs_3_, ...), custom_call_target="tpu_custom_call" | custom-call | flops 1300000000 | bytes 1024 | tf_op jit(solution)/shard_map/attention/pallas_call | solution.py:244
  78.1 1.6 %collective-permute-start.21 = (bf16[512,256]{1,0:T(8,128)(2,1)}, bf16[512,256]{1,0:T(8,128)(2,1)S(1)}, u32[]{:S(2)}, u32[]{:S(2)}) collective-permute-start(bf16[512,256]{1,0:T(8,128)(2,1)} %get-tuple-element.91.refs_0_.refs_6_.refs_8_), channel_id=1, source_target_pairs={{0,8},{4,12},{8,0},{12,4},{16,24},{20,28},{24,16},{28,20},{1,9},{5... | collective-permute-start | bytes 786440 | tf_op jit(solution)/shard_map/ppermute | solution.py:42
  79.7 2.3 %weight_products.6 = (bf16[640,256]{1,0:T(8,128)(2,1)S(1)}, f32[640,256]{1,0:T(8,128)S(1)}) custom-call(bf16[512,256]{1,0:T(8,128)(2,1)} %get-tuple-element.91.refs_0_.refs_6_.refs_8_, s32[1]{0:T(128)} %bitcast.refs_0_.me.refs_1_.refs_2_.refs_3_, bf16[1280,256]{1,0:T(8,128)(2,1)S(1)} %pad_maximum_fusion.1.refs_2_.refs_3_.refs_4_, ...), custom_call_target="tpu_custom_call" | custom-call | flops 1200000000 | bytes 1024 | tf_op jit(solution)/shard_map/weight_products/pallas_call | solution.py:284
  82.6 1.0 convert_add_fusion.5.refs_1_.refs_0_
  83.7 2.7 %collective-permute-start.20 = (bf16[320,256]{1,0:T(8,128)(2,1)S(1)}, bf16[320,256]{1,0:T(8,128)(2,1)S(1)}, u32[]{:S(2)}, u32[]{:S(2)}) collective-permute-start(bf16[320,256]{1,0:T(8,128)(2,1)S(1)} %slice.39), channel_id=1, source_target_pairs={{0,16},{4,20},{8,24},{12,28},{16,0},{20,4},{24,8},{28,12},{1,17},{... | collective-permute-start | bytes 491528 | tf_op jit(solution)/shard_map/ppermute | solution.py:42
  86.4 1.1 weight_products.7
  87.5 1.6 %collective-permute-start.18 = (bf16[640,256]{1,0:T(8,128)(2,1)S(1)}, bf16[640,256]{1,0:T(8,128)(2,1)S(1)}, u32[]{:S(2)}, u32[]{:S(2)}) collective-permute-start(bf16[640,256]{1,0:T(8,128)(2,1)S(1)} %get-tuple-element.101), channel_id=1, source_target_pairs={{0,4},{4,0},{8,12},{12,8},{16,20},{20,16},{24,28},{28,24},{1,5},{5... | collective-permute-start | bytes 983048 | tf_op jit(solution)/shard_map/ppermute | solution.py:42
  89.1 3.2 %collective-permute-done.14 = bf16[640,256]{1,0:T(8,128)(2,1)S(1)} collective-permute-done((bf16[640,256]{1,0:T(8,128)(2,1)S(1)}, bf16[640,256]{1,0:T(8,128)(2,1)S(1)}, u32[]{:S(2)}, u32[]{:S(2)}) %collective-permute-start.14) | collective-permute-done | bytes 327712 | tf_op jit(solution)/shard_map/ppermute | solution.py:42
  93.0 3.1 %collective-permute-start.23 = (bf16[320,256]{1,0:T(8,128)(2,1)}, bf16[320,256]{1,0:T(8,128)(2,1)}, u32[]{:S(2)}, u32[]{:S(2)}) collective-permute-start(bf16[320,256]{1,0:T(8,128)(2,1)} %slice.38), channel_id=1, source_target_pairs={{0,16},{4,20},{8,24},{12,28},{16,0},{20,4},{24,8},{28,12},{1,17},{... | collective-permute-start | bytes 491528 | tf_op jit(solution)/shard_map/ppermute | solution.py:42
  96.1 1.1 weight_products.8
  98.8 5.8 %input_products.1 = (bf16[256,2560]{1,0:T(8,128)(2,1)S(1)}, f32[256,2560]{1,0:T(8,128)S(1)}) custom-call(f32[640,256]{1,0:T(8,128)S(1)} %get-tuple-element.98.refs_0_, s32[1]{0:T(128)} %bitcast.23.refs_1_, bf16[512,256]{1,0:T(8,128)(2,1)S(1)} %copy-done.45, bf16[512,256]{1,0:T(8,128)(2,1)} %get-tuple-element.89.refs_6_.refs_3_, ...), custom_call_target="tpu_custom_call" | custom-call | flops 1000000 | bytes 1024 | tf_op jit(solution)/shard_map/input_products/pallas_call | solution.py:331
  105.5 2.1 %weight_products.9 = (bf16[640,256]{1,0:T(8,128)(2,1)S(1)}, f32[640,256]{1,0:T(8,128)S(1)}) custom-call(bf16[256,2560]{1,0:T(8,128)(2,1)S(1)} %get-tuple-element.100.refs_0_, f32[640,256]{1,0:T(8,128)S(1)} %convert_add_fusion.3.refs_1_.refs_2_, bf16[320,256]{1,0:T(8,128)(2,1)S(1)} %collective-permute-done.20.refs_2_.refs_5_, ...), custom_call_target="tpu_custom_call" | custom-call | flops 30000001024 | bytes 1024 | tf_op jit(solution)/shard_map/weight_products/pallas_call | solution.py:284
  107.6 1.6 %collective-permute-start.22 = (bf16[640,256]{1,0:T(8,128)(2,1)S(1)}, bf16[640,256]{1,0:T(8,128)(2,1)S(1)}, u32[]{:S(2)}, u32[]{:S(2)}) collective-permute-start(bf16[640,256]{1,0:T(8,128)(2,1)S(1)} %get-tuple-element.104), channel_id=1, source_target_pairs={{0,4},{4,0},{8,12},{12,8},{16,20},{20,16},{24,28},{28,24},{1,5},{5... | collective-permute-start | bytes 983048 | tf_op jit(solution)/shard_map/ppermute | solution.py:42
  109.5 1.0 fusion.1
  111.9 2.9 %collective-permute-start.25 = (bf16[320,256]{1,0:T(8,128)(2,1)}, bf16[320,256]{1,0:T(8,128)(2,1)}, u32[]{:S(2)}, u32[]{:S(2)}) collective-permute-start(bf16[320,256]{1,0:T(8,128)(2,1)} %slice.36), channel_id=1, source_target_pairs={{0,16},{4,20},{8,24},{12,28},{16,0},{20,4},{24,8},{28,12},{1,17},{... | collective-permute-start | bytes 491528 | tf_op jit(solution)/shard_map/ppermute | solution.py:42
  114.7 3.0 %collective-permute-done.22 = bf16[640,256]{1,0:T(8,128)(2,1)S(1)} collective-permute-done((bf16[640,256]{1,0:T(8,128)(2,1)S(1)}, bf16[640,256]{1,0:T(8,128)(2,1)S(1)}, u32[]{:S(2)}, u32[]{:S(2)}) %collective-permute-start.22) | collective-permute-done | bytes 327712 | tf_op jit(solution)/shard_map/ppermute | solution.py:42
  118.6 2.6 %collective-permute-start.26 = (bf16[320,256]{1,0:T(8,128)(2,1)}, bf16[320,256]{1,0:T(8,128)(2,1)}, u32[]{:S(2)}, u32[]{:S(2)}) collective-permute-start(bf16[320,256]{1,0:T(8,128)(2,1)} %slice.35), channel_id=1, source_target_pairs={{0,16},{4,20},{8,24},{12,28},{16,0},{20,4},{24,8},{28,12},{1,17},{... | collective-permute-start | bytes 491528 | tf_op jit(solution)/shard_map/ppermute | solution.py:42
  121.1 6.1 %collective-permute-done.25.refs_8_ = bf16[320,256]{1,0:T(8,128)(2,1)} collective-permute-done((bf16[320,256]{1,0:T(8,128)(2,1)}, bf16[320,256]{1,0:T(8,128)(2,1)}, u32[]{:S(2)}, u32[]{:S(2)}) %collective-permute-start.25) | collective-permute-done | bytes 163872 | tf_op jit(solution)/shard_map/ppermute | solution.py:42
  127.2 3.5 %collective-permute-done.26.refs_9_ = bf16[320,256]{1,0:T(8,128)(2,1)} collective-permute-done((bf16[320,256]{1,0:T(8,128)(2,1)}, bf16[320,256]{1,0:T(8,128)(2,1)}, u32[]{:S(2)}, u32[]{:S(2)}) %collective-permute-start.26) | collective-permute-done | bytes 163872 | tf_op jit(solution)/shard_map/ppermute | solution.py:42
  131.6 2.6 %final_sums.1 = (f32[320,1024]{1,0:T(8,128)}, f32[320,128]{1,0:T(8,128)}, f32[320,128]{1,0:T(8,128)}) custom-call(f32[640,256]{1,0:T(8,128)S(1)} %convert_add_fusion.5.refs_1_.refs_0_, f32[640,256]{1,0:T(8,128)S(1)} %convert_add_fusion.4.refs_1_, f32[640,256]{1,0:T(8,128)S(1)} %convert_add_fusion.3.refs_1_.refs_2_, ...), custom_call_target="tpu_custom_call" | custom-call | flops 1024 | bytes 1024 | tf_op jit(solution)/shard_map/final_sums/pallas_call | solution.py:373
  134.2 2.0 %fusion = bf16[128,2560]{1,0:T(8,128)(2,1)} fusion(bf16[128,2560]{1,0:T(8,128)(2,1)} %collective-permute-done.17, f32[2,128,2560]{2,1,0:T(8,128)S(1)} %bitcast.66, s32[]{:T(128)S(6)} %select_n.145), kind=kLoop, calls=%fused_computation.2 | loop fusion | flops 983040 | bytes 2621444 | tf_op jit(solution)/shard_map/convert_element_type | solution.py:511
  (171 shorter events, 20.7 us)
Async XLA Ops:
  0.6 10.2 %collective-permute-start.2 = (bf16[128,2560]{1,0:T(8,128)(2,1)}, bf16[128,2560]{1,0:T(8,128)(2,1)S(1)}, u32[]{:S(2)}, u32[]{:S(2)}) collective-permute-start(bf16[128,2560]{1,0:T(8,128)(2,1)} %s0.1), channel_id=1, source_target_pairs={{0,1},{1,0},{2,3},{3,2},{4,5},{5,4},{6,7},{7,6},{8,9},{9,8},{10,11... | collective-permute-start | bytes 1966088 | tf_op jit(solution)/shard_map/ppermute | solution.py:42
  1.1 19.9 %collective-permute-start = (bf16[128,2560]{1,0:T(8,128)(2,1)}, bf16[128,2560]{1,0:T(8,128)(2,1)}, u32[]{:S(2)}, u32[]{:S(2)}) collective-permute-start(bf16[128,2560]{1,0:T(8,128)(2,1)} %s0.1), channel_id=1, source_target_pairs={{0,2},{1,3},{2,0},{3,1},{4,6},{5,7},{6,4},{7,5},{8,10},{9,11},{10,... | collective-permute-start | bytes 1966088 | tf_op jit(solution)/shard_map/ppermute | solution.py:42
  4.7 6.1 %copy-start.29 = (bf16[128,2560]{1,0:T(8,128)(2,1)S(1)}, bf16[128,2560]{1,0:T(8,128)(2,1)}, u32[]{:S(2)}) copy-start(bf16[128,2560]{1,0:T(8,128)(2,1)} %s0.1) | copy-start | bytes 1966084
  5.5 15.6 %collective-permute-start.1 = (bf16[128,1280]{1,0:T(8,128)(2,1)}, bf16[128,1280]{1,0:T(8,128)(2,1)}, u32[]{:S(2)}, u32[]{:S(2)}) collective-permute-start(bf16[128,1280]{1,0:T(8,128)(2,1)} %pad_maximum_fusion.4), channel_id=1, source_target_pairs={{0,8},{4,12},{8,0},{12,4},{16,24},{20,28},{24,16},{28,20},{1,9},{5... | collective-permute-start | bytes 983048 | tf_op jit(solution)/shard_map/ppermute | solution.py:42
  7.1 5.9 %copy-start.14 = (bf16[2560,128]{1,0:T(8,128)(2,1)S(1)}, bf16[2560,128]{1,0:T(8,128)(2,1)}, u32[]{:S(2)}) copy-start(bf16[2560,128]{1,0:T(8,128)(2,1)} %refs_9_.1) | copy-start | bytes 1966084
  8.1 4.9 %copy-start.1 = (bf16[2560,1024]{1,0:T(8,128)(2,1)S(1)}, bf16[2560,1024]{1,0:T(8,128)(2,1)}, u32[]{:S(2)}) copy-start(bf16[2560,1024]{1,0:T(8,128)(2,1)} %refs_7_.1) | copy-start | bytes 15728644
  21.1 5.6 %collective-permute-start.3 = (bf16[128,2560]{1,0:T(8,128)(2,1)}, bf16[128,2560]{1,0:T(8,128)(2,1)}, u32[]{:S(2)}, u32[]{:S(2)}) collective-permute-start(bf16[128,2560]{1,0:T(8,128)(2,1)} %collective-permute-done.s0.refs_2_), channel_id=1, source_target_pairs={{0,1},{1,0},{2,3},{3,2},{4,5},{5,4},{6,7},{7,6},{8,9},{9,8},{10,11... | collective-permute-start | bytes 1966088 | tf_op jit(solution)/shard_map/ppermute | solution.py:42
  21.9 4.8 %copy-start.4 = (f32[512,128]{1,0:T(8,128)S(1)}, f32[512,128]{1,0:T(8,128)}, u32[]{:S(2)}) copy-start(f32[512,128]{1,0:T(8,128)} %copy-done.3) | copy-start | bytes 786436
  22.0 18.9 %collective-permute-start.4 = (bf16[128,1024]{1,0:T(8,128)(2,1)}, bf16[128,1024]{1,0:T(8,128)(2,1)S(1)}, u32[]{:S(2)}, u32[]{:S(2)}) collective-permute-start(bf16[128,1024]{1,0:T(8,128)(2,1)} %get-tuple-element.74), channel_id=1, source_target_pairs={{0,1},{1,0},{2,3},{3,2},{4,5},{5,4},{6,7},{7,6},{8,9},{9,8},{10,11... | collective-permute-start | bytes 786440 | tf_op jit(solution)/shard_map/ppermute | solution.py:42
  22.4 18.5 %collective-permute-start.5 = (bf16[128,1024]{1,0:T(8,128)(2,1)}, bf16[128,1024]{1,0:T(8,128)(2,1)S(1)}, u32[]{:S(2)}, u32[]{:S(2)}) collective-permute-start(bf16[128,1024]{1,0:T(8,128)(2,1)} %get-tuple-element.75), channel_id=1, source_target_pairs={{0,2},{1,3},{2,0},{3,1},{4,6},{5,7},{6,4},{7,5},{8,10},{9,11},{10,... | collective-permute-start | bytes 786440 | tf_op jit(solution)/shard_map/ppermute | solution.py:42
  22.9 18.0 %collective-permute-start.6 = (bf16[128,1024]{1,0:T(8,128)(2,1)}, bf16[128,1024]{1,0:T(8,128)(2,1)S(1)}, u32[]{:S(2)}, u32[]{:S(2)}) collective-permute-start(bf16[128,1024]{1,0:T(8,128)(2,1)} %get-tuple-element.76), channel_id=1, source_target_pairs={{0,3},{1,2},{2,1},{3,0},{4,7},{5,6},{6,5},{7,4},{8,11},{9,10},{10,... | collective-permute-start | bytes 786440 | tf_op jit(solution)/shard_map/ppermute | solution.py:42
  25.0 19.7 %collective-permute-start.8 = (bf16[128,1280]{1,0:T(8,128)(2,1)S(1)}, bf16[128,1280]{1,0:T(8,128)(2,1)S(1)}, u32[]{:S(2)}, u32[]{:S(2)}) collective-permute-start(bf16[128,1280]{1,0:T(8,128)(2,1)S(1)} %pad_maximum_fusion.5), channel_id=1, source_target_pairs={{0,8},{4,12},{8,0},{12,4},{16,24},{20,28},{24,16},{28,20},{1,9},{5... | collective-permute-start | bytes 983048 | tf_op jit(solution)/shard_map/ppermute | solution.py:42
  35.0 5.3 %copy-start = (f32[512,1024]{1,0:T(8,128)}, f32[512,1024]{1,0:T(8,128)S(1)}, u32[]{:S(2)}) copy-start(f32[512,1024]{1,0:T(8,128)S(1)} %get-tuple-element.69.refs_4_.refs_5_) | copy-start | bytes 6291460
  35.0 19.9 %copy-start.9 = (f32[512,128]{1,0:T(8,128)}, f32[512,128]{1,0:T(8,128)S(1)}, u32[]{:S(2)}) copy-start(f32[512,128]{1,0:T(8,128)S(1)} %get-tuple-element.77.refs_16_.refs_17_) | copy-start | bytes 786436
  35.0 19.9 %copy-start.33 = (bf16[512,128]{1,0:T(8,128)(2,1)}, bf16[512,128]{1,0:T(8,128)(2,1)S(1)}, u32[]{:S(2)}) copy-start(bf16[512,128]{1,0:T(8,128)(2,1)S(1)} %get-tuple-element.72.refs_6_.refs_7_) | copy-start | bytes 393220
  40.4 6.4 %collective-permute-start.7 = (bf16[128,1280]{1,0:T(8,128)(2,1)}, bf16[128,1280]{1,0:T(8,128)(2,1)S(1)}, u32[]{:S(2)}, u32[]{:S(2)}) collective-permute-start(bf16[128,1280]{1,0:T(8,128)(2,1)} %collective-permute-done.1.refs_2_), channel_id=1, source_target_pairs={{0,1},{1,0},{2,3},{3,2},{4,5},{5,4},{6,7},{7,6},{8,9},{9,8},{10,11... | collective-permute-start | bytes 983048 | tf_op jit(solution)/shard_map/ppermute | solution.py:42
  40.9 14.0 %copy-start.23 = (bf16[128,1024]{1,0:T(8,128)(2,1)}, bf16[128,1024]{1,0:T(8,128)(2,1)S(1)}, u32[]{:S(2)}) copy-start(bf16[128,1024]{1,0:T(8,128)(2,1)S(1)} %collective-permute-done.4.refs_8_.refs_9_) | copy-start | bytes 786436
  40.9 14.0 %copy-start.25 = (bf16[128,1024]{1,0:T(8,128)(2,1)}, bf16[128,1024]{1,0:T(8,128)(2,1)S(1)}, u32[]{:S(2)}) copy-start(bf16[128,1024]{1,0:T(8,128)(2,1)S(1)} %collective-permute-done.5.refs_9_.refs_10_) | copy-start | bytes 786436
  40.9 14.0 %copy-start.27 = (bf16[128,1024]{1,0:T(8,128)(2,1)}, bf16[128,1024]{1,0:T(8,128)(2,1)S(1)}, u32[]{:S(2)}) copy-start(bf16[128,1024]{1,0:T(8,128)(2,1)S(1)} %collective-permute-done.6.refs_10_.refs_11_) | copy-start | bytes 786436
  44.6 15.5 %copy-start.44 = (bf16[512,256]{1,0:T(8,128)(2,1)}, bf16[512,256]{1,0:T(8,128)(2,1)S(1)}, u32[]{:S(2)}) copy-start(bf16[512,256]{1,0:T(8,128)(2,1)S(1)} %get-tuple-element.87.refs_6_.refs_2_) | copy-start | bytes 786436
  44.6 9.4 %collective-permute-start.9 = (bf16[128,1280]{1,0:T(8,128)(2,1)S(1)}, bf16[128,1280]{1,0:T(8,128)(2,1)S(1)}, u32[]{:S(2)}, u32[]{:S(2)}) collective-permute-start(bf16[128,1280]{1,0:T(8,128)(2,1)S(1)} %collective-permute-done.8.refs_2_), channel_id=1, source_target_pairs={{0,1},{1,0},{2,3},{3,2},{4,5},{5,4},{6,7},{7,6},{8,9},{9,8},{10,11... | collective-permute-start | bytes 983048 | tf_op jit(solution)/shard_map/ppermute | solution.py:42
  45.1 34.6 %copy-start.17 = (bf16[1280,256]{1,0:T(8,128)(2,1)}, bf16[1280,256]{1,0:T(8,128)(2,1)S(1)}, u32[]{:S(2)}) copy-start(bf16[1280,256]{1,0:T(8,128)(2,1)S(1)} %pad_maximum_fusion.1.refs_2_.refs_3_.refs_4_) | copy-start | bytes 1966084
  45.1 15.0 %collective-permute-start.10 = (bf16[512,256]{1,0:T(8,128)(2,1)S(1)}, bf16[512,256]{1,0:T(8,128)(2,1)S(1)}, u32[]{:S(2)}, u32[]{:S(2)}) collective-permute-start(bf16[512,256]{1,0:T(8,128)(2,1)S(1)} %get-tuple-element.87.refs_6_.refs_2_), channel_id=1, source_target_pairs={{0,8},{4,12},{8,0},{12,4},{16,24},{20,28},{24,16},{28,20},{1,9},{5... | collective-permute-start | bytes 786440 | tf_op jit(solution)/shard_map/ppermute | solution.py:42
  53.6 12.3 %collective-permute-start.11 = (bf16[512,256]{1,0:T(8,128)(2,1)}, bf16[512,256]{1,0:T(8,128)(2,1)}, u32[]{:S(2)}, u32[]{:S(2)}) collective-permute-start(bf16[512,256]{1,0:T(8,128)(2,1)} %get-tuple-element.89.refs_6_.refs_3_), channel_id=1, source_target_pairs={{0,8},{4,12},{8,0},{12,4},{16,24},{20,28},{24,16},{28,20},{1,9},{5... | collective-permute-start | bytes 786440 | tf_op jit(solution)/shard_map/ppermute | solution.py:42
  54.8 5.3 %copy-start.19 = (bf16[1280,256]{1,0:T(8,128)(2,1)}, bf16[1280,256]{1,0:T(8,128)(2,1)S(1)}, u32[]{:S(2)}) copy-start(bf16[1280,256]{1,0:T(8,128)(2,1)S(1)} %pad_maximum_fusion.2.refs_4_.refs_5_.refs_6_) | copy-start | bytes 1966084
  54.9 5.2 %copy-start.21 = (bf16[1280,256]{1,0:T(8,128)(2,1)}, bf16[1280,256]{1,0:T(8,128)(2,1)S(1)}, u32[]{:S(2)}) copy-start(bf16[1280,256]{1,0:T(8,128)(2,1)S(1)} %pad_maximum_fusion.3.refs_5_.refs_6_.refs_7_) | copy-start | bytes 1966084
  60.1 5.8 %copy-start.5 = (f32[512,128]{1,0:T(8,128)S(1)}, f32[512,128]{1,0:T(8,128)}, u32[]{:S(2)}) copy-start(f32[512,128]{1,0:T(8,128)} %copy-done.3) | copy-start | bytes 786436
  60.1 5.8 %copy-start.10 = (f32[512,128]{1,0:T(8,128)S(1)}, f32[512,128]{1,0:T(8,128)}, u32[]{:S(2)}) copy-start(f32[512,128]{1,0:T(8,128)} %copy-done.9) | copy-start | bytes 786436
  62.8 19.8 %collective-permute-start.12 = (bf16[640,256]{1,0:T(8,128)(2,1)}, bf16[640,256]{1,0:T(8,128)(2,1)}, u32[]{:S(2)}, u32[]{:S(2)}) collective-permute-start(bf16[640,256]{1,0:T(8,128)(2,1)} %get-tuple-element.93), channel_id=1, source_target_pairs={{0,4},{4,0},{8,12},{12,8},{16,20},{20,16},{24,28},{28,24},{1,5},{5... | collective-permute-start | bytes 983048 | tf_op jit(solution)/shard_map/ppermute | solution.py:42
  64.3 22.0 %collective-permute-start.13 = (bf16[512,256]{1,0:T(8,128)(2,1)}, bf16[512,256]{1,0:T(8,128)(2,1)S(1)}, u32[]{:S(2)}, u32[]{:S(2)}) collective-permute-start(bf16[512,256]{1,0:T(8,128)(2,1)} %copy-done.40), channel_id=1, source_target_pairs={{0,8},{4,12},{8,0},{12,4},{16,24},{20,28},{24,16},{28,20},{1,9},{5... | collective-permute-start | bytes 786440 | tf_op jit(solution)/shard_map/ppermute | solution.py:42
  72.7 7.0 %copy-start.20 = (bf16[1280,256]{1,0:T(8,128)(2,1)S(1)}, bf16[1280,256]{1,0:T(8,128)(2,1)}, u32[]{:S(2)}) copy-start(bf16[1280,256]{1,0:T(8,128)(2,1)} %copy-done.19) | copy-start | bytes 1966084
  72.7 7.0 %copy-start.22 = (bf16[1280,256]{1,0:T(8,128)(2,1)S(1)}, bf16[1280,256]{1,0:T(8,128)(2,1)}, u32[]{:S(2)}) copy-start(bf16[1280,256]{1,0:T(8,128)(2,1)} %copy-done.21) | copy-start | bytes 1966084
  77.7 18.4 %copy-start.42 = (bf16[512,256]{1,0:T(8,128)(2,1)}, bf16[512,256]{1,0:T(8,128)(2,1)S(1)}, u32[]{:S(2)}) copy-start(bf16[512,256]{1,0:T(8,128)(2,1)S(1)} %get-tuple-element.97.refs_7_.refs_5_) | copy-start | bytes 786436
  77.7 18.4 %collective-permute-start.15 = (bf16[512,256]{1,0:T(8,128)(2,1)S(1)}, bf16[512,256]{1,0:T(8,128)(2,1)S(1)}, u32[]{:S(2)}, u32[]{:S(2)}) collective-permute-start(bf16[512,256]{1,0:T(8,128)(2,1)S(1)} %get-tuple-element.97.refs_7_.refs_5_), channel_id=1, source_target_pairs={{0,8},{4,12},{8,0},{12,4},{16,24},{20,28},{24,16},{28,20},{1,9},{5... | collective-permute-start | bytes 786440 | tf_op jit(solution)/shard_map/ppermute | solution.py:42
  78.1 27.4 %collective-permute-start.21 = (bf16[512,256]{1,0:T(8,128)(2,1)}, bf16[512,256]{1,0:T(8,128)(2,1)S(1)}, u32[]{:S(2)}, u32[]{:S(2)}) collective-permute-start(bf16[512,256]{1,0:T(8,128)(2,1)} %get-tuple-element.91.refs_0_.refs_6_.refs_8_), channel_id=1, source_target_pairs={{0,8},{4,12},{8,0},{12,4},{16,24},{20,28},{24,16},{28,20},{1,9},{5... | collective-permute-start | bytes 786440 | tf_op jit(solution)/shard_map/ppermute | solution.py:42
  79.7 18.1 %slice-start = ((s8[5242880]{0:T(1024)(128)(4,1)}), s8[4194304]{0:T(1024)(128)(4,1)S(1)}, s32[]{:S(2)}) async-start(s8[5242880]{0:T(1024)(128)(4,1)} %bitcast.47), calls=%async_computation | async-start | bytes 8388608
  82.1 10.2 %collective-permute-start.14 = (bf16[640,256]{1,0:T(8,128)(2,1)S(1)}, bf16[640,256]{1,0:T(8,128)(2,1)S(1)}, u32[]{:S(2)}, u32[]{:S(2)}) collective-permute-start(bf16[640,256]{1,0:T(8,128)(2,1)S(1)} %get-tuple-element.96), channel_id=1, source_target_pairs={{0,4},{4,0},{8,12},{12,8},{16,20},{20,16},{24,28},{28,24},{1,5},{5... | collective-permute-start | bytes 983048 | tf_op jit(solution)/shard_map/ppermute | solution.py:42
  83.7 21.8 %collective-permute-start.20 = (bf16[320,256]{1,0:T(8,128)(2,1)S(1)}, bf16[320,256]{1,0:T(8,128)(2,1)S(1)}, u32[]{:S(2)}, u32[]{:S(2)}) collective-permute-start(bf16[320,256]{1,0:T(8,128)(2,1)S(1)} %slice.39), channel_id=1, source_target_pairs={{0,16},{4,20},{8,24},{12,28},{16,0},{20,4},{24,8},{28,12},{1,17},{... | collective-permute-start | bytes 491528 | tf_op jit(solution)/shard_map/ppermute | solution.py:42
  86.4 11.5 %slice-start.1 = ((s8[5242880]{0:T(1024)(128)(4,1)}), s8[1048576]{0:T(1024)(128)(4,1)S(1)}, s32[]{:S(2)}) async-start(s8[5242880]{0:T(1024)(128)(4,1)} %bitcast.47), calls=%async_computation.1 | async-start | bytes 2097152
  87.5 17.1 %collective-permute-start.18 = (bf16[640,256]{1,0:T(8,128)(2,1)S(1)}, bf16[640,256]{1,0:T(8,128)(2,1)S(1)}, u32[]{:S(2)}, u32[]{:S(2)}) collective-permute-start(bf16[640,256]{1,0:T(8,128)(2,1)S(1)} %get-tuple-element.101), channel_id=1, source_target_pairs={{0,4},{4,0},{8,12},{12,8},{16,20},{20,16},{24,28},{28,24},{1,5},{5... | collective-permute-start | bytes 983048 | tf_op jit(solution)/shard_map/ppermute | solution.py:42
  93.0 28.1 %collective-permute-start.23 = (bf16[320,256]{1,0:T(8,128)(2,1)}, bf16[320,256]{1,0:T(8,128)(2,1)}, u32[]{:S(2)}, u32[]{:S(2)}) collective-permute-start(bf16[320,256]{1,0:T(8,128)(2,1)} %slice.38), channel_id=1, source_target_pairs={{0,16},{4,20},{8,24},{12,28},{16,0},{20,4},{24,8},{28,12},{1,17},{... | collective-permute-start | bytes 491528 | tf_op jit(solution)/shard_map/ppermute | solution.py:42
  97.3 13.8 %collective-permute-start.19 = (bf16[640,256]{1,0:T(8,128)(2,1)S(1)}, bf16[640,256]{1,0:T(8,128)(2,1)S(1)}, u32[]{:S(2)}, u32[]{:S(2)}) collective-permute-start(bf16[640,256]{1,0:T(8,128)(2,1)S(1)} %get-tuple-element.102), channel_id=1, source_target_pairs={{0,4},{4,0},{8,12},{12,8},{16,20},{20,16},{24,28},{28,24},{1,5},{5... | collective-permute-start | bytes 983048 | tf_op jit(solution)/shard_map/ppermute | solution.py:42
  104.6 4.6 %collective-permute-start.16 = (bf16[256,2560]{1,0:T(8,128)(2,1)S(1)}, bf16[256,2560]{1,0:T(8,128)(2,1)S(1)}, u32[]{:S(2)}, u32[]{:S(2)}) collective-permute-start(bf16[256,2560]{1,0:T(8,128)(2,1)S(1)} %get-tuple-element.100.refs_0_), channel_id=1, source_target_pairs={{0,1},{1,0},{2,3},{3,2},{4,5},{5,4},{6,7},{7,6},{8,9},{9,8},{10,11... | collective-permute-start | bytes 3932168 | tf_op jit(solution)/shard_map/ppermute | solution.py:42
  105.5 15.7 %collective-permute-start.24 = (bf16[320,256]{1,0:T(8,128)(2,1)}, bf16[320,256]{1,0:T(8,128)(2,1)}, u32[]{:S(2)}, u32[]{:S(2)}) collective-permute-start(bf16[320,256]{1,0:T(8,128)(2,1)} %slice.37), channel_id=1, source_target_pairs={{0,16},{4,20},{8,24},{12,28},{16,0},{20,4},{24,8},{28,12},{1,17},{... | collective-permute-start | bytes 491528 | tf_op jit(solution)/shard_map/ppermute | solution.py:42
  107.6 10.2 %collective-permute-start.22 = (bf16[640,256]{1,0:T(8,128)(2,1)S(1)}, bf16[640,256]{1,0:T(8,128)(2,1)S(1)}, u32[]{:S(2)}, u32[]{:S(2)}) collective-permute-start(bf16[640,256]{1,0:T(8,128)(2,1)S(1)} %get-tuple-element.104), channel_id=1, source_target_pairs={{0,4},{4,0},{8,12},{12,8},{16,20},{20,16},{24,28},{28,24},{1,5},{5... | collective-permute-start | bytes 983048 | tf_op jit(solution)/shard_map/ppermute | solution.py:42
  110.5 23.7 %collective-permute-start.17 = (bf16[128,2560]{1,0:T(8,128)(2,1)}, bf16[128,2560]{1,0:T(8,128)(2,1)}, u32[]{:S(2)}, u32[]{:S(2)}) collective-permute-start(bf16[128,2560]{1,0:T(8,128)(2,1)} %fusion.1), channel_id=1, source_target_pairs={{0,2},{1,3},{2,0},{3,1},{4,6},{5,7},{6,4},{7,5},{8,10},{9,11},{10,... | collective-permute-start | bytes 1966088 | tf_op jit(solution)/shard_map/ppermute | solution.py:42
  111.9 15.4 %collective-permute-start.25 = (bf16[320,256]{1,0:T(8,128)(2,1)}, bf16[320,256]{1,0:T(8,128)(2,1)}, u32[]{:S(2)}, u32[]{:S(2)}) collective-permute-start(bf16[320,256]{1,0:T(8,128)(2,1)} %slice.36), channel_id=1, source_target_pairs={{0,16},{4,20},{8,24},{12,28},{16,0},{20,4},{24,8},{28,12},{1,17},{... | collective-permute-start | bytes 491528 | tf_op jit(solution)/shard_map/ppermute | solution.py:42
  118.6 12.2 %collective-permute-start.26 = (bf16[320,256]{1,0:T(8,128)(2,1)}, bf16[320,256]{1,0:T(8,128)(2,1)}, u32[]{:S(2)}, u32[]{:S(2)}) collective-permute-start(bf16[320,256]{1,0:T(8,128)(2,1)} %slice.35), channel_id=1, source_target_pairs={{0,16},{4,20},{8,24},{12,28},{16,0},{20,4},{24,8},{28,12},{1,17},{... | collective-permute-start | bytes 491528 | tf_op jit(solution)/shard_map/ppermute | solution.py:42
  (37 other events, 72.7 us)

commit v2 on v0

v2 whole, which is shorter than its diff:
```python
import functools
import math

import jax
import jax.numpy as jnp
from jax import lax
from jax.experimental import pallas as pl
from jax.experimental.pallas import tpu as pltpu
from jax.sharding import PartitionSpec as P

epsilon = 1e-06
log_base = math.log(1000000.0)
bf16 = jnp.bfloat16
f32 = jnp.float32
MIB = 1024 * 1024
LONG = 2.3e10
SHORT = 1e6
SMEM = pl.BlockSpec(memory_space=pltpu.SMEM)
VMEM = pl.BlockSpec(memory_space=pltpu.VMEM)
ANY = pl.BlockSpec(memory_space=pl.ANY)


def call(kernel, scalars, inputs, outputs, name, flops, deps=(), scratch=(), aliases=None, limit=14):
    count = len(deps)

    def body(*refs):
        return kernel(*refs[count:])

    return pl.pallas_call(
        body,
        in_specs=[ANY] * count + [SMEM] * len(scalars) + [VMEM] * len(inputs),
        out_specs=[VMEM] * len(outputs),
        out_shape=[jax.ShapeDtypeStruct(shape, dtype) for shape, dtype in outputs],
        scratch_shapes=list(scratch),
        input_output_aliases={
            count + len(scalars) + i: o for i, o in (aliases or {}).items()
        },
        compiler_params=pltpu.CompilerParams(vmem_limit_bytes=limit * MIB),
        cost_estimate=pl.CostEstimate(
            flops=int(flops), bytes_accessed=1024, transcendentals=0
        ),
        name=name,
    )(*deps, *scalars, *inputs)


def angle_tables(length, width):
    position = jnp.arange(length, dtype=jnp.int32).astype(f32)
    freqs = jnp.exp(jnp.arange(width // 2, dtype=f32) * (-2.0 * log_base / width))
    angles = position[:, None] * freqs[None, :]
    cosine = jnp.cos(angles)
    sine = jnp.sin(angles)
    return jnp.concatenate([cosine, cosine], 1), jnp.concatenate([-sine, sine], 1)


def exchange(value, axis, size, bit):
    return lax.ppermute(value, axis, [(d, d ^ bit) for d in range(size)])


def roll_half(a):
    return pltpu.roll(a, a.shape[-1] // 2, a.ndim - 1)


def norm_gradient(values, gain, grads):
    inverse = lax.rsqrt(jnp.mean(values * values, -1, keepdims=True) + epsilon)
    weighted = gain * grads
    mean = jnp.mean(values * weighted, -1, keepdims=True)
    return inverse * weighted - values * (inverse * inverse * inverse * mean)


def place(me, m, rows):
    return pl.ds(pl.multiple_of((me[0] ^ m) * rows, rows), rows)


def projection_kernel(marks, block, me, s0, s1, wq, wk, wv, q_gain, k_gain, cosine, signed, *rest):
    q_out, u_out, k_out, kp_out, v_out = rest[-5:]
    rows = s0.shape[0]
    width = wk.shape[1]
    span = jnp.concatenate([s0[...], s1[...]], 0)

    def normed_rotated(u, gain, at):
        inverse = lax.rsqrt(jnp.mean(u * u, -1, keepdims=True) + epsilon)
        a = u * inverse * gain[...]
        return (a * cosine[at, :] + roll_half(a) * signed[at, :]).astype(bf16)

    kv = jnp.dot(span, jnp.concatenate([wk[...], wv[...]], 1), preferred_element_type=f32)
    for n, m in enumerate(marks):
        at = place(me, m, rows)
        here = kv[n * rows : (n + 1) * rows]
        kp_out[at, :] = here[:, :width]
        k_out[at, :] = normed_rotated(here[:, :width], k_gain, at)
        v_out[at, :] = here[:, width:].astype(bf16)

    @pl.loop(0, wq.shape[1] // block)
    def _(step):
        start = pl.multiple_of(step * block, block)
        span = jnp.concatenate([s0[...], s1[...]], 0)
        u = jnp.dot(span, wq[:, pl.ds(start, block)], preferred_element_type=f32)
        for n, m in enumerate(marks):
            at = place(me, m, rows)
            for h in range(block // width):
                part = u[n * rows : (n + 1) * rows, h * width : (h + 1) * width]
                columns = pl.ds(pl.multiple_of(start + h * width, width), width)
                u_out[at, columns] = part
                q_out[at, columns] = normed_rotated(part, q_gain, at)


def projections(me, marks, pair, wq, wk, wv, q_gain, k_gain, cosine, signed, previous):
    rows = pair[0].shape[0]
    length = cosine.shape[0]
    columns, width = wq.shape[1], wk.shape[1]
    inputs = (*pair, wq, wk, wv, q_gain, k_gain, cosine, signed)
    return call(
        functools.partial(projection_kernel, marks, 2 * width),
        (me,),
        (*inputs, *previous),
        [
            ((length, columns), bf16),
            ((length, columns), f32),
            ((length, width), bf16),
            ((length, width), f32),
            ((length, width), bf16),
        ],
        "projections",
        LONG,
        aliases={len(inputs) + n: n for n in range(len(previous))},
    )


class Order:
    def __init__(self, dp, features):
        self.dp = dp
        self.pair = 2 if dp > 2 else 1
        self.halving = [1 << i for i in range(dp.bit_length() - 1) if 1 << i != self.pair]
        self.share = features // dp
        self.group = self.pair * self.share
        self.groups = features // (2 * self.group)
        self.aligned = self.group % 128 == 0 and self.share % 16 == 0

    def rank(self, me, shard):
        result = 0
        for n, bit in enumerate(self.halving):
            same = 1 - (((me ^ shard) // bit) & 1)
            result = result + (same << (len(self.halving) - 1 - n))
        return result

    def wanted(self, me, place):
        target = me & self.pair
        for n, bit in enumerate(self.halving):
            same = (place >> (len(self.halving) - 1 - n)) & 1
            target = target | ((me if same else ~me) & bit)
        return target


def transpose_kernel(order, both, me_dp, *refs):
    count = len(refs) - (2 if both else 1)
    for target in range(2 if both else 1):
        owner = me_dp[0] ^ (order.pair * target)
        side = (owner // order.pair) & 1
        out = refs[count + target]
        for n, source in enumerate(refs[:count]):
            rows = source.shape[0]
            for g in range(order.groups):
                start = pl.multiple_of((2 * g + side) * order.group, order.group)
                turned = source[:, pl.ds(start, order.group)].T
                for low in range(order.pair):
                    shard = (2 * g + side) * order.pair + low
                    at = pl.multiple_of(order.rank(owner, shard) * order.share, order.share)
                    out[pl.ds(at, order.share), n * rows : (n + 1) * rows] = turned[
                        low * order.share : (low + 1) * order.share
                    ]


def transposed(order, me_dp, shards, both, deps=()):
    rows, features = shards[0].shape
    size = (features // 2, rows * len(shards))
    if order.aligned:
        return call(
            functools.partial(transpose_kernel, order, both),
            (me_dp.astype(jnp.int32).reshape(1),),
            shards,
            [(size, bf16)] * (2 if both else 1),
            "transposed",
            1e8,
            deps,
        )
    whole = jnp.concatenate(shards, 0).T.reshape(order.dp, order.share, size[1])
    results = []
    for target in range(2 if both else 1):
        owner = me_dp ^ (order.pair * target)
        results.append(
            jnp.concatenate(
                [
                    lax.dynamic_index_in_dim(whole, order.wanted(owner, i), 0, False)
                    for i in range(order.dp // 2)
                ],
                0,
            )
        )
    return results


def attention_kernel(
    group, block, tile, me, lengths, q, u, k, v, c0, c1, c2, c3, q_gain, cosine, signed, *rest
):
    *sums_in, qg_out, dk_out, dv_out, d_out = rest
    length, width = k.shape
    rows = c0.shape[0]
    base = group * block
    c_base = base % c0.shape[1]
    scale = width ** (-0.5)
    constant = scale * math.log2(math.e)
    valid = lengths[0]
    for m, c in enumerate((c0, c1, c2, c3)):
        at = place(me, m, rows)
        part = c[:, c_base : c_base + block].astype(f32)
        position = lax.broadcasted_iota(jnp.int32, part.shape, 0) + (me[0] ^ m) * rows
        d_out[at, :] = jnp.where(position < valid, part, 0.0).astype(bf16)
    for block_index in range(length // tile):
        here = slice(block_index * tile, (block_index + 1) * tile)
        size = (block_index + 1) * tile
        seen = slice(0, size)
        keys = lax.broadcasted_iota(jnp.int32, (size, tile), 0)
        queries = lax.broadcasted_iota(jnp.int32, (size, tile), 1) + block_index * tile
        allowed = (keys <= queries) & (keys < valid)
        dk_sum = dv_sum = None
        for h in range(block // width):
            part = slice(base + h * width, base + (h + 1) * width)
            local_part = slice(h * width, (h + 1) * width)
            q_head = q[here, part]
            o_grad = d_out[here, local_part]
            scores = lax.dot_general(
                k[seen, :], q_head, (((1,), (1,)), ((), ())), preferred_element_type=f32
            )
            weights = jnp.where(allowed, jnp.exp2(scores * constant), 0.0)
            probs = weights * (1.0 / jnp.sum(weights, 0, keepdims=True))
            low = probs.astype(bf16)
            dprob = lax.dot_general(
                v[seen, :], o_grad, (((1,), (1,)), ((), ())), preferred_element_type=f32
            )
            delta = jnp.sum(low.astype(f32) * dprob, 0, keepdims=True)
            dscore = (probs * (dprob - delta)).astype(bf16)
            dq = lax.dot_general(
                dscore, k[seen, :], (((0,), (0,)), ((), ())), preferred_element_type=f32
            ) * scale
            dk_head = jnp.dot(dscore, q_head, preferred_element_type=f32)
            dv_head = jnp.dot(low, o_grad, preferred_element_type=f32)
            dk_sum = dk_head if dk_sum is None else dk_sum + dk_head
            dv_sum = dv_head if dv_sum is None else dv_sum + dv_head
            back = dq * cosine[here, :] - roll_half(dq) * signed[here, :]
            qg_out[here, local_part] = norm_gradient(u[here, part], q_gain[...], back).astype(bf16)
        for out, total, index in ((dk_out, dk_sum, 0), (dv_out, dv_sum, 1)):
            old = size - tile
            if block_index:
                out[:old, :] += total[:old]
            out[old:size, :] = total[old:]
            if sums_in:
                out[old:size, :] += sums_in[index][old:size, :]


def attention_last_kernel(group, block, tile, *refs):
    *inputs, kp, k_gain, dk_in, dv_in, out, d_out, dk_out, dv_out = refs
    attention_kernel(group, block, tile, *inputs, dk_in, dv_in, out, dk_out, dv_out, d_out)
    cosine, signed = inputs[-2:]
    width = kp.shape[1]
    dk = dk_out[...] * width ** (-0.5)
    back = dk * cosine[...] - roll_half(dk) * signed[...]
    out[:, block : block + width] = norm_gradient(kp[...], k_gain[...], back).astype(bf16)
    out[:, block + width :] = dv_out[...].astype(bf16)


def attention(group, last, block, scalars, inputs, k_inputs, sums, deps, flops):
    length, width = inputs[2].shape
    tile = min(256, length)
    settings = (group, block, tile)
    scratch = [pltpu.VMEM((length, block), bf16)]
    grads = ((length, block), bf16)
    if last:
        return call(
            functools.partial(attention_last_kernel, *settings),
            scalars,
            (*inputs, *k_inputs, *sums),
            [((length, block + 2 * width), bf16)],
            "attention",
            flops,
            deps,
            scratch + [pltpu.VMEM((length, width), f32)] * 2,
        )
    return call(
        functools.partial(attention_kernel, *settings),
        scalars,
        (*inputs, *sums),
        [grads] + [((length, width), f32)] * 2,
        "attention",
        flops,
        deps,
        scratch,
    )


def weight_sums(start, me, transposes, own_g, other_g, send, keep):
    columns = slice(start, start + send.shape[1])
    rows = own_g.shape[0] // 4
    half = send.shape[0]
    rhs = [g[place(me, m, rows), columns] for g in (own_g, other_g) for m in range(4)]
    rhs = jnp.concatenate(rhs, 0)
    for out, at in ((send, 0), (keep, half)):
        lhs = jnp.concatenate([t[at : at + half, :] for t in transposes], 1)
        out[...] = jnp.dot(lhs, rhs, preferred_element_type=f32).astype(out.dtype)


def weight_kernel(start, me, *refs):
    *transposes, own_g, other_g, send, keep = refs
    weight_sums(start, me, transposes, own_g, other_g, send, keep)


def both_kernel(start, count, first, tile, me, *refs):
    transposes, refs = refs[:count], refs[count:]
    own_g, other_g, *parts, wq, wk, wv, send, keep, in_send, in_keep, grads = refs
    weight_sums(start, me, transposes, own_g, other_g, send, keep)
    half = in_send.shape[0]
    rows = half // 2
    block = parts[0].shape[1]
    for n, m in enumerate((3, 1, 2, 0)):
        at = place(me, m, rows)
        for g, ref in enumerate(parts):
            here = slice(g * block, g * block + ref.shape[1])
            grads[n * rows : (n + 1) * rows, here] = ref[at, :]

    @pl.loop(0, in_send.shape[1] // tile)
    def _(step):
        at = pl.ds(pl.multiple_of(first + step * tile, tile), tile)
        to = pl.ds(pl.multiple_of(step * tile, tile), tile)
        weights = jnp.concatenate([wq[at, :], wk[at, :], wv[at, :]], 1)
        total = lax.dot_general(
            grads[...], weights, (((1,), (1,)), ((), ())), preferred_element_type=f32
        )
        in_send[:, to] = total[:half].astype(bf16)
        in_keep[:, to] = total[half:]


def weight_products(me, transposes, start, columns, own_g, other_g, deps, flops, extra=None):
    half = transposes[0].shape[0] // 2
    length = own_g.shape[0]
    outputs = [((half, columns), bf16), ((half, columns), f32)]
    inputs = (*transposes, own_g, other_g)
    if extra is None:
        kernel = functools.partial(weight_kernel, start)
        return call(kernel, (me,), inputs, outputs, "weight_products", flops, deps)
    (first, count), parts, weights = extra
    tile = 256 if count % 256 == 0 else count
    return call(
        functools.partial(both_kernel, start, len(transposes), first, tile),
        (me,),
        (*inputs, *parts, *weights),
        outputs + [((length // 2, count), bf16), ((length // 2, count), f32)],
        "both_products",
        flops,
        deps,
        [pltpu.VMEM((length, sum(p.shape[1] for p in parts)), bf16)],
        limit=16,
    )


def halve_kernel(keep, received, send, rest):
    half = send.shape[0]
    send[...] = (keep[:half] + received[:half].astype(f32)).astype(bf16)
    rest[...] = keep[half:] + received[half:].astype(f32)


def halve(keep, received, deps=()):
    rows, columns = keep.shape
    half = rows // 2
    if half % 16:
        total = keep + received.astype(f32)
        return total[:half].astype(bf16), total[half:]
    size = (half, columns)
    return call(halve_kernel, (), (keep, received), [(size, bf16), (size, f32)], "halve", 1e6, deps)


def input_sum_kernel(*refs):
    *inputs, out = refs
    count = len(inputs) // 2
    columns = inputs[0].shape[1]
    for n in range(count):
        total = inputs[n][...] + inputs[count + n][...].astype(f32)
        out[:, n * columns : (n + 1) * columns] = total.astype(bf16)


def final_kernel(first, *refs):
    *inputs, query_out, key_out, value_out = refs[first:]
    width = key_out.shape[1]
    count = len(inputs) // 2
    for n in range(count):
        total = inputs[n][...] + inputs[count + n][...].astype(f32)
        columns = total.shape[1]
        if n < count - 1:
            query_out[:, n * columns : (n + 1) * columns] = total
        else:
            key_out[...] = total[:, :width]
            value_out[...] = total[:, width:]


def final_sums(ends, width, deps):
    share, columns = ends[0][0].shape
    kept = [end[0] for end in ends]
    received = [end[1] for end in ends]
    widths = ((len(ends) - 1) * columns, width, width)
    return pl.pallas_call(
        functools.partial(final_kernel, len(deps)),
        in_specs=[ANY] * len(deps) + [VMEM] * (2 * len(ends)),
        out_shape=[jax.ShapeDtypeStruct((share, w), f32) for w in widths],
        compiler_params=pltpu.CompilerParams(vmem_limit_bytes=14 * MIB),
        cost_estimate=pl.CostEstimate(flops=1024, bytes_accessed=1024, transcendentals=0),
        name="final_sums",
    )(*deps, *kept, *received)


def local(dp, sp, normed, wq, wk, wv, q_gain, k_gain, ctx_grad, lengths):
    rows, features = normed.shape
    width = q_gain.shape[0]
    columns = wq.shape[1]
    length = rows * sp
    block = 2 * width
    groups = columns // block
    me_sp = lax.axis_index("sp")
    me_dp = lax.axis_index("dp")
    me = me_sp.astype(jnp.int32).reshape(1)
    q_gain = q_gain.reshape(1, width)
    k_gain = k_gain.reshape(1, width)
    cosine, signed = angle_tables(length, width)
    over_sp = functools.partial(exchange, axis="sp", size=sp)
    over_dp = functools.partial(exchange, axis="dp", size=dp)
    order = Order(dp, features)

    def cotangent(m, part):
        size = columns // 2
        return lax.dynamic_slice_in_dim(ctx_grad, (me_sp ^ m) * columns + part * size, size, 1)

    far = over_sp(normed, bit=2)
    near = over_sp(normed, bit=1)

    own_o, pair_o = transposed(order, me_dp, (normed,), True)
    other_o = over_dp(pair_o, bit=order.pair)
    (own_n,) = transposed(order, me_dp, (near,), False)
    previous = projections(
        me, (0, 1), (normed, near), wq, wk, wv, q_gain, k_gain, cosine, signed, ()
    )
    cots = [cotangent(m, part) for part in range(2) for m in range(4)]
    far, other_o, own_n, *rest = lax.optimization_barrier((far, other_o, own_n, *previous, *cots))
    previous, cots = rest[: len(previous)], rest[len(previous) :]

    diagonal = over_sp(far, bit=1)
    cs = [
        (cots[4 * part],) + tuple(over_sp(cots[4 * part + m], bit=m) for m in (1, 2, 3))
        for part in range(2)
    ]
    own_f, pair_f = transposed(order, me_dp, (far,), True)
    other_f = over_dp(pair_f, bit=order.pair)
    q, u, k, kp, v = projections(
        me, (2, 3), (far, diagonal), wq, wk, wv, q_gain, k_gain, cosine, signed, previous
    )
    (own_d,) = transposed(order, me_dp, (diagonal,), False, (k, *cs[0][2:]))

    parts, received, firsts = [], [], []
    sums = ()

    def heads(g, deps, flops):
        inputs = (q, u, k, v, *cs[2 * g // groups], q_gain, cosine, signed)
        result = attention(
            g, g == groups - 1, block, (me, lengths), inputs, (kp, k_gain), sums, deps, flops
        )
        parts.append(result[0])
        received.append(over_dp(result[0], bit=order.pair))
        return result[1:]

    def product(n, deps, flops, extra=None):
        send, keep, *more = weight_products(
            me, (own_o, own_n, own_f, own_d, other_o, other_n, other_f, other_d), max(n - groups + 1, 0) * block, block,
            parts[min(n, groups - 1)], received[min(n, groups - 1)], deps, flops, extra,
        )
        firsts.append((keep, over_dp(send, bit=order.halving[0])))
        return (keep, *more)

    def input_part(n):
        return ((n * features // 2, features // 2), parts, (wq, wk, wv))

    def halved(sent, kept):
        sent, kept = halve(kept, over_sp(sent, bit=1))
        return kept, over_sp(sent, bit=2)

    def last_steps(keep, came, deps=()):
        for bit in order.halving[1:]:
            send, keep = halve(keep, came, deps)
            came = over_dp(send, bit=bit)
        return keep, came

    sums = heads(0, (own_d,), SHORT)
    other_o, other_f, tied = lax.optimization_barrier((other_o, other_f, sums[0]))
    sums = (tied, sums[1])
    other_n, other_d = over_sp(other_o, bit=1), over_sp(other_f, bit=1)
    sums = heads(1, (), LONG)
    sums = heads(2, (received[0],), LONG)
    keep, = product(0, (sums[0],), SHORT)
    heads(3, (keep, received[1]), LONG)
    keep, = product(1, (parts[3],), SHORT)
    ends = [last_steps(*firsts[0])]
    keep, sent, kept = product(2, (keep, ends[0][0]), LONG, input_part(0))
    inputs = [halved(sent, kept)]
    ends.append(last_steps(*firsts[1]))
    keep, sent, kept = product(3, (keep, ends[1][0], ends[0][1]), LONG, input_part(1))
    ends.append(last_steps(*firsts[2]))
    product(4, (keep, ends[2][0], ends[1][1], inputs[0][0]), LONG)
    inputs.append(halved(sent, kept))
    ends.append(last_steps(*firsts[3]))
    ends.append(last_steps(*firsts[4], (ends[2][1],)))
    pieces = [i[0] for i in inputs] + [i[1] for i in inputs]
    input_gradient = pl.pallas_call(
        input_sum_kernel,
        in_specs=[VMEM] * len(pieces),
        out_shape=jax.ShapeDtypeStruct((rows, features), bf16),
        compiler_params=pltpu.CompilerParams(vmem_limit_bytes=14 * MIB),
        cost_estimate=pl.CostEstimate(flops=1024, bytes_accessed=1024, transcendentals=0),
        name="input_sum",
    )(*pieces)
    return (input_gradient, *final_sums(ends, width, (input_gradient,)))


def solution(mesh):
    in_specs = (
        P(("dp", "sp"), None),
        P(None, "sp"),
        P(None, "sp"),
        P(None, "sp"),
        P(),
        P(),
        P(("dp", "sp"), None),
        P("dp"),
    )
    out_specs = (P(("dp", "sp"), None), P("dp", "sp"), P("dp", "sp"), P("dp", "sp"))
    body = functools.partial(local, mesh.shape["dp"], mesh.shape["sp"])
    return jax.shard_map(body, mesh=mesh, in_specs=in_specs, out_specs=out_specs, check_vma=False)
```

time: 397 us -> 104 us (0.26)
  waiting for transfers between devices: 271 us -> 32.3 us
  matrix products: 52.9 us -> 0 us
  local copies, waits for them, and re-layouts: 41.8 us -> 4.91 us
  Pallas kernels: 0 us -> 30.7 us
  starting transfers between devices: 4.29 us -> 33.1 us
  between operations: 15.3 us -> 1.59 us
  other arithmetic: 11.1 us -> 1.21 us
    unnamed x4 -> x0, waiting for transfers between devices: 218 us -> none
    dot_general x55 -> x0, matrix products: 52.9 us -> none  [the longest x1 10.7 us: column_product(): lax.dot_general(span, grads, (((0,), (0,)), ((), ())), preferred_element_...]
    ppermute x0 -> x31, starting transfers between devices: none -> 33.1 us  [exchange(): return lax.ppermute(value, axis, [(d, d ^ bit) for d in range(size)])]
    ppermute x0 -> x31, waiting for transfers between devices: none -> 32.3 us  [exchange(): return lax.ppermute(value, axis, [(d, d ^ bit) for d in range(size)])]
    pallas_call x0 -> x24, Pallas kernels: none -> 30.7 us  [the longest x22 28.5 us: call(): pl.pallas_call(body, in_specs=[ANY] * count + [SMEM] * len(scalars) + [VM...]
    reduce_scatter x1 -> x0, waiting for transfers between devices: 26.5 us -> none  [local(): lax.psum_scatter(total + lax.dot_general(value_gradient, value_weight, ((...]
    unnamed x79 -> x20, local copies, waits for them, and re-layouts: 29.1 us -> 4.79 us
    all_to_all x1 -> x0, waiting for transfers between devices: 20.4 us -> none  [local(): lax.all_to_all(ctx_grad, 'sp', split_axis=1, concat_axis=0, tiled=True)]
  transfers between devices with their start and end apart: 4 -> 31, of which waited for: 4 -> 11; matrix products, arithmetic and copies ran while one was open for 8% -> 1% of each run, Pallas kernels for 0% -> 28%
where the time goes in v2:
time: 104 us
  starting transfers between devices  33.1 us (32%)
  waiting for transfers between devices  32.3 us (31%)
  Pallas kernels  30.7 us (30%)
  local copies, waits for them, and re-layouts  4.91 us (5%)
  between operations  1.59 us (2%)
  other arithmetic  1.21 us (1%)
    ppermute x31, starting transfers between devices, exchange(): return lax.ppermute(value, axis, [(d, d ^ bit) for d in range(size)])  33.1 us
    ppermute x31, waiting for transfers between devices, exchange(): return lax.ppermute(value, axis, [(d, d ^ bit) for d in range(size)])  32.3 us
    pallas_call x22, Pallas kernels, call(): pl.pallas_call(body, in_specs=[ANY] * count + [SMEM] * len(scalars) + [VM...  28.5 us
    unnamed x20, local copies, waits for them, and re-layouts  4.79 us
  transfers between devices with their start and end apart: 31, of which 11 were waited for; matrix products, arithmetic and copies ran while one was open for 1% of the time, Pallas kernels for 28%

profile of v2, /device:TPU:0, one launch (start us, length us, event | category | flops | bytes accessed | tf_op | source)
XLA Modules:
  0.0 103.8 jit_solution(11741768387682128746)
XLA Ops:
  0.6 3.0 %collective-permute-start = (bf16[128,2560]{1,0:T(8,128)(2,1)}, bf16[128,2560]{1,0:T(8,128)(2,1)S(1)}, u32[]{:S(2)}, u32[]{:S(2)}) collective-permute-start(bf16[128,2560]{1,0:T(8,128)(2,1)} %refs_1_.4), channel_id=1, source_target_pairs={{0,2},{1,3},{2,0},{3,1},{4,6},{5,7},{6,4},{7,5},{8,10},{9,11},{10,... | collective-permute-start | bytes 1966088 | tf_op jit(solution)/shard_map/ppermute | solution.py:56
  3.6 1.1 %copy-done.1 = bf16[128,2560]{1,0:T(8,128)(2,1)S(1)} copy-done((bf16[128,2560]{1,0:T(8,128)(2,1)S(1)}, bf16[128,2560]{1,0:T(8,128)(2,1)}, u32[]{:S(2)}) %copy-start.1) | copy-done | bytes 655384
  5.0 1.6 %collective-permute-start.1 = (bf16[1280,128]{1,0:T(8,128)(2,1)S(1)}, bf16[1280,128]{1,0:T(8,128)(2,1)S(1)}, u32[]{:S(2)}, u32[]{:S(2)}) collective-permute-start(bf16[1280,128]{1,0:T(8,128)(2,1)S(1)} %get-tuple-element.77), channel_id=1, source_target_pairs={{0,8},{4,12},{8,0},{12,4},{16,24},{20,28},{24,16},{28,20},{1,9},{5... | collective-permute-start | bytes 983048 | tf_op jit(solution)/shard_map/ppermute | solution.py:56
  6.7 1.0 fusion
  8.2 2.5 %copy-done.4 = bf16[2560,1024]{1,0:T(8,128)(2,1)S(1)} copy-done((bf16[2560,1024]{1,0:T(8,128)(2,1)S(1)}, bf16[2560,1024]{1,0:T(8,128)(2,1)}, u32[]{:S(2)}) %copy-start.4) | copy-done | bytes 5242904
  10.6 3.6 %projections.2 = (bf16[512,1024]{1,0:T(8,128)(2,1)S(1)}, f32[512,1024]{1,0:T(8,128)S(1)}, bf16[512,128]{1,0:T(8,128)(2,1)S(1)}, f32[512,128]{1,0:T(8,128)S(1)}, bf16[512,128]{1,0:T(8,128)(2,1)S(1)}) custom-call(s32[1]{0:T(128)} %bitcast.refs_0_.refs_1_.refs_2_.refs_3_.refs_4_, bf16[128,2560]{1,0:T(8,128)(2,1)S(1)} %copy-done.2, ...), custom_call_target="tpu_custom_call" | custom-call | flops 23000000512 | bytes 1024 | tf_op jit(solution)/shard_map/projections/pallas_call | solution.py:29
  14.4 0.8 collective-permute-done.1.refs_6_.refs_7_.refs_8_.refs_9_
  15.1 3.4 %collective-permute-done.refs_1_ = bf16[128,2560]{1,0:T(8,128)(2,1)S(1)} collective-permute-done((bf16[128,2560]{1,0:T(8,128)(2,1)}, bf16[128,2560]{1,0:T(8,128)(2,1)S(1)}, u32[]{:S(2)}, u32[]{:S(2)}) %collective-permute-start) | collective-permute-done | bytes 655392 | tf_op jit(solution)/shard_map/ppermute | solution.py:56
  19.2 1.8 %collective-permute-start.4 = (bf16[128,512]{1,0:T(8,128)(2,1)S(1)}, bf16[128,512]{1,0:T(8,128)(2,1)S(1)}, u32[]{:S(2)}, u32[]{:S(2)}) collective-permute-start(bf16[128,512]{1,0:T(8,128)(2,1)S(1)} %get-tuple-element.90), channel_id=1, source_target_pairs={{0,2},{1,3},{2,0},{3,1},{4,6},{5,7},{6,4},{7,5},{8,10},{9,11},{10,... | collective-permute-start | bytes 393224 | tf_op jit(solution)/shard_map/ppermute | solution.py:56
  22.0 1.8 %collective-permute-start.11 = (bf16[1280,128]{1,0:T(8,128)(2,1)S(1)}, bf16[1280,128]{1,0:T(8,128)(2,1)S(1)}, u32[]{:S(2)}, u32[]{:S(2)}) collective-permute-start(bf16[1280,128]{1,0:T(8,128)(2,1)S(1)} %get-tuple-element.103), channel_id=1, source_target_pairs={{0,8},{4,12},{8,0},{12,4},{16,24},{20,28},{24,16},{28,20},{1,9},{5... | collective-permute-start | bytes 983048 | tf_op jit(solution)/shard_map/ppermute | solution.py:56
  23.8 3.7 %projections.3 = (bf16[512,1024]{1,0:T(8,128)(2,1)S(1)}, f32[512,1024]{1,0:T(8,128)S(1)}, bf16[512,128]{1,0:T(8,128)(2,1)S(1)}, f32[512,128]{1,0:T(8,128)S(1)}, bf16[512,128]{1,0:T(8,128)(2,1)S(1)}) custom-call(s32[1]{0:T(128)} %bitcast.refs_0_.refs_1_.refs_2_.refs_3_.refs_4_, ...), custom_call_target="tpu_custom_call", output_to_operand_aliasing={{0}: (10, {}), {1}: (11, {}), {2}: (12, {}), {3}: (13, {}),... | custom-call | flops 23000000512 | bytes 1024 | tf_op jit(solution)/shard_map/projections/pallas_call | solution.py:29
  27.6 1.6 %collective-permute-start.9 = (bf16[128,512]{1,0:T(8,128)(2,1)S(1)}, bf16[128,512]{1,0:T(8,128)(2,1)S(1)}, u32[]{:S(2)}, u32[]{:S(2)}) collective-permute-start(bf16[128,512]{1,0:T(8,128)(2,1)S(1)} %get-tuple-element.100), channel_id=1, source_target_pairs={{0,2},{1,3},{2,0},{3,1},{4,6},{5,7},{6,4},{7,5},{8,10},{9,11},{10,... | collective-permute-start | bytes 393224 | tf_op jit(solution)/shard_map/ppermute | solution.py:56
  29.6 2.4 %attention.4 = (bf16[512,256]{1,0:T(8,128)(2,1)S(1)}, f32[512,128]{1,0:T(8,128)S(1)}, f32[512,128]{1,0:T(8,128)S(1)}) custom-call(bf16[1280,128]{1,0:T(8,128)(2,1)S(1)} %transposed.6.refs_0_.refs_5_.refs_6_.refs_7_.refs_8_, s32[1]{0:T(128)} %bitcast.refs_0_.refs_1_.refs_2_.refs_3_.refs_4_, s32[1]{0:T(128)S(6)} %copy.22.refs_2_.refs_1_.refs_3_, ...), custom_call_target="tpu_custom_call" | custom-call | flops 1000000 | bytes 1024 | tf_op jit(solution)/shard_map/attention/pallas_call | solution.py:29
  32.0 1.6 %collective-permute-start.7 = (bf16[512,256]{1,0:T(8,128)(2,1)S(1)}, bf16[512,256]{1,0:T(8,128)(2,1)S(1)}, u32[]{:S(2)}, u32[]{:S(2)}) collective-permute-start(bf16[512,256]{1,0:T(8,128)(2,1)S(1)} %get-tuple-element.97.refs_10_.refs_13_.refs_14_), channel_id=1, source_target_pairs={{0,8},{4,12},{8,0},{12,4},{16,24},{20,28},{24,16},{28,20},{1,9},{5... | collective-permute-start | bytes 786440 | tf_op jit(solution)/shard_map/ppermute | solution.py:56
  33.6 2.4 %attention.5 = (bf16[512,256]{1,0:T(8,128)(2,1)S(1)}, f32[512,128]{1,0:T(8,128)S(1)}, f32[512,128]{1,0:T(8,128)S(1)}) custom-call(s32[1]{0:T(128)} %bitcast.refs_0_.refs_1_.refs_2_.refs_3_.refs_4_, s32[1]{0:T(128)S(6)} %copy.22.refs_2_.refs_1_.refs_3_, bf16[512,1024]{1,0:T(8,128)(2,1)S(1)} %get-tuple-element.92.refs_3_.refs_2_.refs_4_, ...), custom_call_target="tpu_custom_call" | custom-call | flops 23000000512 | bytes 1024 | tf_op jit(solution)/shard_map/attention/pallas_call | solution.py:29
  36.0 0.6 collective-permute-start.13
  37.1 4.1 %collective-permute-done.7.refs_0_.refs_11_ = bf16[512,256]{1,0:T(8,128)(2,1)S(1)} collective-permute-done((bf16[512,256]{1,0:T(8,128)(2,1)S(1)}, bf16[512,256]{1,0:T(8,128)(2,1)S(1)}, u32[]{:S(2)}, u32[]{:S(2)}) %collective-permute-start.7) | collective-permute-done | bytes 262176 | tf_op jit(solution)/shard_map/ppermute | solution.py:56
  41.2 2.4 %attention.6 = (bf16[512,256]{1,0:T(8,128)(2,1)S(1)}, f32[512,128]{1,0:T(8,128)S(1)}, f32[512,128]{1,0:T(8,128)S(1)}) custom-call(bf16[512,256]{1,0:T(8,128)(2,1)S(1)} %collective-permute-done.7.refs_0_.refs_11_, s32[1]{0:T(128)} %bitcast.refs_0_.refs_1_.refs_2_.refs_3_.refs_4_, s32[1]{0:T(128)S(6)} %copy.22.refs_2_.refs_1_.refs_3_, ...), custom_call_target="tpu_custom_call" | custom-call | flops 23000000512 | bytes 1024 | tf_op jit(solution)/shard_map/attention/pallas_call | solution.py:29
  43.6 1.7 %collective-permute-start.16 = (bf16[512,256]{1,0:T(8,128)(2,1)S(1)}, bf16[512,256]{1,0:T(8,128)(2,1)S(1)}, u32[]{:S(2)}, u32[]{:S(2)}) collective-permute-start(bf16[512,256]{1,0:T(8,128)(2,1)S(1)} %get-tuple-element.122.refs_11_.refs_15_.refs_16_), channel_id=1, source_target_pairs={{0,8},{4,12},{8,0},{12,4},{16,24},{20,28},{24,16},{28,20},{1,9},{5... | collective-permute-start | bytes 786440 | tf_op jit(solution)/shard_map/ppermute | solution.py:56
  45.3 0.8 weight_products.3
  46.1 1.6 %collective-permute-start.15 = (bf16[640,256]{1,0:T(8,128)(2,1)S(1)}, bf16[640,256]{1,0:T(8,128)(2,1)S(1)}, u32[]{:S(2)}, u32[]{:S(2)}) collective-permute-start(bf16[640,256]{1,0:T(8,128)(2,1)S(1)} %get-tuple-element.120), channel_id=1, source_target_pairs={{0,4},{4,0},{8,12},{12,8},{16,20},{20,16},{24,28},{28,24},{1,5},{5... | collective-permute-start | bytes 983048 | tf_op jit(solution)/shard_map/ppermute | solution.py:56
  47.7 2.9 %attention.7.refs_0_.refs_16_.refs_12_.refs_17_.refs_13_ = bf16[512,512]{1,0:T(8,128)(2,1)S(1)} custom-call(f32[640,256]{1,0:T(8,128)S(1)} %get-tuple-element.115.refs_0_, bf16[512,256]{1,0:T(8,128)(2,1)S(1)} %collective-permute-done.14.refs_1_.refs_11_, s32[1]{0:T(128)} %bitcast.refs_0_.refs_1_.refs_2_.refs_3_.refs_4_, s32[1]{0:T(128)S(6)} %copy.22.refs_2_.refs_1_.refs_3_, ...), custom_call_target="tpu_custom_call" | custom-call | flops 23000000512 | bytes 1024 | tf_op jit(solution)/shard_map/attention/pallas_call | solution.py:29
  50.6 0.8 collective-permute-start.20
  51.3 0.8 weight_products.4
  52.2 1.6 %collective-permute-start.18 = (bf16[640,256]{1,0:T(8,128)(2,1)S(1)}, bf16[640,256]{1,0:T(8,128)(2,1)S(1)}, u32[]{:S(2)}, u32[]{:S(2)}) collective-permute-start(bf16[640,256]{1,0:T(8,128)(2,1)S(1)} %get-tuple-element.127), channel_id=1, source_target_pairs={{0,4},{4,0},{8,12},{12,8},{16,20},{20,16},{24,28},{28,24},{1,5},{5... | collective-permute-start | bytes 983048 | tf_op jit(solution)/shard_map/ppermute | solution.py:56
  53.8 0.8 collective-permute-done.15.refs_1_
  54.7 2.7 %collective-permute-start.19 = (bf16[320,256]{1,0:T(8,128)(2,1)S(1)}, bf16[320,256]{1,0:T(8,128)(2,1)S(1)}, u32[]{:S(2)}, u32[]{:S(2)}) collective-permute-start(bf16[320,256]{1,0:T(8,128)(2,1)S(1)} %get-tuple-element.129), channel_id=1, source_target_pairs={{0,16},{4,20},{8,24},{12,28},{16,0},{20,4},{24,8},{28,12},{1,17},{... | collective-permute-start | bytes 491528 | tf_op jit(solution)/shard_map/ppermute | solution.py:56
  57.3 3.8 %both_products.2 = (bf16[640,256]{1,0:T(8,128)(2,1)S(1)}, f32[640,256]{1,0:T(8,128)S(1)}, bf16[256,1280]{1,0:T(8,128)(2,1)S(1)}, f32[256,1280]{1,0:T(8,128)S(1)}) custom-call(f32[640,256]{1,0:T(8,128)S(1)} %get-tuple-element.119.refs_0_, f32[320,256]{1,0:T(8,128)S(1)} %get-tuple-element.121.refs_1_, s32[1]{0:T(128)} %bitcast.refs_0_.refs_1_.refs_2_.refs_3_.refs_4_, ...), custom_call_target="tpu_custom_call" | custom-call | flops 23000000512 | bytes 1024 | tf_op jit(solution)/shard_map/both_products/pallas_call | solution.py:29
  61.3 1.6 %collective-permute-start.24 = (bf16[640,256]{1,0:T(8,128)(2,1)S(1)}, bf16[640,256]{1,0:T(8,128)(2,1)S(1)}, u32[]{:S(2)}, u32[]{:S(2)}) collective-permute-start(bf16[640,256]{1,0:T(8,128)(2,1)S(1)} %get-tuple-element.135), channel_id=1, source_target_pairs={{0,4},{4,0},{8,12},{12,8},{16,20},{20,16},{24,28},{28,24},{1,5},{5... | collective-permute-start | bytes 983048 | tf_op jit(solution)/shard_map/ppermute | solution.py:56
  62.9 0.6 collective-permute-start.27
  63.5 3.7 %collective-permute-done.19.refs_2_.refs_6_ = bf16[320,256]{1,0:T(8,128)(2,1)S(1)} collective-permute-done((bf16[320,256]{1,0:T(8,128)(2,1)S(1)}, bf16[320,256]{1,0:T(8,128)(2,1)S(1)}, u32[]{:S(2)}, u32[]{:S(2)}) %collective-permute-start.19) | collective-permute-done | bytes 163872 | tf_op jit(solution)/shard_map/ppermute | solution.py:56
  67.1 3.6 %both_products.3 = (bf16[640,256]{1,0:T(8,128)(2,1)S(1)}, f32[640,256]{1,0:T(8,128)S(1)}, bf16[256,1280]{1,0:T(8,128)(2,1)S(1)}, f32[256,1280]{1,0:T(8,128)S(1)}) custom-call(f32[640,256]{1,0:T(8,128)S(1)} %get-tuple-element.126.refs_0_, f32[320,256]{1,0:T(8,128)S(1)} %get-tuple-element.128.refs_1_.refs_2_, ...), custom_call_target="tpu_custom_call" | custom-call | flops 23000000512 | bytes 1024 | tf_op jit(solution)/shard_map/both_products/pallas_call | solution.py:29
  70.8 1.6 %collective-permute-start.25 = (bf16[640,256]{1,0:T(8,128)(2,1)S(1)}, bf16[640,256]{1,0:T(8,128)(2,1)S(1)}, u32[]{:S(2)}, u32[]{:S(2)}) collective-permute-start(bf16[640,256]{1,0:T(8,128)(2,1)S(1)} %get-tuple-element.138), channel_id=1, source_target_pairs={{0,4},{4,0},{8,12},{12,8},{16,20},{20,16},{24,28},{28,24},{1,5},{5... | collective-permute-start | bytes 983048 | tf_op jit(solution)/shard_map/ppermute | solution.py:56
  72.6 2.8 %collective-permute-done.27.refs_2_.refs_7_ = bf16[320,256]{1,0:T(8,128)(2,1)S(1)} collective-permute-done((bf16[320,256]{1,0:T(8,128)(2,1)S(1)}, bf16[320,256]{1,0:T(8,128)(2,1)S(1)}, u32[]{:S(2)}, u32[]{:S(2)}) %collective-permute-start.27) | collective-permute-done | bytes 163872 | tf_op jit(solution)/shard_map/ppermute | solution.py:56
  75.4 0.8 weight_products.5
  76.2 1.3 %collective-permute-start.28 = (bf16[640,256]{1,0:T(8,128)(2,1)S(1)}, bf16[640,256]{1,0:T(8,128)(2,1)S(1)}, u32[]{:S(2)}, u32[]{:S(2)}) collective-permute-start(bf16[640,256]{1,0:T(8,128)(2,1)S(1)} %get-tuple-element.143), channel_id=1, source_target_pairs={{0,4},{4,0},{8,12},{12,8},{16,20},{20,16},{24,28},{28,24},{1,5},{5... | collective-permute-start | bytes 983048 | tf_op jit(solution)/shard_map/ppermute | solution.py:56
  77.5 1.5 %collective-permute-start.22 = (bf16[128,1280]{1,0:T(8,128)(2,1)S(1)}, bf16[128,1280]{1,0:T(8,128)(2,1)S(1)}, u32[]{:S(2)}, u32[]{:S(2)}) collective-permute-start(bf16[128,1280]{1,0:T(8,128)(2,1)S(1)} %get-tuple-element.133), channel_id=1, source_target_pairs={{0,2},{1,3},{2,0},{3,1},{4,6},{5,7},{6,4},{7,5},{8,10},{9,11},{10,... | collective-permute-start | bytes 983048 | tf_op jit(solution)/shard_map/ppermute | solution.py:56
  79.1 0.6 collective-permute-start.23
  79.7 1.7 %collective-permute-done.25.refs_1_ = bf16[640,256]{1,0:T(8,128)(2,1)S(1)} collective-permute-done((bf16[640,256]{1,0:T(8,128)(2,1)S(1)}, bf16[640,256]{1,0:T(8,128)(2,1)S(1)}, u32[]{:S(2)}, u32[]{:S(2)}) %collective-permute-start.25) | collective-permute-done | bytes 327712 | tf_op jit(solution)/shard_map/ppermute | solution.py:56
  81.5 3.5 %collective-permute-start.29 = (bf16[320,256]{1,0:T(8,128)(2,1)S(1)}, bf16[320,256]{1,0:T(8,128)(2,1)S(1)}, u32[]{:S(2)}, u32[]{:S(2)}) collective-permute-start(bf16[320,256]{1,0:T(8,128)(2,1)S(1)} %get-tuple-element.145), channel_id=1, source_target_pairs={{0,16},{4,20},{8,24},{12,28},{16,0},{20,4},{24,8},{28,12},{1,17},{... | collective-permute-start | bytes 491528 | tf_op jit(solution)/shard_map/ppermute | solution.py:56
  85.0 6.0 %collective-permute-done.26.refs_0_.refs_8_ = bf16[320,256]{1,0:T(8,128)(2,1)S(1)} collective-permute-done((bf16[320,256]{1,0:T(8,128)(2,1)S(1)}, bf16[320,256]{1,0:T(8,128)(2,1)S(1)}, u32[]{:S(2)}, u32[]{:S(2)}) %collective-permute-start.26) | collective-permute-done | bytes 163872 | tf_op jit(solution)/shard_map/ppermute | solution.py:56
  91.0 0.5 collective-permute-start.30
  91.5 2.2 %collective-permute-done.23.refs_3_ = bf16[128,1280]{1,0:T(8,128)(2,1)S(1)} collective-permute-done((bf16[128,1280]{1,0:T(8,128)(2,1)S(1)}, bf16[128,1280]{1,0:T(8,128)(2,1)S(1)}, u32[]{:S(2)}, u32[]{:S(2)}) %collective-permute-start.23) | collective-permute-done | bytes 327712 | tf_op jit(solution)/shard_map/ppermute | solution.py:56
  93.7 1.0 input_sum.1.refs_0_
  94.7 3.3 %collective-permute-done.29.refs_9_ = bf16[320,256]{1,0:T(8,128)(2,1)S(1)} collective-permute-done((bf16[320,256]{1,0:T(8,128)(2,1)S(1)}, bf16[320,256]{1,0:T(8,128)(2,1)S(1)}, u32[]{:S(2)}, u32[]{:S(2)}) %collective-permute-start.29) | collective-permute-done | bytes 163872 | tf_op jit(solution)/shard_map/ppermute | solution.py:56
  98.0 3.4 %collective-permute-done.30.refs_10_ = bf16[320,256]{1,0:T(8,128)(2,1)S(1)} collective-permute-done((bf16[320,256]{1,0:T(8,128)(2,1)S(1)}, bf16[320,256]{1,0:T(8,128)(2,1)S(1)}, u32[]{:S(2)}, u32[]{:S(2)}) %collective-permute-start.30) | collective-permute-done | bytes 163872 | tf_op jit(solution)/shard_map/ppermute | solution.py:56
  101.4 1.1 %copy-done = bf16[128,2560]{1,0:T(8,128)(2,1)S(1)} copy-done((bf16[128,2560]{1,0:T(8,128)(2,1)S(1)}, bf16[128,2560]{1,0:T(8,128)(2,1)}, u32[]{:S(2)}) %copy-start) | copy-done | bytes 655384
  102.5 1.3 %final_sums.1 = (f32[320,1024]{1,0:T(8,128)}, f32[320,128]{1,0:T(8,128)}, f32[320,128]{1,0:T(8,128)}) custom-call(bf16[128,2560]{1,0:T(8,128)(2,1)S(1)} %copy-done, f32[320,256]{1,0:T(8,128)S(1)} %get-tuple-element.121.refs_1_, f32[320,256]{1,0:T(8,128)S(1)} %get-tuple-element.128.refs_1_.refs_2_, f32[320,256]{1,0:T(8,128)S(1)} %get-tuple-element.136.refs_1_.refs_3_, ...), custom_call_target="tpu_custom_call" | custom-call | flops 1024 | bytes 1024 | tf_op jit(solution)/shard_map/final_sums/pallas_call | solution.py:408
  (63 shorter events, 3.4 us)
Async XLA Ops:
  0.6 17.9 %collective-permute-start = (bf16[128,2560]{1,0:T(8,128)(2,1)}, bf16[128,2560]{1,0:T(8,128)(2,1)S(1)}, u32[]{:S(2)}, u32[]{:S(2)}) collective-permute-start(bf16[128,2560]{1,0:T(8,128)(2,1)} %refs_1_.4), channel_id=1, source_target_pairs={{0,2},{1,3},{2,0},{3,1},{4,6},{5,7},{6,4},{7,5},{8,10},{9,11},{10,... | collective-permute-start | bytes 1966088 | tf_op jit(solution)/shard_map/ppermute | solution.py:56
  3.6 4.4 %collective-permute-start.2 = (bf16[128,2560]{1,0:T(8,128)(2,1)}, bf16[128,2560]{1,0:T(8,128)(2,1)S(1)}, u32[]{:S(2)}, u32[]{:S(2)}) collective-permute-start(bf16[128,2560]{1,0:T(8,128)(2,1)} %refs_1_.4), channel_id=1, source_target_pairs={{0,1},{1,0},{2,3},{3,2},{4,5},{5,4},{6,7},{7,6},{8,9},{9,8},{10,11... | collective-permute-start | bytes 1966088 | tf_op jit(solution)/shard_map/ppermute | solution.py:56
  3.6 1.1 %copy-start.1 = (bf16[128,2560]{1,0:T(8,128)(2,1)S(1)}, bf16[128,2560]{1,0:T(8,128)(2,1)}, u32[]{:S(2)}) copy-start(bf16[128,2560]{1,0:T(8,128)(2,1)} %refs_1_.4) | copy-start | bytes 1966084
  4.8 3.2 %copy-start.9 = (bf16[128,4096]{1,0:T(8,128)(2,1)S(1)}, bf16[128,4096]{1,0:T(8,128)(2,1)}, u32[]{:S(2)}) copy-start(bf16[128,4096]{1,0:T(8,128)(2,1)} %param.14) | copy-start | bytes 3145732
  5.0 10.2 %collective-permute-start.1 = (bf16[1280,128]{1,0:T(8,128)(2,1)S(1)}, bf16[1280,128]{1,0:T(8,128)(2,1)S(1)}, u32[]{:S(2)}, u32[]{:S(2)}) collective-permute-start(bf16[1280,128]{1,0:T(8,128)(2,1)S(1)} %get-tuple-element.77), channel_id=1, source_target_pairs={{0,8},{4,12},{8,0},{12,4},{16,24},{20,28},{24,16},{28,20},{1,9},{5... | collective-permute-start | bytes 983048 | tf_op jit(solution)/shard_map/ppermute | solution.py:56
  6.6 1.4 %copy-start.2 = (bf16[128,2560]{1,0:T(8,128)(2,1)S(1)}, bf16[128,2560]{1,0:T(8,128)(2,1)}, u32[]{:S(2)}) copy-start(bf16[128,2560]{1,0:T(8,128)(2,1)} %refs_1_.4) | copy-start | bytes 1966084
  6.6 1.4 %copy-start.3 = (f32[128]{0:T(128)S(1)}, f32[128]{0:T(128)}, u32[]{:S(2)}) copy-start(f32[128]{0:T(128)} %param.12) | copy-start | bytes 1540
  6.7 1.4 %copy-start.6 = (bf16[2560,128]{1,0:T(8,128)(2,1)S(1)}, bf16[2560,128]{1,0:T(8,128)(2,1)}, u32[]{:S(2)}) copy-start(bf16[2560,128]{1,0:T(8,128)(2,1)} %refs_19_.3) | copy-start | bytes 1966084
  6.7 1.5 %copy-start.7 = (bf16[2560,128]{1,0:T(8,128)(2,1)S(1)}, bf16[2560,128]{1,0:T(8,128)(2,1)}, u32[]{:S(2)}) copy-start(bf16[2560,128]{1,0:T(8,128)(2,1)} %refs_20_.1) | copy-start | bytes 1966084
  6.7 1.5 %copy-start.8 = (f32[128]{0:T(128)S(1)}, f32[128]{0:T(128)}, u32[]{:S(2)}) copy-start(f32[128]{0:T(128)} %param.13) | copy-start | bytes 1540
  8.2 2.5 %copy-start.4 = (bf16[2560,1024]{1,0:T(8,128)(2,1)S(1)}, bf16[2560,1024]{1,0:T(8,128)(2,1)}, u32[]{:S(2)}) copy-start(bf16[2560,1024]{1,0:T(8,128)(2,1)} %refs_18_.3) | copy-start | bytes 15728644
  10.6 13.2 %copy-start.5 = (bf16[2560,1024]{1,0:T(8,128)(2,1)S(1)}, bf16[2560,1024]{1,0:T(8,128)(2,1)}, u32[]{:S(2)}) copy-start(bf16[2560,1024]{1,0:T(8,128)(2,1)} %refs_18_.3) | copy-start | bytes 15728644
  18.6 3.4 %collective-permute-start.3 = (bf16[128,2560]{1,0:T(8,128)(2,1)S(1)}, bf16[128,2560]{1,0:T(8,128)(2,1)S(1)}, u32[]{:S(2)}, u32[]{:S(2)}) collective-permute-start(bf16[128,2560]{1,0:T(8,128)(2,1)S(1)} %collective-permute-done.refs_1_), channel_id=1, source_target_pairs={{0,1},{1,0},{2,3},{3,2},{4,5},{5,4},{6,7},{7,6},{8,9},{9,8},{10,11... | collective-permute-start | bytes 1966088 | tf_op jit(solution)/shard_map/ppermute | solution.py:56
  19.2 8.3 %collective-permute-start.4 = (bf16[128,512]{1,0:T(8,128)(2,1)S(1)}, bf16[128,512]{1,0:T(8,128)(2,1)S(1)}, u32[]{:S(2)}, u32[]{:S(2)}) collective-permute-start(bf16[128,512]{1,0:T(8,128)(2,1)S(1)} %get-tuple-element.90), channel_id=1, source_target_pairs={{0,2},{1,3},{2,0},{3,1},{4,6},{5,7},{6,4},{7,5},{8,10},{9,11},{10,... | collective-permute-start | bytes 393224 | tf_op jit(solution)/shard_map/ppermute | solution.py:56
  21.0 8.1 %collective-permute-start.5 = (bf16[128,512]{1,0:T(8,128)(2,1)S(1)}, bf16[128,512]{1,0:T(8,128)(2,1)S(1)}, u32[]{:S(2)}, u32[]{:S(2)}) collective-permute-start(bf16[128,512]{1,0:T(8,128)(2,1)S(1)} %get-tuple-element.91), channel_id=1, source_target_pairs={{0,3},{1,2},{2,1},{3,0},{4,7},{5,6},{6,5},{7,4},{8,11},{9,10},{10,... | collective-permute-start | bytes 393224 | tf_op jit(solution)/shard_map/ppermute | solution.py:56
  21.2 8.4 %collective-permute-start.6 = (bf16[128,512]{1,0:T(8,128)(2,1)S(1)}, bf16[128,512]{1,0:T(8,128)(2,1)S(1)}, u32[]{:S(2)}, u32[]{:S(2)}) collective-permute-start(bf16[128,512]{1,0:T(8,128)(2,1)S(1)} %get-tuple-element.96), channel_id=1, source_target_pairs={{0,1},{1,0},{2,3},{3,2},{4,5},{5,4},{6,7},{7,6},{8,9},{9,8},{10,11... | collective-permute-start | bytes 393224 | tf_op jit(solution)/shard_map/ppermute | solution.py:56
  21.4 14.6 %collective-permute-start.8 = (bf16[128,512]{1,0:T(8,128)(2,1)S(1)}, bf16[128,512]{1,0:T(8,128)(2,1)S(1)}, u32[]{:S(2)}, u32[]{:S(2)}) collective-permute-start(bf16[128,512]{1,0:T(8,128)(2,1)S(1)} %get-tuple-element.99), channel_id=1, source_target_pairs={{0,1},{1,0},{2,3},{3,2},{4,5},{5,4},{6,7},{7,6},{8,9},{9,8},{10,11... | collective-permute-start | bytes 393224 | tf_op jit(solution)/shard_map/ppermute | solution.py:56
  22.0 11.7 %collective-permute-start.11 = (bf16[1280,128]{1,0:T(8,128)(2,1)S(1)}, bf16[1280,128]{1,0:T(8,128)(2,1)S(1)}, u32[]{:S(2)}, u32[]{:S(2)}) collective-permute-start(bf16[1280,128]{1,0:T(8,128)(2,1)S(1)} %get-tuple-element.103), channel_id=1, source_target_pairs={{0,8},{4,12},{8,0},{12,4},{16,24},{20,28},{24,16},{28,20},{1,9},{5... | collective-permute-start | bytes 983048 | tf_op jit(solution)/shard_map/ppermute | solution.py:56
  27.6 9.1 %collective-permute-start.9 = (bf16[128,512]{1,0:T(8,128)(2,1)S(1)}, bf16[128,512]{1,0:T(8,128)(2,1)S(1)}, u32[]{:S(2)}, u32[]{:S(2)}) collective-permute-start(bf16[128,512]{1,0:T(8,128)(2,1)S(1)} %get-tuple-element.100), channel_id=1, source_target_pairs={{0,2},{1,3},{2,0},{3,1},{4,6},{5,7},{6,4},{7,5},{8,10},{9,11},{10,... | collective-permute-start | bytes 393224 | tf_op jit(solution)/shard_map/ppermute | solution.py:56
  29.1 8.0 %collective-permute-start.10 = (bf16[128,512]{1,0:T(8,128)(2,1)S(1)}, bf16[128,512]{1,0:T(8,128)(2,1)S(1)}, u32[]{:S(2)}, u32[]{:S(2)}) collective-permute-start(bf16[128,512]{1,0:T(8,128)(2,1)S(1)} %get-tuple-element.101), channel_id=1, source_target_pairs={{0,3},{1,2},{2,1},{3,0},{4,7},{5,6},{6,5},{7,4},{8,11},{9,10},{10,... | collective-permute-start | bytes 393224 | tf_op jit(solution)/shard_map/ppermute | solution.py:56
  32.0 9.2 %collective-permute-start.7 = (bf16[512,256]{1,0:T(8,128)(2,1)S(1)}, bf16[512,256]{1,0:T(8,128)(2,1)S(1)}, u32[]{:S(2)}, u32[]{:S(2)}) collective-permute-start(bf16[512,256]{1,0:T(8,128)(2,1)S(1)} %get-tuple-element.97.refs_10_.refs_13_.refs_14_), channel_id=1, source_target_pairs={{0,8},{4,12},{8,0},{12,4},{16,24},{20,28},{24,16},{28,20},{1,9},{5... | collective-permute-start | bytes 786440 | tf_op jit(solution)/shard_map/ppermute | solution.py:56
  33.6 11.6 %collective-permute-start.12 = (bf16[1280,128]{1,0:T(8,128)(2,1)S(1)}, bf16[1280,128]{1,0:T(8,128)(2,1)S(1)}, u32[]{:S(2)}, u32[]{:S(2)}) collective-permute-start(bf16[1280,128]{1,0:T(8,128)(2,1)S(1)} %collective-permute-done.1.refs_6_.refs_7_.refs_8_.refs_9_), channel_id=1, source_target_pairs={{0,1},{1,0},{2,3},{3,2},{4,5},{5,4},{6,7},{7,6},{8,9},{9,8},{10,11... | collective-permute-start | bytes 983048 | tf_op jit(solution)/shard_map/ppermute | solution.py:56
  36.0 9.2 %collective-permute-start.13 = (bf16[1280,128]{1,0:T(8,128)(2,1)S(1)}, bf16[1280,128]{1,0:T(8,128)(2,1)S(1)}, u32[]{:S(2)}, u32[]{:S(2)}) collective-permute-start(bf16[1280,128]{1,0:T(8,128)(2,1)S(1)} %collective-permute-done.11.refs_8_.refs_9_.refs_10_.refs_11_), channel_id=1, source_target_pairs={{0,1},{1,0},{2,3},{3,2},{4,5},{5,4},{6,7},{7,6},{8,9},{9,8},{10,11... | collective-permute-start | bytes 983048 | tf_op jit(solution)/shard_map/ppermute | solution.py:56
  36.6 11.1 %collective-permute-start.14 = (bf16[512,256]{1,0:T(8,128)(2,1)S(1)}, bf16[512,256]{1,0:T(8,128)(2,1)S(1)}, u32[]{:S(2)}, u32[]{:S(2)}) collective-permute-start(bf16[512,256]{1,0:T(8,128)(2,1)S(1)} %get-tuple-element.116.refs_10_.refs_14_.refs_15_), channel_id=1, source_target_pairs={{0,8},{4,12},{8,0},{12,4},{16,24},{20,28},{24,16},{28,20},{1,9},{5... | collective-permute-start | bytes 786440 | tf_op jit(solution)/shard_map/ppermute | solution.py:56
  43.6 13.8 %collective-permute-start.16 = (bf16[512,256]{1,0:T(8,128)(2,1)S(1)}, bf16[512,256]{1,0:T(8,128)(2,1)S(1)}, u32[]{:S(2)}, u32[]{:S(2)}) collective-permute-start(bf16[512,256]{1,0:T(8,128)(2,1)S(1)} %get-tuple-element.122.refs_11_.refs_15_.refs_16_), channel_id=1, source_target_pairs={{0,8},{4,12},{8,0},{12,4},{16,24},{20,28},{24,16},{28,20},{1,9},{5... | collective-permute-start | bytes 786440 | tf_op jit(solution)/shard_map/ppermute | solution.py:56
  46.1 8.5 %collective-permute-start.15 = (bf16[640,256]{1,0:T(8,128)(2,1)S(1)}, bf16[640,256]{1,0:T(8,128)(2,1)S(1)}, u32[]{:S(2)}, u32[]{:S(2)}) collective-permute-start(bf16[640,256]{1,0:T(8,128)(2,1)S(1)} %get-tuple-element.120), channel_id=1, source_target_pairs={{0,4},{4,0},{8,12},{12,8},{16,20},{20,16},{24,28},{28,24},{1,5},{5... | collective-permute-start | bytes 983048 | tf_op jit(solution)/shard_map/ppermute | solution.py:56
  50.6 16.6 %collective-permute-start.20 = (bf16[512,512]{1,0:T(8,128)(2,1)S(1)}, bf16[512,512]{1,0:T(8,128)(2,1)S(1)}, u32[]{:S(2)}, u32[]{:S(2)}) collective-permute-start(bf16[512,512]{1,0:T(8,128)(2,1)S(1)} %attention.7.refs_0_.refs_16_.refs_12_.refs_17_.refs_13_), channel_id=1, source_target_pairs={{0,8},{4,12},{8,0},{12,4},{16,24},{20,28},{24,16},{28,20},{1,9},{5... | collective-permute-start | bytes 1572872 | tf_op jit(solution)/shard_map/ppermute | solution.py:56
  52.2 10.7 %collective-permute-start.18 = (bf16[640,256]{1,0:T(8,128)(2,1)S(1)}, bf16[640,256]{1,0:T(8,128)(2,1)S(1)}, u32[]{:S(2)}, u32[]{:S(2)}) collective-permute-start(bf16[640,256]{1,0:T(8,128)(2,1)S(1)} %get-tuple-element.127), channel_id=1, source_target_pairs={{0,4},{4,0},{8,12},{12,8},{16,20},{20,16},{24,28},{28,24},{1,5},{5... | collective-permute-start | bytes 983048 | tf_op jit(solution)/shard_map/ppermute | solution.py:56
  54.7 12.5 %collective-permute-start.19 = (bf16[320,256]{1,0:T(8,128)(2,1)S(1)}, bf16[320,256]{1,0:T(8,128)(2,1)S(1)}, u32[]{:S(2)}, u32[]{:S(2)}) collective-permute-start(bf16[320,256]{1,0:T(8,128)(2,1)S(1)} %get-tuple-element.129), channel_id=1, source_target_pairs={{0,16},{4,20},{8,24},{12,28},{16,0},{20,4},{24,8},{28,12},{1,17},{... | collective-permute-start | bytes 491528 | tf_op jit(solution)/shard_map/ppermute | solution.py:56
  61.2 11.3 %collective-permute-start.17 = (bf16[256,1280]{1,0:T(8,128)(2,1)S(1)}, bf16[256,1280]{1,0:T(8,128)(2,1)S(1)}, u32[]{:S(2)}, u32[]{:S(2)}) collective-permute-start(bf16[256,1280]{1,0:T(8,128)(2,1)S(1)} %get-tuple-element.124), channel_id=1, source_target_pairs={{0,1},{1,0},{2,3},{3,2},{4,5},{5,4},{6,7},{7,6},{8,9},{9,8},{10,11... | collective-permute-start | bytes 1966088 | tf_op jit(solution)/shard_map/ppermute | solution.py:56
  61.3 11.2 %collective-permute-start.24 = (bf16[640,256]{1,0:T(8,128)(2,1)S(1)}, bf16[640,256]{1,0:T(8,128)(2,1)S(1)}, u32[]{:S(2)}, u32[]{:S(2)}) collective-permute-start(bf16[640,256]{1,0:T(8,128)(2,1)S(1)} %get-tuple-element.135), channel_id=1, source_target_pairs={{0,4},{4,0},{8,12},{12,8},{16,20},{20,16},{24,28},{28,24},{1,5},{5... | collective-permute-start | bytes 983048 | tf_op jit(solution)/shard_map/ppermute | solution.py:56
  62.9 12.5 %collective-permute-start.27 = (bf16[320,256]{1,0:T(8,128)(2,1)S(1)}, bf16[320,256]{1,0:T(8,128)(2,1)S(1)}, u32[]{:S(2)}, u32[]{:S(2)}) collective-permute-start(bf16[320,256]{1,0:T(8,128)(2,1)S(1)} %get-tuple-element.141), channel_id=1, source_target_pairs={{0,16},{4,20},{8,24},{12,28},{16,0},{20,4},{24,8},{28,12},{1,17},{... | collective-permute-start | bytes 491528 | tf_op jit(solution)/shard_map/ppermute | solution.py:56
  70.7 8.3 %collective-permute-start.21 = (bf16[256,1280]{1,0:T(8,128)(2,1)S(1)}, bf16[256,1280]{1,0:T(8,128)(2,1)S(1)}, u32[]{:S(2)}, u32[]{:S(2)}) collective-permute-start(bf16[256,1280]{1,0:T(8,128)(2,1)S(1)} %get-tuple-element.131), channel_id=1, source_target_pairs={{0,1},{1,0},{2,3},{3,2},{4,5},{5,4},{6,7},{7,6},{8,9},{9,8},{10,11... | collective-permute-start | bytes 1966088 | tf_op jit(solution)/shard_map/ppermute | solution.py:56
  70.8 10.6 %collective-permute-start.25 = (bf16[640,256]{1,0:T(8,128)(2,1)S(1)}, bf16[640,256]{1,0:T(8,128)(2,1)S(1)}, u32[]{:S(2)}, u32[]{:S(2)}) collective-permute-start(bf16[640,256]{1,0:T(8,128)(2,1)S(1)} %get-tuple-element.138), channel_id=1, source_target_pairs={{0,4},{4,0},{8,12},{12,8},{16,20},{20,16},{24,28},{28,24},{1,5},{5... | collective-permute-start | bytes 983048 | tf_op jit(solution)/shard_map/ppermute | solution.py:56
  76.2 14.7 %collective-permute-start.28 = (bf16[640,256]{1,0:T(8,128)(2,1)S(1)}, bf16[640,256]{1,0:T(8,128)(2,1)S(1)}, u32[]{:S(2)}, u32[]{:S(2)}) collective-permute-start(bf16[640,256]{1,0:T(8,128)(2,1)S(1)} %get-tuple-element.143), channel_id=1, source_target_pairs={{0,4},{4,0},{8,12},{12,8},{16,20},{20,16},{24,28},{28,24},{1,5},{5... | collective-permute-start | bytes 983048 | tf_op jit(solution)/shard_map/ppermute | solution.py:56
  77.5 13.5 %collective-permute-start.26 = (bf16[320,256]{1,0:T(8,128)(2,1)S(1)}, bf16[320,256]{1,0:T(8,128)(2,1)S(1)}, u32[]{:S(2)}, u32[]{:S(2)}) collective-permute-start(bf16[320,256]{1,0:T(8,128)(2,1)S(1)} %get-tuple-element.140), channel_id=1, source_target_pairs={{0,16},{4,20},{8,24},{12,28},{16,0},{20,4},{24,8},{28,12},{1,17},{... | collective-permute-start | bytes 491528 | tf_op jit(solution)/shard_map/ppermute | solution.py:56
  77.5 14.0 %collective-permute-start.22 = (bf16[128,1280]{1,0:T(8,128)(2,1)S(1)}, bf16[128,1280]{1,0:T(8,128)(2,1)S(1)}, u32[]{:S(2)}, u32[]{:S(2)}) collective-permute-start(bf16[128,1280]{1,0:T(8,128)(2,1)S(1)} %get-tuple-element.133), channel_id=1, source_target_pairs={{0,2},{1,3},{2,0},{3,1},{4,6},{5,7},{6,4},{7,5},{8,10},{9,11},{10,... | collective-permute-start | bytes 983048 | tf_op jit(solution)/shard_map/ppermute | solution.py:56
  79.1 14.6 %collective-permute-start.23 = (bf16[128,1280]{1,0:T(8,128)(2,1)S(1)}, bf16[128,1280]{1,0:T(8,128)(2,1)S(1)}, u32[]{:S(2)}, u32[]{:S(2)}) collective-permute-start(bf16[128,1280]{1,0:T(8,128)(2,1)S(1)} %get-tuple-element.134), channel_id=1, source_target_pairs={{0,2},{1,3},{2,0},{3,1},{4,6},{5,7},{6,4},{7,5},{8,10},{9,11},{10,... | collective-permute-start | bytes 983048 | tf_op jit(solution)/shard_map/ppermute | solution.py:56
  81.5 16.5 %collective-permute-start.29 = (bf16[320,256]{1,0:T(8,128)(2,1)S(1)}, bf16[320,256]{1,0:T(8,128)(2,1)S(1)}, u32[]{:S(2)}, u32[]{:S(2)}) collective-permute-start(bf16[320,256]{1,0:T(8,128)(2,1)S(1)} %get-tuple-element.145), channel_id=1, source_target_pairs={{0,16},{4,20},{8,24},{12,28},{16,0},{20,4},{24,8},{28,12},{1,17},{... | collective-permute-start | bytes 491528 | tf_op jit(solution)/shard_map/ppermute | solution.py:56
  91.0 10.4 %collective-permute-start.30 = (bf16[320,256]{1,0:T(8,128)(2,1)S(1)}, bf16[320,256]{1,0:T(8,128)(2,1)S(1)}, u32[]{:S(2)}, u32[]{:S(2)}) collective-permute-start(bf16[320,256]{1,0:T(8,128)(2,1)S(1)} %get-tuple-element.146), channel_id=1, source_target_pairs={{0,16},{4,20},{8,24},{12,28},{16,0},{20,4},{24,8},{28,12},{1,17},{... | collective-permute-start | bytes 491528 | tf_op jit(solution)/shard_map/ppermute | solution.py:56
  101.4 1.1 %copy-start = (bf16[128,2560]{1,0:T(8,128)(2,1)S(1)}, bf16[128,2560]{1,0:T(8,128)(2,1)}, u32[]{:S(2)}) copy-start(bf16[128,2560]{1,0:T(8,128)(2,1)} %input_sum.1.refs_0_) | copy-start | bytes 1966084

commit v3 on v2

--- a/solution.py
+++ b/solution.py
@@ -374,45 +374,46 @@
         total = keep + received.astype(f32)
         return total[:half].astype(bf16), total[half:]
     size = (half, columns)
-    return call(halve_kernel, (), (keep, received), [(size, bf16), (size, f32)], "halve", 1e6, deps)
+    return call(halve_kernel, (), (keep, received), [(size, bf16), (size, f32)], "halve", 2e9, deps)
 
 
 def input_sum_kernel(*refs):
-    *inputs, out = refs
+    *inputs, out, token = refs
     count = len(inputs) // 2
     columns = inputs[0].shape[1]
     for n in range(count):
         total = inputs[n][...] + inputs[count + n][...].astype(f32)
         out[:, n * columns : (n + 1) * columns] = total.astype(bf16)
-
-
-def final_kernel(first, *refs):
-    *inputs, query_out, key_out, value_out = refs[first:]
-    width = key_out.shape[1]
+    token[...] = jnp.zeros_like(token)
+
+
+def query_sum_kernel(first, *refs):
+    *inputs, out, token = refs[first:]
     count = len(inputs) // 2
+    columns = inputs[0].shape[1]
     for n in range(count):
         total = inputs[n][...] + inputs[count + n][...].astype(f32)
-        columns = total.shape[1]
-        if n < count - 1:
-            query_out[:, n * columns : (n + 1) * columns] = total
-        else:
-            key_out[...] = total[:, :width]
-            value_out[...] = total[:, width:]
-
-
-def final_sums(ends, width, deps):
-    share, columns = ends[0][0].shape
-    kept = [end[0] for end in ends]
-    received = [end[1] for end in ends]
-    widths = ((len(ends) - 1) * columns, width, width)
+        out[:, n * columns : (n + 1) * columns] = total
+    token[...] = jnp.zeros_like(token)
+
+
+def pair_sum_kernel(first, *refs):
+    kept, received, key_out, value_out = refs[first:]
+    width = key_out.shape[1]
+    total = kept[...] + received[...].astype(f32)
+    key_out[...] = total[:, :width]
+    value_out[...] = total[:, width:]
+
+
+def last_sum(kernel, deps, inputs, outputs):
     return pl.pallas_call(
-        functools.partial(final_kernel, len(deps)),
-        in_specs=[ANY] * len(deps) + [VMEM] * (2 * len(ends)),
-        out_shape=[jax.ShapeDtypeStruct((share, w), f32) for w in widths],
+        functools.partial(kernel, len(deps)) if deps else kernel,
+        in_specs=[ANY] * len(deps) + [VMEM] * len(inputs),
+        out_shape=[jax.ShapeDtypeStruct(shape, dtype) for shape, dtype in outputs],
         compiler_params=pltpu.CompilerParams(vmem_limit_bytes=14 * MIB),
         cost_estimate=pl.CostEstimate(flops=1024, bytes_accessed=1024, transcendentals=0),
-        name="final_sums",
-    )(*deps, *kept, *received)
+        name="last_sum",
+    )(*deps, *inputs)
 
 
 def local(dp, sp, normed, wq, wk, wv, q_gain, k_gain, ctx_grad, lengths):
@@ -484,8 +485,8 @@
     def input_part(n):
         return ((n * features // 2, features // 2), parts, (wq, wk, wv))
 
-    def halved(sent, kept):
-        sent, kept = halve(kept, over_sp(sent, bit=1))
+    def halved(sent, kept, deps=()):
+        sent, kept = halve(kept, over_sp(sent, bit=1), deps)
         return kept, over_sp(sent, bit=2)
 
     def last_steps(keep, came, deps=()):
@@ -504,25 +505,27 @@
     heads(3, (keep, received[1]), LONG)
     keep, = product(1, (parts[3],), SHORT)
     ends = [last_steps(*firsts[0])]
-    keep, sent, kept = product(2, (keep, ends[0][0]), LONG, input_part(0))
-    inputs = [halved(sent, kept)]
+    keep, *first_half = product(2, (keep, ends[0][0]), LONG, input_part(0))
     ends.append(last_steps(*firsts[1]))
-    keep, sent, kept = product(3, (keep, ends[1][0], ends[0][1]), LONG, input_part(1))
+    keep, *second_half = product(3, (keep, ends[1][0], ends[0][1]), LONG, input_part(1))
     ends.append(last_steps(*firsts[2]))
-    product(4, (keep, ends[2][0], ends[1][1], inputs[0][0]), LONG)
-    inputs.append(halved(sent, kept))
-    ends.append(last_steps(*firsts[3]))
+    tied = product(4, (keep, ends[2][0], ), LONG)
+    inputs = [halved(*half, (tied[0],)) for half in (first_half, second_half)]
+    ends.append(last_steps(*firsts[3], (ends[1][1],)))
     ends.append(last_steps(*firsts[4], (ends[2][1],)))
     pieces = [i[0] for i in inputs] + [i[1] for i in inputs]
-    input_gradient = pl.pallas_call(
-        input_sum_kernel,
-        in_specs=[VMEM] * len(pieces),
-        out_shape=jax.ShapeDtypeStruct((rows, features), bf16),
-        compiler_params=pltpu.CompilerParams(vmem_limit_bytes=14 * MIB),
-        cost_estimate=pl.CostEstimate(flops=1024, bytes_accessed=1024, transcendentals=0),
-        name="input_sum",
-    )(*pieces)
-    return (input_gradient, *final_sums(ends, width, (input_gradient,)))
+    token = ((8, 128), f32)
+    input_gradient, order_mark = last_sum(
+        input_sum_kernel, (), pieces, [((rows, features), bf16), token]
+    )
+    pieces = [end[0] for end in ends[:-1]] + [end[1] for end in ends[:-1]]
+    grad_query, order_mark = last_sum(
+        query_sum_kernel, (order_mark,), pieces, [((order.share, columns), f32), token]
+    )
+    grad_key, grad_value = last_sum(
+        pair_sum_kernel, (order_mark,), ends[-1], [((order.share, width), f32)] * 2
+    )
+    return input_gradient, grad_query, grad_key, grad_value
 
 
 def solution(mesh):

time: 104 us -> 104 us (level)
  starting transfers between devices: 33.1 us -> 41.1 us
  waiting for transfers between devices: 32.3 us -> 24.3 us
  local copies, waits for them, and re-layouts: 4.91 us -> 3.82 us
    ppermute x31, starting transfers between devices: 33.1 us -> 41.1 us  [exchange(): return lax.ppermute(value, axis, [(d, d ^ bit) for d in range(size)])]
    ppermute x31, waiting for transfers between devices: 32.3 us -> 24.3 us  [exchange(): return lax.ppermute(value, axis, [(d, d ^ bit) for d in range(size)])]
    unnamed x20 -> x18, local copies, waits for them, and re-layouts: 4.79 us -> 3.7 us
    pallas_call x2 -> x3, Pallas kernels: 2.26 us -> 2.89 us  [last_sum(): pl.pallas_call(functools.partial(kernel, len(deps)) if deps else kernel,...]
  transfers between devices with their start and end apart: 31 -> 31, of which waited for: 11 -> 9; matrix products, arithmetic and copies ran while one was open for 1% -> 1% of each run, Pallas kernels for 28% -> 30%
where the time goes in v3:
time: 104 us; the launch traced here: 103 us
  starting transfers between devices  41.1 us (40%)
  Pallas kernels  31.4 us (30%)
  waiting for transfers between devices  24.3 us (23%)
  local copies, waits for them, and re-layouts  3.82 us (4%)
  between operations  1.57 us (2%)
  other arithmetic  1.21 us (1%)
    ppermute x31, starting transfers between devices, exchange(): return lax.ppermute(value, axis, [(d, d ^ bit) for d in range(size)])  41.1 us
    pallas_call x22, Pallas kernels, call(): pl.pallas_call(body, in_specs=[ANY] * count + [SMEM] * len(scalars) + [VM...  28.5 us
    ppermute x31, waiting for transfers between devices, exchange(): return lax.ppermute(value, axis, [(d, d ^ bit) for d in range(size)])  24.3 us
    unnamed x18, local copies, waits for them, and re-layouts  3.7 us
    pallas_call x3, Pallas kernels, last_sum(): pl.pallas_call(functools.partial(kernel, len(deps)) if deps else kernel,...  2.89 us
  transfers between devices with their start and end apart: 31, of which 9 were waited for; matrix products, arithmetic and copies ran while one was open for 1% of the time, Pallas kernels for 30%

profile of v3, /device:TPU:0, one launch (start us, length us, event | category | flops | bytes accessed | tf_op | source)
XLA Modules:
  0.0 103.5 jit_solution(15990812812818958659)
XLA Ops:
  0.6 3.0 %collective-permute-start = (bf16[128,2560]{1,0:T(8,128)(2,1)}, bf16[128,2560]{1,0:T(8,128)(2,1)S(1)}, u32[]{:S(2)}, u32[]{:S(2)}) collective-permute-start(bf16[128,2560]{1,0:T(8,128)(2,1)} %refs_1_.4), channel_id=1, source_target_pairs={{0,2},{1,3},{2,0},{3,1},{4,6},{5,7},{6,4},{7,5},{8,10},{9,11},{10,... | collective-permute-start | bytes 1966088 | tf_op jit(solution)/shard_map/ppermute | solution.py:56
  3.6 1.1 %copy-done = bf16[128,2560]{1,0:T(8,128)(2,1)S(1)} copy-done((bf16[128,2560]{1,0:T(8,128)(2,1)S(1)}, bf16[128,2560]{1,0:T(8,128)(2,1)}, u32[]{:S(2)}) %copy-start) | copy-done | bytes 655384
  5.0 1.6 %collective-permute-start.1 = (bf16[1280,128]{1,0:T(8,128)(2,1)S(1)}, bf16[1280,128]{1,0:T(8,128)(2,1)S(1)}, u32[]{:S(2)}, u32[]{:S(2)}) collective-permute-start(bf16[1280,128]{1,0:T(8,128)(2,1)S(1)} %get-tuple-element.80), channel_id=1, source_target_pairs={{0,8},{4,12},{8,0},{12,4},{16,24},{20,28},{24,16},{28,20},{1,9},{5... | collective-permute-start | bytes 983048 | tf_op jit(solution)/shard_map/ppermute | solution.py:56
  6.7 1.0 fusion
  8.2 2.5 %copy-done.3 = bf16[2560,1024]{1,0:T(8,128)(2,1)S(1)} copy-done((bf16[2560,1024]{1,0:T(8,128)(2,1)S(1)}, bf16[2560,1024]{1,0:T(8,128)(2,1)}, u32[]{:S(2)}) %copy-start.3) | copy-done | bytes 5242904
  10.6 3.6 %projections.2 = (bf16[512,1024]{1,0:T(8,128)(2,1)S(1)}, f32[512,1024]{1,0:T(8,128)S(1)}, bf16[512,128]{1,0:T(8,128)(2,1)S(1)}, f32[512,128]{1,0:T(8,128)S(1)}, bf16[512,128]{1,0:T(8,128)(2,1)S(1)}) custom-call(s32[1]{0:T(128)} %bitcast.refs_0_.refs_1_.refs_2_.refs_3_, bf16[128,2560]{1,0:T(8,128)(2,1)S(1)} %copy-done.1, ...), custom_call_target="tpu_custom_call" | custom-call | flops 23000000512 | bytes 1024 | tf_op jit(solution)/shard_map/projections/pallas_call | solution.py:29
  14.4 0.8 collective-permute-done.1.refs_6_.refs_7_.refs_8_
  15.1 3.4 %collective-permute-done.refs_1_ = bf16[128,2560]{1,0:T(8,128)(2,1)S(1)} collective-permute-done((bf16[128,2560]{1,0:T(8,128)(2,1)}, bf16[128,2560]{1,0:T(8,128)(2,1)S(1)}, u32[]{:S(2)}, u32[]{:S(2)}) %collective-permute-start) | collective-permute-done | bytes 655392 | tf_op jit(solution)/shard_map/ppermute | solution.py:56
  19.2 1.8 %collective-permute-start.4 = (bf16[128,512]{1,0:T(8,128)(2,1)S(1)}, bf16[128,512]{1,0:T(8,128)(2,1)S(1)}, u32[]{:S(2)}, u32[]{:S(2)}) collective-permute-start(bf16[128,512]{1,0:T(8,128)(2,1)S(1)} %get-tuple-element.93), channel_id=1, source_target_pairs={{0,2},{1,3},{2,0},{3,1},{4,6},{5,7},{6,4},{7,5},{8,10},{9,11},{10,... | collective-permute-start | bytes 393224 | tf_op jit(solution)/shard_map/ppermute | solution.py:56
  22.0 1.8 %collective-permute-start.11 = (bf16[1280,128]{1,0:T(8,128)(2,1)S(1)}, bf16[1280,128]{1,0:T(8,128)(2,1)S(1)}, u32[]{:S(2)}, u32[]{:S(2)}) collective-permute-start(bf16[1280,128]{1,0:T(8,128)(2,1)S(1)} %get-tuple-element.106), channel_id=1, source_target_pairs={{0,8},{4,12},{8,0},{12,4},{16,24},{20,28},{24,16},{28,20},{1,9},{5... | collective-permute-start | bytes 983048 | tf_op jit(solution)/shard_map/ppermute | solution.py:56
  23.8 3.7 %projections.3 = (bf16[512,1024]{1,0:T(8,128)(2,1)S(1)}, f32[512,1024]{1,0:T(8,128)S(1)}, bf16[512,128]{1,0:T(8,128)(2,1)S(1)}, f32[512,128]{1,0:T(8,128)S(1)}, bf16[512,128]{1,0:T(8,128)(2,1)S(1)}) custom-call(s32[1]{0:T(128)} %bitcast.refs_0_.refs_1_.refs_2_.refs_3_, ...), custom_call_target="tpu_custom_call", output_to_operand_aliasing={{0}: (10, {}), {1}: (11, {}), {2}: (12, {}), {3}: (13, {}),... | custom-call | flops 23000000512 | bytes 1024 | tf_op jit(solution)/shard_map/projections/pallas_call | solution.py:29
  27.6 1.6 %collective-permute-start.9 = (bf16[128,512]{1,0:T(8,128)(2,1)S(1)}, bf16[128,512]{1,0:T(8,128)(2,1)S(1)}, u32[]{:S(2)}, u32[]{:S(2)}) collective-permute-start(bf16[128,512]{1,0:T(8,128)(2,1)S(1)} %get-tuple-element.103), channel_id=1, source_target_pairs={{0,2},{1,3},{2,0},{3,1},{4,6},{5,7},{6,4},{7,5},{8,10},{9,11},{10,... | collective-permute-start | bytes 393224 | tf_op jit(solution)/shard_map/ppermute | solution.py:56
  29.1 0.4 collective-permute-start.10
  29.6 2.4 %attention.4 = (bf16[512,256]{1,0:T(8,128)(2,1)S(1)}, f32[512,128]{1,0:T(8,128)S(1)}, f32[512,128]{1,0:T(8,128)S(1)}) custom-call(bf16[1280,128]{1,0:T(8,128)(2,1)S(1)} %transposed.6.refs_0_.refs_5_.refs_6_.refs_7_, s32[1]{0:T(128)} %bitcast.refs_0_.refs_1_.refs_2_.refs_3_, s32[1]{0:T(128)S(6)} %copy.22.refs_2_.refs_1_.refs_3_, ...), custom_call_target="tpu_custom_call" | custom-call | flops 1000000 | bytes 1024 | tf_op jit(solution)/shard_map/attention/pallas_call | solution.py:29
  32.0 1.6 %collective-permute-start.7 = (bf16[512,256]{1,0:T(8,128)(2,1)S(1)}, bf16[512,256]{1,0:T(8,128)(2,1)S(1)}, u32[]{:S(2)}, u32[]{:S(2)}) collective-permute-start(bf16[512,256]{1,0:T(8,128)(2,1)S(1)} %get-tuple-element.100.refs_10_.refs_13_.refs_14_), channel_id=1, source_target_pairs={{0,8},{4,12},{8,0},{12,4},{16,24},{20,28},{24,16},{28,20},{1,9},{5... | collective-permute-start | bytes 786440 | tf_op jit(solution)/shard_map/ppermute | solution.py:56
  33.6 2.4 %attention.5 = (bf16[512,256]{1,0:T(8,128)(2,1)S(1)}, f32[512,128]{1,0:T(8,128)S(1)}, f32[512,128]{1,0:T(8,128)S(1)}) custom-call(s32[1]{0:T(128)} %bitcast.refs_0_.refs_1_.refs_2_.refs_3_, s32[1]{0:T(128)S(6)} %copy.22.refs_2_.refs_1_.refs_3_, bf16[512,1024]{1,0:T(8,128)(2,1)S(1)} %get-tuple-element.95.refs_3_.refs_2_.refs_4_, ...), custom_call_target="tpu_custom_call" | custom-call | flops 23000000512 | bytes 1024 | tf_op jit(solution)/shard_map/attention/pallas_call | solution.py:29
  36.0 0.6 collective-permute-start.13
  36.6 0.4 collective-permute-start.14
  37.1 4.1 %collective-permute-done.7.refs_0_.refs_11_ = bf16[512,256]{1,0:T(8,128)(2,1)S(1)} collective-permute-done((bf16[512,256]{1,0:T(8,128)(2,1)S(1)}, bf16[512,256]{1,0:T(8,128)(2,1)S(1)}, u32[]{:S(2)}, u32[]{:S(2)}) %collective-permute-start.7) | collective-permute-done | bytes 262176 | tf_op jit(solution)/shard_map/ppermute | solution.py:56
  41.2 2.4 %attention.6 = (bf16[512,256]{1,0:T(8,128)(2,1)S(1)}, f32[512,128]{1,0:T(8,128)S(1)}, f32[512,128]{1,0:T(8,128)S(1)}) custom-call(bf16[512,256]{1,0:T(8,128)(2,1)S(1)} %collective-permute-done.7.refs_0_.refs_11_, s32[1]{0:T(128)} %bitcast.refs_0_.refs_1_.refs_2_.refs_3_, s32[1]{0:T(128)S(6)} %copy.22.refs_2_.refs_1_.refs_3_, ...), custom_call_target="tpu_custom_call" | custom-call | flops 23000000512 | bytes 1024 | tf_op jit(solution)/shard_map/attention/pallas_call | solution.py:29
  43.6 1.7 %collective-permute-start.16 = (bf16[512,256]{1,0:T(8,128)(2,1)S(1)}, bf16[512,256]{1,0:T(8,128)(2,1)S(1)}, u32[]{:S(2)}, u32[]{:S(2)}) collective-permute-start(bf16[512,256]{1,0:T(8,128)(2,1)S(1)} %get-tuple-element.125.refs_11_.refs_15_.refs_16_), channel_id=1, source_target_pairs={{0,8},{4,12},{8,0},{12,4},{16,24},{20,28},{24,16},{28,20},{1,9},{5... | collective-permute-start | bytes 786440 | tf_op jit(solution)/shard_map/ppermute | solution.py:56
  45.3 0.8 weight_products.3
  46.1 1.6 %collective-permute-start.15 = (bf16[640,256]{1,0:T(8,128)(2,1)S(1)}, bf16[640,256]{1,0:T(8,128)(2,1)S(1)}, u32[]{:S(2)}, u32[]{:S(2)}) collective-permute-start(bf16[640,256]{1,0:T(8,128)(2,1)S(1)} %get-tuple-element.123), channel_id=1, source_target_pairs={{0,4},{4,0},{8,12},{12,8},{16,20},{20,16},{24,28},{28,24},{1,5},{5... | collective-permute-start | bytes 983048 | tf_op jit(solution)/shard_map/ppermute | solution.py:56
  47.7 2.9 %attention.7.refs_0_.refs_16_.refs_12_.refs_17_.refs_11_ = bf16[512,512]{1,0:T(8,128)(2,1)S(1)} custom-call(f32[640,256]{1,0:T(8,128)S(1)} %get-tuple-element.118.refs_0_, bf16[512,256]{1,0:T(8,128)(2,1)S(1)} %collective-permute-done.14.refs_1_.refs_11_, s32[1]{0:T(128)} %bitcast.refs_0_.refs_1_.refs_2_.refs_3_, s32[1]{0:T(128)S(6)} %copy.22.refs_2_.refs_1_.refs_3_, ...), custom_call_target="tpu_custom_call" | custom-call | flops 23000000512 | bytes 1024 | tf_op jit(solution)/shard_map/attention/pallas_call | solution.py:29
  50.6 0.8 collective-permute-start.19
  51.3 0.8 weight_products.4
  52.2 1.6 %collective-permute-start.17 = (bf16[640,256]{1,0:T(8,128)(2,1)S(1)}, bf16[640,256]{1,0:T(8,128)(2,1)S(1)}, u32[]{:S(2)}, u32[]{:S(2)}) collective-permute-start(bf16[640,256]{1,0:T(8,128)(2,1)S(1)} %get-tuple-element.127), channel_id=1, source_target_pairs={{0,4},{4,0},{8,12},{12,8},{16,20},{20,16},{24,28},{28,24},{1,5},{5... | collective-permute-start | bytes 983048 | tf_op jit(solution)/shard_map/ppermute | solution.py:56
  53.8 0.8 collective-permute-done.15.refs_1_
  54.7 2.6 %collective-permute-start.18 = (bf16[320,256]{1,0:T(8,128)(2,1)S(1)}, bf16[320,256]{1,0:T(8,128)(2,1)S(1)}, u32[]{:S(2)}, u32[]{:S(2)}) collective-permute-start(bf16[320,256]{1,0:T(8,128)(2,1)S(1)} %get-tuple-element.129), channel_id=1, source_target_pairs={{0,16},{4,20},{8,24},{12,28},{16,0},{20,4},{24,8},{28,12},{1,17},{... | collective-permute-start | bytes 491528 | tf_op jit(solution)/shard_map/ppermute | solution.py:56
  57.3 3.8 %both_products.2 = (bf16[640,256]{1,0:T(8,128)(2,1)S(1)}, f32[640,256]{1,0:T(8,128)S(1)}, bf16[256,1280]{1,0:T(8,128)(2,1)S(1)}, f32[256,1280]{1,0:T(8,128)S(1)}) custom-call(f32[640,256]{1,0:T(8,128)S(1)} %get-tuple-element.122.refs_0_, f32[320,256]{1,0:T(8,128)S(1)} %get-tuple-element.124.refs_1_, s32[1]{0:T(128)} %bitcast.refs_0_.refs_1_.refs_2_.refs_3_, ...), custom_call_target="tpu_custom_call" | custom-call | flops 23000000512 | bytes 1024 | tf_op jit(solution)/shard_map/both_products/pallas_call | solution.py:29
  61.1 1.6 %collective-permute-start.20 = (bf16[640,256]{1,0:T(8,128)(2,1)S(1)}, bf16[640,256]{1,0:T(8,128)(2,1)S(1)}, u32[]{:S(2)}, u32[]{:S(2)}) collective-permute-start(bf16[640,256]{1,0:T(8,128)(2,1)S(1)} %get-tuple-element.131), channel_id=1, source_target_pairs={{0,4},{4,0},{8,12},{12,8},{16,20},{20,16},{24,28},{28,24},{1,5},{5... | collective-permute-start | bytes 983048 | tf_op jit(solution)/shard_map/ppermute | solution.py:56
  62.8 2.8 %collective-permute-start.25 = (bf16[320,256]{1,0:T(8,128)(2,1)S(1)}, bf16[320,256]{1,0:T(8,128)(2,1)S(1)}, u32[]{:S(2)}, u32[]{:S(2)}) collective-permute-start(bf16[320,256]{1,0:T(8,128)(2,1)S(1)} %get-tuple-element.144), channel_id=1, source_target_pairs={{0,16},{4,20},{8,24},{12,28},{16,0},{20,4},{24,8},{28,12},{1,17},{... | collective-permute-start | bytes 491528 | tf_op jit(solution)/shard_map/ppermute | solution.py:56
  65.6 1.2 %collective-permute-done.18.refs_2_.refs_5_ = bf16[320,256]{1,0:T(8,128)(2,1)S(1)} collective-permute-done((bf16[320,256]{1,0:T(8,128)(2,1)S(1)}, bf16[320,256]{1,0:T(8,128)(2,1)S(1)}, u32[]{:S(2)}, u32[]{:S(2)}) %collective-permute-start.18) | collective-permute-done | bytes 163872 | tf_op jit(solution)/shard_map/ppermute | solution.py:56
  66.9 3.6 %both_products.3 = (bf16[640,256]{1,0:T(8,128)(2,1)S(1)}, f32[640,256]{1,0:T(8,128)S(1)}, bf16[256,1280]{1,0:T(8,128)(2,1)S(1)}, f32[256,1280]{1,0:T(8,128)S(1)}) custom-call(f32[640,256]{1,0:T(8,128)S(1)} %get-tuple-element.126.refs_0_, f32[320,256]{1,0:T(8,128)S(1)} %get-tuple-element.128.refs_1_.refs_2_, ...), custom_call_target="tpu_custom_call" | custom-call | flops 23000000512 | bytes 1024 | tf_op jit(solution)/shard_map/both_products/pallas_call | solution.py:29
  70.5 1.9 %collective-permute-start.26 = (bf16[640,256]{1,0:T(8,128)(2,1)S(1)}, bf16[640,256]{1,0:T(8,128)(2,1)S(1)}, u32[]{:S(2)}, u32[]{:S(2)}) collective-permute-start(bf16[640,256]{1,0:T(8,128)(2,1)S(1)} %get-tuple-element.145), channel_id=1, source_target_pairs={{0,4},{4,0},{8,12},{12,8},{16,20},{20,16},{24,28},{28,24},{1,5},{5... | collective-permute-start | bytes 983048 | tf_op jit(solution)/shard_map/ppermute | solution.py:56
  72.5 3.5 %collective-permute-start.27 = (bf16[320,256]{1,0:T(8,128)(2,1)S(1)}, bf16[320,256]{1,0:T(8,128)(2,1)S(1)}, u32[]{:S(2)}, u32[]{:S(2)}) collective-permute-start(bf16[320,256]{1,0:T(8,128)(2,1)S(1)} %get-tuple-element.147), channel_id=1, source_target_pairs={{0,16},{4,20},{8,24},{12,28},{16,0},{20,4},{24,8},{28,12},{1,17},{... | collective-permute-start | bytes 491528 | tf_op jit(solution)/shard_map/ppermute | solution.py:56
  76.0 0.8 weight_products.5
  77.1 4.0 %collective-permute-done.26.refs_2_ = bf16[640,256]{1,0:T(8,128)(2,1)S(1)} collective-permute-done((bf16[640,256]{1,0:T(8,128)(2,1)S(1)}, bf16[640,256]{1,0:T(8,128)(2,1)S(1)}, u32[]{:S(2)}, u32[]{:S(2)}) %collective-permute-start.26) | collective-permute-done | bytes 327712 | tf_op jit(solution)/shard_map/ppermute | solution.py:56
  81.2 3.5 %collective-permute-start.28 = (bf16[320,256]{1,0:T(8,128)(2,1)S(1)}, bf16[320,256]{1,0:T(8,128)(2,1)S(1)}, u32[]{:S(2)}, u32[]{:S(2)}) collective-permute-start(bf16[320,256]{1,0:T(8,128)(2,1)S(1)} %get-tuple-element.148), channel_id=1, source_target_pairs={{0,16},{4,20},{8,24},{12,28},{16,0},{20,4},{24,8},{28,12},{1,17},{... | collective-permute-start | bytes 491528 | tf_op jit(solution)/shard_map/ppermute | solution.py:56
  84.8 0.6 collective-permute-start.23
  85.6 1.6 %collective-permute-start.24 = (bf16[128,1280]{1,0:T(8,128)(2,1)S(1)}, bf16[128,1280]{1,0:T(8,128)(2,1)S(1)}, u32[]{:S(2)}, u32[]{:S(2)}) collective-permute-start(bf16[128,1280]{1,0:T(8,128)(2,1)S(1)} %get-tuple-element.141), channel_id=1, source_target_pairs={{0,2},{1,3},{2,0},{3,1},{4,6},{5,7},{6,4},{7,5},{8,10},{9,11},{10,... | collective-permute-start | bytes 983048 | tf_op jit(solution)/shard_map/ppermute | solution.py:56
  87.1 0.6 collective-permute-done.29.refs_2_
  87.8 3.5 %collective-permute-start.30 = (bf16[320,256]{1,0:T(8,128)(2,1)S(1)}, bf16[320,256]{1,0:T(8,128)(2,1)S(1)}, u32[]{:S(2)}, u32[]{:S(2)}) collective-permute-start(bf16[320,256]{1,0:T(8,128)(2,1)S(1)} %get-tuple-element.153), channel_id=1, source_target_pairs={{0,16},{4,20},{8,24},{12,28},{16,0},{20,4},{24,8},{28,12},{1,17},{... | collective-permute-start | bytes 491528 | tf_op jit(solution)/shard_map/ppermute | solution.py:56
  91.3 4.2 %collective-permute-done.23.refs_2_ = bf16[128,1280]{1,0:T(8,128)(2,1)S(1)} collective-permute-done((bf16[128,1280]{1,0:T(8,128)(2,1)S(1)}, bf16[128,1280]{1,0:T(8,128)(2,1)S(1)}, u32[]{:S(2)}, u32[]{:S(2)}) %collective-permute-start.23) | collective-permute-done | bytes 327712 | tf_op jit(solution)/shard_map/ppermute | solution.py:56
  95.5 5.0 %collective-permute-done.24.refs_3_ = bf16[128,1280]{1,0:T(8,128)(2,1)S(1)} collective-permute-done((bf16[128,1280]{1,0:T(8,128)(2,1)S(1)}, bf16[128,1280]{1,0:T(8,128)(2,1)S(1)}, u32[]{:S(2)}, u32[]{:S(2)}) %collective-permute-start.24) | collective-permute-done | bytes 327712 | tf_op jit(solution)/shard_map/ppermute | solution.py:56
  100.6 1.0 last_sum.3
  101.6 1.2 %last_sum.4 = (f32[320,1024]{1,0:T(8,128)}, f32[8,128]{1,0:T(8,128)S(1)}) custom-call(f32[8,128]{1,0:T(8,128)S(1)} %get-tuple-element.143.refs_0_, f32[320,256]{1,0:T(8,128)S(1)} %get-tuple-element.124.refs_1_, f32[320,256]{1,0:T(8,128)S(1)} %get-tuple-element.128.refs_1_.refs_2_, f32[320,256]{1,0:T(8,128)S(1)} %get-tuple-element.132.refs_1_.refs_3_, ...), custom_call_target="tpu_custom_call" | custom-call | flops 1024 | bytes 1024 | tf_op jit(solution)/shard_map/last_sum/pallas_call | solution.py:409
  102.7 0.8 last_sum.5
  (62 shorter events, 2.8 us)
Async XLA Ops:
  0.6 17.9 %collective-permute-start = (bf16[128,2560]{1,0:T(8,128)(2,1)}, bf16[128,2560]{1,0:T(8,128)(2,1)S(1)}, u32[]{:S(2)}, u32[]{:S(2)}) collective-permute-start(bf16[128,2560]{1,0:T(8,128)(2,1)} %refs_1_.4), channel_id=1, source_target_pairs={{0,2},{1,3},{2,0},{3,1},{4,6},{5,7},{6,4},{7,5},{8,10},{9,11},{10,... | collective-permute-start | bytes 1966088 | tf_op jit(solution)/shard_map/ppermute | solution.py:56
  3.6 4.4 %collective-permute-start.2 = (bf16[128,2560]{1,0:T(8,128)(2,1)}, bf16[128,2560]{1,0:T(8,128)(2,1)S(1)}, u32[]{:S(2)}, u32[]{:S(2)}) collective-permute-start(bf16[128,2560]{1,0:T(8,128)(2,1)} %refs_1_.4), channel_id=1, source_target_pairs={{0,1},{1,0},{2,3},{3,2},{4,5},{5,4},{6,7},{7,6},{8,9},{9,8},{10,11... | collective-permute-start | bytes 1966088 | tf_op jit(solution)/shard_map/ppermute | solution.py:56
  3.6 1.1 %copy-start = (bf16[128,2560]{1,0:T(8,128)(2,1)S(1)}, bf16[128,2560]{1,0:T(8,128)(2,1)}, u32[]{:S(2)}) copy-start(bf16[128,2560]{1,0:T(8,128)(2,1)} %refs_1_.4) | copy-start | bytes 1966084
  4.8 3.2 %copy-start.8 = (bf16[128,4096]{1,0:T(8,128)(2,1)S(1)}, bf16[128,4096]{1,0:T(8,128)(2,1)}, u32[]{:S(2)}) copy-start(bf16[128,4096]{1,0:T(8,128)(2,1)} %param.14) | copy-start | bytes 3145732
  5.0 10.2 %collective-permute-start.1 = (bf16[1280,128]{1,0:T(8,128)(2,1)S(1)}, bf16[1280,128]{1,0:T(8,128)(2,1)S(1)}, u32[]{:S(2)}, u32[]{:S(2)}) collective-permute-start(bf16[1280,128]{1,0:T(8,128)(2,1)S(1)} %get-tuple-element.80), channel_id=1, source_target_pairs={{0,8},{4,12},{8,0},{12,4},{16,24},{20,28},{24,16},{28,20},{1,9},{5... | collective-permute-start | bytes 983048 | tf_op jit(solution)/shard_map/ppermute | solution.py:56
  6.6 1.4 %copy-start.1 = (bf16[128,2560]{1,0:T(8,128)(2,1)S(1)}, bf16[128,2560]{1,0:T(8,128)(2,1)}, u32[]{:S(2)}) copy-start(bf16[128,2560]{1,0:T(8,128)(2,1)} %refs_1_.4) | copy-start | bytes 1966084
  6.6 1.4 %copy-start.2 = (f32[128]{0:T(128)S(1)}, f32[128]{0:T(128)}, u32[]{:S(2)}) copy-start(f32[128]{0:T(128)} %param.12) | copy-start | bytes 1540
  6.7 1.4 %copy-start.5 = (bf16[2560,128]{1,0:T(8,128)(2,1)S(1)}, bf16[2560,128]{1,0:T(8,128)(2,1)}, u32[]{:S(2)}) copy-start(bf16[2560,128]{1,0:T(8,128)(2,1)} %refs_19_.3) | copy-start | bytes 1966084
  6.7 1.5 %copy-start.6 = (bf16[2560,128]{1,0:T(8,128)(2,1)S(1)}, bf16[2560,128]{1,0:T(8,128)(2,1)}, u32[]{:S(2)}) copy-start(bf16[2560,128]{1,0:T(8,128)(2,1)} %refs_20_.1) | copy-start | bytes 1966084
  6.7 1.5 %copy-start.7 = (f32[128]{0:T(128)S(1)}, f32[128]{0:T(128)}, u32[]{:S(2)}) copy-start(f32[128]{0:T(128)} %param.13) | copy-start | bytes 1540
  8.2 2.5 %copy-start.3 = (bf16[2560,1024]{1,0:T(8,128)(2,1)S(1)}, bf16[2560,1024]{1,0:T(8,128)(2,1)}, u32[]{:S(2)}) copy-start(bf16[2560,1024]{1,0:T(8,128)(2,1)} %refs_18_.3) | copy-start | bytes 15728644
  10.6 13.2 %copy-start.4 = (bf16[2560,1024]{1,0:T(8,128)(2,1)S(1)}, bf16[2560,1024]{1,0:T(8,128)(2,1)}, u32[]{:S(2)}) copy-start(bf16[2560,1024]{1,0:T(8,128)(2,1)} %refs_18_.3) | copy-start | bytes 15728644
  18.6 3.4 %collective-permute-start.3 = (bf16[128,2560]{1,0:T(8,128)(2,1)S(1)}, bf16[128,2560]{1,0:T(8,128)(2,1)S(1)}, u32[]{:S(2)}, u32[]{:S(2)}) collective-permute-start(bf16[128,2560]{1,0:T(8,128)(2,1)S(1)} %collective-permute-done.refs_1_), channel_id=1, source_target_pairs={{0,1},{1,0},{2,3},{3,2},{4,5},{5,4},{6,7},{7,6},{8,9},{9,8},{10,11... | collective-permute-start | bytes 1966088 | tf_op jit(solution)/shard_map/ppermute | solution.py:56
  19.2 8.3 %collective-permute-start.4 = (bf16[128,512]{1,0:T(8,128)(2,1)S(1)}, bf16[128,512]{1,0:T(8,128)(2,1)S(1)}, u32[]{:S(2)}, u32[]{:S(2)}) collective-permute-start(bf16[128,512]{1,0:T(8,128)(2,1)S(1)} %get-tuple-element.93), channel_id=1, source_target_pairs={{0,2},{1,3},{2,0},{3,1},{4,6},{5,7},{6,4},{7,5},{8,10},{9,11},{10,... | collective-permute-start | bytes 393224 | tf_op jit(solution)/shard_map/ppermute | solution.py:56
  21.0 8.1 %collective-permute-start.5 = (bf16[128,512]{1,0:T(8,128)(2,1)S(1)}, bf16[128,512]{1,0:T(8,128)(2,1)S(1)}, u32[]{:S(2)}, u32[]{:S(2)}) collective-permute-start(bf16[128,512]{1,0:T(8,128)(2,1)S(1)} %get-tuple-element.94), channel_id=1, source_target_pairs={{0,3},{1,2},{2,1},{3,0},{4,7},{5,6},{6,5},{7,4},{8,11},{9,10},{10,... | collective-permute-start | bytes 393224 | tf_op jit(solution)/shard_map/ppermute | solution.py:56
  21.2 8.4 %collective-permute-start.6 = (bf16[128,512]{1,0:T(8,128)(2,1)S(1)}, bf16[128,512]{1,0:T(8,128)(2,1)S(1)}, u32[]{:S(2)}, u32[]{:S(2)}) collective-permute-start(bf16[128,512]{1,0:T(8,128)(2,1)S(1)} %get-tuple-element.99), channel_id=1, source_target_pairs={{0,1},{1,0},{2,3},{3,2},{4,5},{5,4},{6,7},{7,6},{8,9},{9,8},{10,11... | collective-permute-start | bytes 393224 | tf_op jit(solution)/shard_map/ppermute | solution.py:56
  21.4 14.6 %collective-permute-start.8 = (bf16[128,512]{1,0:T(8,128)(2,1)S(1)}, bf16[128,512]{1,0:T(8,128)(2,1)S(1)}, u32[]{:S(2)}, u32[]{:S(2)}) collective-permute-start(bf16[128,512]{1,0:T(8,128)(2,1)S(1)} %get-tuple-element.102), channel_id=1, source_target_pairs={{0,1},{1,0},{2,3},{3,2},{4,5},{5,4},{6,7},{7,6},{8,9},{9,8},{10,11... | collective-permute-start | bytes 393224 | tf_op jit(solution)/shard_map/ppermute | solution.py:56
  22.0 11.7 %collective-permute-start.11 = (bf16[1280,128]{1,0:T(8,128)(2,1)S(1)}, bf16[1280,128]{1,0:T(8,128)(2,1)S(1)}, u32[]{:S(2)}, u32[]{:S(2)}) collective-permute-start(bf16[1280,128]{1,0:T(8,128)(2,1)S(1)} %get-tuple-element.106), channel_id=1, source_target_pairs={{0,8},{4,12},{8,0},{12,4},{16,24},{20,28},{24,16},{28,20},{1,9},{5... | collective-permute-start | bytes 983048 | tf_op jit(solution)/shard_map/ppermute | solution.py:56
  27.6 9.1 %collective-permute-start.9 = (bf16[128,512]{1,0:T(8,128)(2,1)S(1)}, bf16[128,512]{1,0:T(8,128)(2,1)S(1)}, u32[]{:S(2)}, u32[]{:S(2)}) collective-permute-start(bf16[128,512]{1,0:T(8,128)(2,1)S(1)} %get-tuple-element.103), channel_id=1, source_target_pairs={{0,2},{1,3},{2,0},{3,1},{4,6},{5,7},{6,4},{7,5},{8,10},{9,11},{10,... | collective-permute-start | bytes 393224 | tf_op jit(solution)/shard_map/ppermute | solution.py:56
  29.1 8.0 %collective-permute-start.10 = (bf16[128,512]{1,0:T(8,128)(2,1)S(1)}, bf16[128,512]{1,0:T(8,128)(2,1)S(1)}, u32[]{:S(2)}, u32[]{:S(2)}) collective-permute-start(bf16[128,512]{1,0:T(8,128)(2,1)S(1)} %get-tuple-element.104), channel_id=1, source_target_pairs={{0,3},{1,2},{2,1},{3,0},{4,7},{5,6},{6,5},{7,4},{8,11},{9,10},{10,... | collective-permute-start | bytes 393224 | tf_op jit(solution)/shard_map/ppermute | solution.py:56
  32.0 9.2 %collective-permute-start.7 = (bf16[512,256]{1,0:T(8,128)(2,1)S(1)}, bf16[512,256]{1,0:T(8,128)(2,1)S(1)}, u32[]{:S(2)}, u32[]{:S(2)}) collective-permute-start(bf16[512,256]{1,0:T(8,128)(2,1)S(1)} %get-tuple-element.100.refs_10_.refs_13_.refs_14_), channel_id=1, source_target_pairs={{0,8},{4,12},{8,0},{12,4},{16,24},{20,28},{24,16},{28,20},{1,9},{5... | collective-permute-start | bytes 786440 | tf_op jit(solution)/shard_map/ppermute | solution.py:56
  33.6 11.6 %collective-permute-start.12 = (bf16[1280,128]{1,0:T(8,128)(2,1)S(1)}, bf16[1280,128]{1,0:T(8,128)(2,1)S(1)}, u32[]{:S(2)}, u32[]{:S(2)}) collective-permute-start(bf16[1280,128]{1,0:T(8,128)(2,1)S(1)} %collective-permute-done.1.refs_6_.refs_7_.refs_8_), channel_id=1, source_target_pairs={{0,1},{1,0},{2,3},{3,2},{4,5},{5,4},{6,7},{7,6},{8,9},{9,8},{10,11... | collective-permute-start | bytes 983048 | tf_op jit(solution)/shard_map/ppermute | solution.py:56
  36.0 9.2 %collective-permute-start.13 = (bf16[1280,128]{1,0:T(8,128)(2,1)S(1)}, bf16[1280,128]{1,0:T(8,128)(2,1)S(1)}, u32[]{:S(2)}, u32[]{:S(2)}) collective-permute-start(bf16[1280,128]{1,0:T(8,128)(2,1)S(1)} %collective-permute-done.11.refs_8_.refs_9_.refs_10_), channel_id=1, source_target_pairs={{0,1},{1,0},{2,3},{3,2},{4,5},{5,4},{6,7},{7,6},{8,9},{9,8},{10,11... | collective-permute-start | bytes 983048 | tf_op jit(solution)/shard_map/ppermute | solution.py:56
  36.6 11.1 %collective-permute-start.14 = (bf16[512,256]{1,0:T(8,128)(2,1)S(1)}, bf16[512,256]{1,0:T(8,128)(2,1)S(1)}, u32[]{:S(2)}, u32[]{:S(2)}) collective-permute-start(bf16[512,256]{1,0:T(8,128)(2,1)S(1)} %get-tuple-element.119.refs_10_.refs_14_.refs_15_), channel_id=1, source_target_pairs={{0,8},{4,12},{8,0},{12,4},{16,24},{20,28},{24,16},{28,20},{1,9},{5... | collective-permute-start | bytes 786440 | tf_op jit(solution)/shard_map/ppermute | solution.py:56
  43.6 13.7 %collective-permute-start.16 = (bf16[512,256]{1,0:T(8,128)(2,1)S(1)}, bf16[512,256]{1,0:T(8,128)(2,1)S(1)}, u32[]{:S(2)}, u32[]{:S(2)}) collective-permute-start(bf16[512,256]{1,0:T(8,128)(2,1)S(1)} %get-tuple-element.125.refs_11_.refs_15_.refs_16_), channel_id=1, source_target_pairs={{0,8},{4,12},{8,0},{12,4},{16,24},{20,28},{24,16},{28,20},{1,9},{5... | collective-permute-start | bytes 786440 | tf_op jit(solution)/shard_map/ppermute | solution.py:56
  46.1 8.5 %collective-permute-start.15 = (bf16[640,256]{1,0:T(8,128)(2,1)S(1)}, bf16[640,256]{1,0:T(8,128)(2,1)S(1)}, u32[]{:S(2)}, u32[]{:S(2)}) collective-permute-start(bf16[640,256]{1,0:T(8,128)(2,1)S(1)} %get-tuple-element.123), channel_id=1, source_target_pairs={{0,4},{4,0},{8,12},{12,8},{16,20},{20,16},{24,28},{28,24},{1,5},{5... | collective-permute-start | bytes 983048 | tf_op jit(solution)/shard_map/ppermute | solution.py:56
  50.6 16.3 %collective-permute-start.19 = (bf16[512,512]{1,0:T(8,128)(2,1)S(1)}, bf16[512,512]{1,0:T(8,128)(2,1)S(1)}, u32[]{:S(2)}, u32[]{:S(2)}) collective-permute-start(bf16[512,512]{1,0:T(8,128)(2,1)S(1)} %attention.7.refs_0_.refs_16_.refs_12_.refs_17_.refs_11_), channel_id=1, source_target_pairs={{0,8},{4,12},{8,0},{12,4},{16,24},{20,28},{24,16},{28,20},{1,9},{5... | collective-permute-start | bytes 1572872 | tf_op jit(solution)/shard_map/ppermute | solution.py:56
  52.2 10.6 %collective-permute-start.17 = (bf16[640,256]{1,0:T(8,128)(2,1)S(1)}, bf16[640,256]{1,0:T(8,128)(2,1)S(1)}, u32[]{:S(2)}, u32[]{:S(2)}) collective-permute-start(bf16[640,256]{1,0:T(8,128)(2,1)S(1)} %get-tuple-element.127), channel_id=1, source_target_pairs={{0,4},{4,0},{8,12},{12,8},{16,20},{20,16},{24,28},{28,24},{1,5},{5... | collective-permute-start | bytes 983048 | tf_op jit(solution)/shard_map/ppermute | solution.py:56
  54.7 12.2 %collective-permute-start.18 = (bf16[320,256]{1,0:T(8,128)(2,1)S(1)}, bf16[320,256]{1,0:T(8,128)(2,1)S(1)}, u32[]{:S(2)}, u32[]{:S(2)}) collective-permute-start(bf16[320,256]{1,0:T(8,128)(2,1)S(1)} %get-tuple-element.129), channel_id=1, source_target_pairs={{0,16},{4,20},{8,24},{12,28},{16,0},{20,4},{24,8},{28,12},{1,17},{... | collective-permute-start | bytes 491528 | tf_op jit(solution)/shard_map/ppermute | solution.py:56
  61.1 11.3 %collective-permute-start.20 = (bf16[640,256]{1,0:T(8,128)(2,1)S(1)}, bf16[640,256]{1,0:T(8,128)(2,1)S(1)}, u32[]{:S(2)}, u32[]{:S(2)}) collective-permute-start(bf16[640,256]{1,0:T(8,128)(2,1)S(1)} %get-tuple-element.131), channel_id=1, source_target_pairs={{0,4},{4,0},{8,12},{12,8},{16,20},{20,16},{24,28},{28,24},{1,5},{5... | collective-permute-start | bytes 983048 | tf_op jit(solution)/shard_map/ppermute | solution.py:56
  62.7 21.9 %collective-permute-start.21 = (bf16[256,1280]{1,0:T(8,128)(2,1)S(1)}, bf16[256,1280]{1,0:T(8,128)(2,1)S(1)}, u32[]{:S(2)}, u32[]{:S(2)}) collective-permute-start(bf16[256,1280]{1,0:T(8,128)(2,1)S(1)} %get-tuple-element.135), channel_id=1, source_target_pairs={{0,1},{1,0},{2,3},{3,2},{4,5},{5,4},{6,7},{7,6},{8,9},{9,8},{10,11... | collective-permute-start | bytes 1966088 | tf_op jit(solution)/shard_map/ppermute | solution.py:56
  62.8 14.0 %collective-permute-start.25 = (bf16[320,256]{1,0:T(8,128)(2,1)S(1)}, bf16[320,256]{1,0:T(8,128)(2,1)S(1)}, u32[]{:S(2)}, u32[]{:S(2)}) collective-permute-start(bf16[320,256]{1,0:T(8,128)(2,1)S(1)} %get-tuple-element.144), channel_id=1, source_target_pairs={{0,16},{4,20},{8,24},{12,28},{16,0},{20,4},{24,8},{28,12},{1,17},{... | collective-permute-start | bytes 491528 | tf_op jit(solution)/shard_map/ppermute | solution.py:56
  70.5 14.9 %collective-permute-start.22 = (bf16[256,1280]{1,0:T(8,128)(2,1)S(1)}, bf16[256,1280]{1,0:T(8,128)(2,1)S(1)}, u32[]{:S(2)}, u32[]{:S(2)}) collective-permute-start(bf16[256,1280]{1,0:T(8,128)(2,1)S(1)} %get-tuple-element.138), channel_id=1, source_target_pairs={{0,1},{1,0},{2,3},{3,2},{4,5},{5,4},{6,7},{7,6},{8,9},{9,8},{10,11... | collective-permute-start | bytes 1966088 | tf_op jit(solution)/shard_map/ppermute | solution.py:56
  70.5 10.6 %collective-permute-start.26 = (bf16[640,256]{1,0:T(8,128)(2,1)S(1)}, bf16[640,256]{1,0:T(8,128)(2,1)S(1)}, u32[]{:S(2)}, u32[]{:S(2)}) collective-permute-start(bf16[640,256]{1,0:T(8,128)(2,1)S(1)} %get-tuple-element.145), channel_id=1, source_target_pairs={{0,4},{4,0},{8,12},{12,8},{16,20},{20,16},{24,28},{28,24},{1,5},{5... | collective-permute-start | bytes 983048 | tf_op jit(solution)/shard_map/ppermute | solution.py:56
  72.5 14.6 %collective-permute-start.27 = (bf16[320,256]{1,0:T(8,128)(2,1)S(1)}, bf16[320,256]{1,0:T(8,128)(2,1)S(1)}, u32[]{:S(2)}, u32[]{:S(2)}) collective-permute-start(bf16[320,256]{1,0:T(8,128)(2,1)S(1)} %get-tuple-element.147), channel_id=1, source_target_pairs={{0,16},{4,20},{8,24},{12,28},{16,0},{20,4},{24,8},{28,12},{1,17},{... | collective-permute-start | bytes 491528 | tf_op jit(solution)/shard_map/ppermute | solution.py:56
  76.8 10.9 %collective-permute-start.29 = (bf16[640,256]{1,0:T(8,128)(2,1)S(1)}, bf16[640,256]{1,0:T(8,128)(2,1)S(1)}, u32[]{:S(2)}, u32[]{:S(2)}) collective-permute-start(bf16[640,256]{1,0:T(8,128)(2,1)S(1)} %get-tuple-element.151), channel_id=1, source_target_pairs={{0,4},{4,0},{8,12},{12,8},{16,20},{20,16},{24,28},{28,24},{1,5},{5... | collective-permute-start | bytes 983048 | tf_op jit(solution)/shard_map/ppermute | solution.py:56
  81.2 20.4 %collective-permute-start.28 = (bf16[320,256]{1,0:T(8,128)(2,1)S(1)}, bf16[320,256]{1,0:T(8,128)(2,1)S(1)}, u32[]{:S(2)}, u32[]{:S(2)}) collective-permute-start(bf16[320,256]{1,0:T(8,128)(2,1)S(1)} %get-tuple-element.148), channel_id=1, source_target_pairs={{0,16},{4,20},{8,24},{12,28},{16,0},{20,4},{24,8},{28,12},{1,17},{... | collective-permute-start | bytes 491528 | tf_op jit(solution)/shard_map/ppermute | solution.py:56
  84.8 10.7 %collective-permute-start.23 = (bf16[128,1280]{1,0:T(8,128)(2,1)S(1)}, bf16[128,1280]{1,0:T(8,128)(2,1)S(1)}, u32[]{:S(2)}, u32[]{:S(2)}) collective-permute-start(bf16[128,1280]{1,0:T(8,128)(2,1)S(1)} %get-tuple-element.140), channel_id=1, source_target_pairs={{0,2},{1,3},{2,0},{3,1},{4,6},{5,7},{6,4},{7,5},{8,10},{9,11},{10,... | collective-permute-start | bytes 983048 | tf_op jit(solution)/shard_map/ppermute | solution.py:56
  85.6 15.0 %collective-permute-start.24 = (bf16[128,1280]{1,0:T(8,128)(2,1)S(1)}, bf16[128,1280]{1,0:T(8,128)(2,1)S(1)}, u32[]{:S(2)}, u32[]{:S(2)}) collective-permute-start(bf16[128,1280]{1,0:T(8,128)(2,1)S(1)} %get-tuple-element.141), channel_id=1, source_target_pairs={{0,2},{1,3},{2,0},{3,1},{4,6},{5,7},{6,4},{7,5},{8,10},{9,11},{10,... | collective-permute-start | bytes 983048 | tf_op jit(solution)/shard_map/ppermute | solution.py:56
  87.8 14.9 %collective-permute-start.30 = (bf16[320,256]{1,0:T(8,128)(2,1)S(1)}, bf16[320,256]{1,0:T(8,128)(2,1)S(1)}, u32[]{:S(2)}, u32[]{:S(2)}) collective-permute-start(bf16[320,256]{1,0:T(8,128)(2,1)S(1)} %get-tuple-element.153), channel_id=1, source_target_pairs={{0,16},{4,20},{8,24},{12,28},{16,0},{20,4},{24,8},{28,12},{1,17},{... | collective-permute-start | bytes 491528 | tf_op jit(solution)/shard_map/ppermute | solution.py:56

commit v4 on v3

--- a/solution.py
+++ b/solution.py
@@ -509,9 +509,9 @@
     ends.append(last_steps(*firsts[1]))
     keep, *second_half = product(3, (keep, ends[1][0], ends[0][1]), LONG, input_part(1))
     ends.append(last_steps(*firsts[2]))
-    tied = product(4, (keep, ends[2][0], ), LONG)
+    tied = product(4, (keep, ends[2][0], ends[1][1]), LONG)
     inputs = [halved(*half, (tied[0],)) for half in (first_half, second_half)]
-    ends.append(last_steps(*firsts[3], (ends[1][1],)))
+    ends.append(last_steps(*firsts[3], (inputs[0][0], inputs[1][0], )))
     ends.append(last_steps(*firsts[4], (ends[2][1],)))
     pieces = [i[0] for i in inputs] + [i[1] for i in inputs]
     token = ((8, 128), f32)

time: 104 us -> 101 us (0.971)
  starting transfers between devices: 41.1 us -> 37.1 us
    ppermute x31, starting transfers between devices: 41.1 us -> 37.1 us  [exchange(): return lax.ppermute(value, axis, [(d, d ^ bit) for d in range(size)])]
  transfers between devices with their start and end apart: 31 -> 31, of which waited for: 9 -> 10; matrix products, arithmetic and copies ran while one was open for 1% -> 1% of each run, Pallas kernels for 30% -> 31%
where the time goes in v4:
time: 101 us; the launch traced here: 100 us
  starting transfers between devices  37.1 us (37%)
  Pallas kernels  31.4 us (31%)
  waiting for transfers between devices  25.3 us (25%)
  local copies, waits for them, and re-layouts  3.82 us (4%)
  between operations  1.57 us (2%)
  other arithmetic  1.21 us (1%)
    ppermute x31, starting transfers between devices, exchange(): return lax.ppermute(value, axis, [(d, d ^ bit) for d in range(size)])  37.1 us
    pallas_call x22, Pallas kernels, call(): pl.pallas_call(body, in_specs=[ANY] * count + [SMEM] * len(scalars) + [VM...  28.5 us
    ppermute x31, waiting for transfers between devices, exchange(): return lax.ppermute(value, axis, [(d, d ^ bit) for d in range(size)])  25.3 us
    unnamed x18, local copies, waits for them, and re-layouts  3.7 us
    pallas_call x3, Pallas kernels, last_sum(): pl.pallas_call(functools.partial(kernel, len(deps)) if deps else kernel,...  2.89 us
  transfers between devices with their start and end apart: 31, of which 10 were waited for; matrix products, arithmetic and copies ran while one was open for 1% of the time, Pallas kernels for 31%

profile of v4, /device:TPU:0, one launch (start us, length us, event | category | flops | bytes accessed | tf_op | source)
XLA Modules:
  0.0 100.4 jit_solution(14430363706624024800)
XLA Ops:
  0.6 3.0 %collective-permute-start = (bf16[128,2560]{1,0:T(8,128)(2,1)}, bf16[128,2560]{1,0:T(8,128)(2,1)S(1)}, u32[]{:S(2)}, u32[]{:S(2)}) collective-permute-start(bf16[128,2560]{1,0:T(8,128)(2,1)} %refs_1_.4), channel_id=1, source_target_pairs={{0,2},{1,3},{2,0},{3,1},{4,6},{5,7},{6,4},{7,5},{8,10},{9,11},{10,... | collective-permute-start | bytes 1966088 | tf_op jit(solution)/shard_map/ppermute | solution.py:56
  3.6 1.1 %copy-done = bf16[128,2560]{1,0:T(8,128)(2,1)S(1)} copy-done((bf16[128,2560]{1,0:T(8,128)(2,1)S(1)}, bf16[128,2560]{1,0:T(8,128)(2,1)}, u32[]{:S(2)}) %copy-start) | copy-done | bytes 655384
  5.0 1.6 %collective-permute-start.1 = (bf16[1280,128]{1,0:T(8,128)(2,1)S(1)}, bf16[1280,128]{1,0:T(8,128)(2,1)S(1)}, u32[]{:S(2)}, u32[]{:S(2)}) collective-permute-start(bf16[1280,128]{1,0:T(8,128)(2,1)S(1)} %get-tuple-element.80), channel_id=1, source_target_pairs={{0,8},{4,12},{8,0},{12,4},{16,24},{20,28},{24,16},{28,20},{1,9},{5... | collective-permute-start | bytes 983048 | tf_op jit(solution)/shard_map/ppermute | solution.py:56
  6.7 1.0 fusion
  8.2 2.5 %copy-done.3 = bf16[2560,1024]{1,0:T(8,128)(2,1)S(1)} copy-done((bf16[2560,1024]{1,0:T(8,128)(2,1)S(1)}, bf16[2560,1024]{1,0:T(8,128)(2,1)}, u32[]{:S(2)}) %copy-start.3) | copy-done | bytes 5242904
  10.6 3.6 %projections.2 = (bf16[512,1024]{1,0:T(8,128)(2,1)S(1)}, f32[512,1024]{1,0:T(8,128)S(1)}, bf16[512,128]{1,0:T(8,128)(2,1)S(1)}, f32[512,128]{1,0:T(8,128)S(1)}, bf16[512,128]{1,0:T(8,128)(2,1)S(1)}) custom-call(s32[1]{0:T(128)} %bitcast.refs_0_.refs_1_.refs_2_.refs_3_, bf16[128,2560]{1,0:T(8,128)(2,1)S(1)} %copy-done.1, ...), custom_call_target="tpu_custom_call" | custom-call | flops 23000000512 | bytes 1024 | tf_op jit(solution)/shard_map/projections/pallas_call | solution.py:29
  14.4 0.8 collective-permute-done.1.refs_6_.refs_7_.refs_8_
  15.1 3.4 %collective-permute-done.refs_1_ = bf16[128,2560]{1,0:T(8,128)(2,1)S(1)} collective-permute-done((bf16[128,2560]{1,0:T(8,128)(2,1)}, bf16[128,2560]{1,0:T(8,128)(2,1)S(1)}, u32[]{:S(2)}, u32[]{:S(2)}) %collective-permute-start) | collective-permute-done | bytes 655392 | tf_op jit(solution)/shard_map/ppermute | solution.py:56
  19.2 1.8 %collective-permute-start.4 = (bf16[128,512]{1,0:T(8,128)(2,1)S(1)}, bf16[128,512]{1,0:T(8,128)(2,1)S(1)}, u32[]{:S(2)}, u32[]{:S(2)}) collective-permute-start(bf16[128,512]{1,0:T(8,128)(2,1)S(1)} %get-tuple-element.93), channel_id=1, source_target_pairs={{0,2},{1,3},{2,0},{3,1},{4,6},{5,7},{6,4},{7,5},{8,10},{9,11},{10,... | collective-permute-start | bytes 393224 | tf_op jit(solution)/shard_map/ppermute | solution.py:56
  22.0 1.8 %collective-permute-start.11 = (bf16[1280,128]{1,0:T(8,128)(2,1)S(1)}, bf16[1280,128]{1,0:T(8,128)(2,1)S(1)}, u32[]{:S(2)}, u32[]{:S(2)}) collective-permute-start(bf16[1280,128]{1,0:T(8,128)(2,1)S(1)} %get-tuple-element.106), channel_id=1, source_target_pairs={{0,8},{4,12},{8,0},{12,4},{16,24},{20,28},{24,16},{28,20},{1,9},{5... | collective-permute-start | bytes 983048 | tf_op jit(solution)/shard_map/ppermute | solution.py:56
  23.8 3.7 %projections.3 = (bf16[512,1024]{1,0:T(8,128)(2,1)S(1)}, f32[512,1024]{1,0:T(8,128)S(1)}, bf16[512,128]{1,0:T(8,128)(2,1)S(1)}, f32[512,128]{1,0:T(8,128)S(1)}, bf16[512,128]{1,0:T(8,128)(2,1)S(1)}) custom-call(s32[1]{0:T(128)} %bitcast.refs_0_.refs_1_.refs_2_.refs_3_, ...), custom_call_target="tpu_custom_call", output_to_operand_aliasing={{0}: (10, {}), {1}: (11, {}), {2}: (12, {}), {3}: (13, {}),... | custom-call | flops 23000000512 | bytes 1024 | tf_op jit(solution)/shard_map/projections/pallas_call | solution.py:29
  27.6 1.6 %collective-permute-start.9 = (bf16[128,512]{1,0:T(8,128)(2,1)S(1)}, bf16[128,512]{1,0:T(8,128)(2,1)S(1)}, u32[]{:S(2)}, u32[]{:S(2)}) collective-permute-start(bf16[128,512]{1,0:T(8,128)(2,1)S(1)} %get-tuple-element.103), channel_id=1, source_target_pairs={{0,2},{1,3},{2,0},{3,1},{4,6},{5,7},{6,4},{7,5},{8,10},{9,11},{10,... | collective-permute-start | bytes 393224 | tf_op jit(solution)/shard_map/ppermute | solution.py:56
  29.6 2.4 %attention.4 = (bf16[512,256]{1,0:T(8,128)(2,1)S(1)}, f32[512,128]{1,0:T(8,128)S(1)}, f32[512,128]{1,0:T(8,128)S(1)}) custom-call(bf16[1280,128]{1,0:T(8,128)(2,1)S(1)} %transposed.6.refs_0_.refs_5_.refs_6_.refs_7_, s32[1]{0:T(128)} %bitcast.refs_0_.refs_1_.refs_2_.refs_3_, s32[1]{0:T(128)S(6)} %copy.22.refs_2_.refs_1_.refs_3_, ...), custom_call_target="tpu_custom_call" | custom-call | flops 1000000 | bytes 1024 | tf_op jit(solution)/shard_map/attention/pallas_call | solution.py:29
  32.0 1.6 %collective-permute-start.7 = (bf16[512,256]{1,0:T(8,128)(2,1)S(1)}, bf16[512,256]{1,0:T(8,128)(2,1)S(1)}, u32[]{:S(2)}, u32[]{:S(2)}) collective-permute-start(bf16[512,256]{1,0:T(8,128)(2,1)S(1)} %get-tuple-element.100.refs_10_.refs_13_.refs_14_), channel_id=1, source_target_pairs={{0,8},{4,12},{8,0},{12,4},{16,24},{20,28},{24,16},{28,20},{1,9},{5... | collective-permute-start | bytes 786440 | tf_op jit(solution)/shard_map/ppermute | solution.py:56
  33.6 2.4 %attention.5 = (bf16[512,256]{1,0:T(8,128)(2,1)S(1)}, f32[512,128]{1,0:T(8,128)S(1)}, f32[512,128]{1,0:T(8,128)S(1)}) custom-call(s32[1]{0:T(128)} %bitcast.refs_0_.refs_1_.refs_2_.refs_3_, s32[1]{0:T(128)S(6)} %copy.22.refs_2_.refs_1_.refs_3_, bf16[512,1024]{1,0:T(8,128)(2,1)S(1)} %get-tuple-element.95.refs_3_.refs_2_.refs_4_, ...), custom_call_target="tpu_custom_call" | custom-call | flops 23000000512 | bytes 1024 | tf_op jit(solution)/shard_map/attention/pallas_call | solution.py:29
  36.0 0.6 collective-permute-start.13
  37.1 4.1 %collective-permute-done.7.refs_0_.refs_11_ = bf16[512,256]{1,0:T(8,128)(2,1)S(1)} collective-permute-done((bf16[512,256]{1,0:T(8,128)(2,1)S(1)}, bf16[512,256]{1,0:T(8,128)(2,1)S(1)}, u32[]{:S(2)}, u32[]{:S(2)}) %collective-permute-start.7) | collective-permute-done | bytes 262176 | tf_op jit(solution)/shard_map/ppermute | solution.py:56
  41.2 2.4 %attention.6 = (bf16[512,256]{1,0:T(8,128)(2,1)S(1)}, f32[512,128]{1,0:T(8,128)S(1)}, f32[512,128]{1,0:T(8,128)S(1)}) custom-call(bf16[512,256]{1,0:T(8,128)(2,1)S(1)} %collective-permute-done.7.refs_0_.refs_11_, s32[1]{0:T(128)} %bitcast.refs_0_.refs_1_.refs_2_.refs_3_, s32[1]{0:T(128)S(6)} %copy.22.refs_2_.refs_1_.refs_3_, ...), custom_call_target="tpu_custom_call" | custom-call | flops 23000000512 | bytes 1024 | tf_op jit(solution)/shard_map/attention/pallas_call | solution.py:29
  43.6 1.7 %collective-permute-start.16 = (bf16[512,256]{1,0:T(8,128)(2,1)S(1)}, bf16[512,256]{1,0:T(8,128)(2,1)S(1)}, u32[]{:S(2)}, u32[]{:S(2)}) collective-permute-start(bf16[512,256]{1,0:T(8,128)(2,1)S(1)} %get-tuple-element.125.refs_11_.refs_15_.refs_16_), channel_id=1, source_target_pairs={{0,8},{4,12},{8,0},{12,4},{16,24},{20,28},{24,16},{28,20},{1,9},{5... | collective-permute-start | bytes 786440 | tf_op jit(solution)/shard_map/ppermute | solution.py:56
  45.3 0.8 weight_products.3
  46.1 1.6 %collective-permute-start.15 = (bf16[640,256]{1,0:T(8,128)(2,1)S(1)}, bf16[640,256]{1,0:T(8,128)(2,1)S(1)}, u32[]{:S(2)}, u32[]{:S(2)}) collective-permute-start(bf16[640,256]{1,0:T(8,128)(2,1)S(1)} %get-tuple-element.123), channel_id=1, source_target_pairs={{0,4},{4,0},{8,12},{12,8},{16,20},{20,16},{24,28},{28,24},{1,5},{5... | collective-permute-start | bytes 983048 | tf_op jit(solution)/shard_map/ppermute | solution.py:56
  47.7 2.9 %attention.7.refs_0_.refs_16_.refs_12_.refs_17_ = bf16[512,512]{1,0:T(8,128)(2,1)S(1)} custom-call(f32[640,256]{1,0:T(8,128)S(1)} %get-tuple-element.118.refs_0_, bf16[512,256]{1,0:T(8,128)(2,1)S(1)} %collective-permute-done.14.refs_1_.refs_11_, s32[1]{0:T(128)} %bitcast.refs_0_.refs_1_.refs_2_.refs_3_, s32[1]{0:T(128)S(6)} %copy.22.refs_2_.refs_1_.refs_3_, ...), custom_call_target="tpu_custom_call" | custom-call | flops 23000000512 | bytes 1024 | tf_op jit(solution)/shard_map/attention/pallas_call | solution.py:29
  50.6 0.8 collective-permute-start.19
  51.3 0.8 weight_products.4
  52.2 1.6 %collective-permute-start.17 = (bf16[640,256]{1,0:T(8,128)(2,1)S(1)}, bf16[640,256]{1,0:T(8,128)(2,1)S(1)}, u32[]{:S(2)}, u32[]{:S(2)}) collective-permute-start(bf16[640,256]{1,0:T(8,128)(2,1)S(1)} %get-tuple-element.127), channel_id=1, source_target_pairs={{0,4},{4,0},{8,12},{12,8},{16,20},{20,16},{24,28},{28,24},{1,5},{5... | collective-permute-start | bytes 983048 | tf_op jit(solution)/shard_map/ppermute | solution.py:56
  53.8 0.8 collective-permute-done.15.refs_1_
  54.7 2.6 %collective-permute-start.18 = (bf16[320,256]{1,0:T(8,128)(2,1)S(1)}, bf16[320,256]{1,0:T(8,128)(2,1)S(1)}, u32[]{:S(2)}, u32[]{:S(2)}) collective-permute-start(bf16[320,256]{1,0:T(8,128)(2,1)S(1)} %get-tuple-element.129), channel_id=1, source_target_pairs={{0,16},{4,20},{8,24},{12,28},{16,0},{20,4},{24,8},{28,12},{1,17},{... | collective-permute-start | bytes 491528 | tf_op jit(solution)/shard_map/ppermute | solution.py:56
  57.3 3.8 %both_products.2 = (bf16[640,256]{1,0:T(8,128)(2,1)S(1)}, f32[640,256]{1,0:T(8,128)S(1)}, bf16[256,1280]{1,0:T(8,128)(2,1)S(1)}, f32[256,1280]{1,0:T(8,128)S(1)}) custom-call(f32[640,256]{1,0:T(8,128)S(1)} %get-tuple-element.122.refs_0_, f32[320,256]{1,0:T(8,128)S(1)} %get-tuple-element.124.refs_1_, s32[1]{0:T(128)} %bitcast.refs_0_.refs_1_.refs_2_.refs_3_, ...), custom_call_target="tpu_custom_call" | custom-call | flops 23000000512 | bytes 1024 | tf_op jit(solution)/shard_map/both_products/pallas_call | solution.py:29
  61.2 1.6 %collective-permute-start.20 = (bf16[640,256]{1,0:T(8,128)(2,1)S(1)}, bf16[640,256]{1,0:T(8,128)(2,1)S(1)}, u32[]{:S(2)}, u32[]{:S(2)}) collective-permute-start(bf16[640,256]{1,0:T(8,128)(2,1)S(1)} %get-tuple-element.131), channel_id=1, source_target_pairs={{0,4},{4,0},{8,12},{12,8},{16,20},{20,16},{24,28},{28,24},{1,5},{5... | collective-permute-start | bytes 983048 | tf_op jit(solution)/shard_map/ppermute | solution.py:56
  62.8 2.8 %collective-permute-start.21 = (bf16[320,256]{1,0:T(8,128)(2,1)S(1)}, bf16[320,256]{1,0:T(8,128)(2,1)S(1)}, u32[]{:S(2)}, u32[]{:S(2)}) collective-permute-start(bf16[320,256]{1,0:T(8,128)(2,1)S(1)} %get-tuple-element.133), channel_id=1, source_target_pairs={{0,16},{4,20},{8,24},{12,28},{16,0},{20,4},{24,8},{28,12},{1,17},{... | collective-permute-start | bytes 491528 | tf_op jit(solution)/shard_map/ppermute | solution.py:56
  65.6 1.5 %collective-permute-done.18.refs_2_.refs_5_ = bf16[320,256]{1,0:T(8,128)(2,1)S(1)} collective-permute-done((bf16[320,256]{1,0:T(8,128)(2,1)S(1)}, bf16[320,256]{1,0:T(8,128)(2,1)S(1)}, u32[]{:S(2)}, u32[]{:S(2)}) %collective-permute-start.18) | collective-permute-done | bytes 163872 | tf_op jit(solution)/shard_map/ppermute | solution.py:56
  67.2 1.3 %collective-permute-done.19.refs_13_ = bf16[512,512]{1,0:T(8,128)(2,1)S(1)} collective-permute-done((bf16[512,512]{1,0:T(8,128)(2,1)S(1)}, bf16[512,512]{1,0:T(8,128)(2,1)S(1)}, u32[]{:S(2)}, u32[]{:S(2)}) %collective-permute-start.19) | collective-permute-done | bytes 524320 | tf_op jit(solution)/shard_map/ppermute | solution.py:56
  68.5 3.6 %both_products.3 = (bf16[640,256]{1,0:T(8,128)(2,1)S(1)}, f32[640,256]{1,0:T(8,128)S(1)}, bf16[256,1280]{1,0:T(8,128)(2,1)S(1)}, f32[256,1280]{1,0:T(8,128)S(1)}) custom-call(f32[640,256]{1,0:T(8,128)S(1)} %get-tuple-element.126.refs_0_, f32[320,256]{1,0:T(8,128)S(1)} %get-tuple-element.128.refs_1_.refs_2_, ...), custom_call_target="tpu_custom_call" | custom-call | flops 23000000512 | bytes 1024 | tf_op jit(solution)/shard_map/both_products/pallas_call | solution.py:29
  72.2 1.5 %collective-permute-start.26 = (bf16[640,256]{1,0:T(8,128)(2,1)S(1)}, bf16[640,256]{1,0:T(8,128)(2,1)S(1)}, u32[]{:S(2)}, u32[]{:S(2)}) collective-permute-start(bf16[640,256]{1,0:T(8,128)(2,1)S(1)} %get-tuple-element.145), channel_id=1, source_target_pairs={{0,4},{4,0},{8,12},{12,8},{16,20},{20,16},{24,28},{28,24},{1,5},{5... | collective-permute-start | bytes 983048 | tf_op jit(solution)/shard_map/ppermute | solution.py:56
  73.7 2.3 %collective-permute-start.27 = (bf16[320,256]{1,0:T(8,128)(2,1)S(1)}, bf16[320,256]{1,0:T(8,128)(2,1)S(1)}, u32[]{:S(2)}, u32[]{:S(2)}) collective-permute-start(bf16[320,256]{1,0:T(8,128)(2,1)S(1)} %get-tuple-element.147), channel_id=1, source_target_pairs={{0,16},{4,20},{8,24},{12,28},{16,0},{20,4},{24,8},{28,12},{1,17},{... | collective-permute-start | bytes 491528 | tf_op jit(solution)/shard_map/ppermute | solution.py:56
  76.0 0.8 weight_products.5
  76.8 0.6 collective-permute-start.29
  77.6 0.8 collective-permute-start.24
  78.5 1.3 %collective-permute-start.25 = (bf16[128,1280]{1,0:T(8,128)(2,1)S(1)}, bf16[128,1280]{1,0:T(8,128)(2,1)S(1)}, u32[]{:S(2)}, u32[]{:S(2)}) collective-permute-start(bf16[128,1280]{1,0:T(8,128)(2,1)S(1)} %get-tuple-element.142), channel_id=1, source_target_pairs={{0,2},{1,3},{2,0},{3,1},{4,6},{5,7},{6,4},{7,5},{8,10},{9,11},{10,... | collective-permute-start | bytes 983048 | tf_op jit(solution)/shard_map/ppermute | solution.py:56
  79.8 2.9 %collective-permute-done.26.refs_3_ = bf16[640,256]{1,0:T(8,128)(2,1)S(1)} collective-permute-done((bf16[640,256]{1,0:T(8,128)(2,1)S(1)}, bf16[640,256]{1,0:T(8,128)(2,1)S(1)}, u32[]{:S(2)}, u32[]{:S(2)}) %collective-permute-start.26) | collective-permute-done | bytes 327712 | tf_op jit(solution)/shard_map/ppermute | solution.py:56
  82.8 2.2 %collective-permute-start.28 = (bf16[320,256]{1,0:T(8,128)(2,1)S(1)}, bf16[320,256]{1,0:T(8,128)(2,1)S(1)}, u32[]{:S(2)}, u32[]{:S(2)}) collective-permute-start(bf16[320,256]{1,0:T(8,128)(2,1)S(1)} %get-tuple-element.148), channel_id=1, source_target_pairs={{0,16},{4,20},{8,24},{12,28},{16,0},{20,4},{24,8},{28,12},{1,17},{... | collective-permute-start | bytes 491528 | tf_op jit(solution)/shard_map/ppermute | solution.py:56
  85.0 4.3 %collective-permute-done.29.refs_2_ = bf16[640,256]{1,0:T(8,128)(2,1)S(1)} collective-permute-done((bf16[640,256]{1,0:T(8,128)(2,1)S(1)}, bf16[640,256]{1,0:T(8,128)(2,1)S(1)}, u32[]{:S(2)}, u32[]{:S(2)}) %collective-permute-start.29) | collective-permute-done | bytes 327712 | tf_op jit(solution)/shard_map/ppermute | solution.py:56
  89.4 2.2 %collective-permute-start.30 = (bf16[320,256]{1,0:T(8,128)(2,1)S(1)}, bf16[320,256]{1,0:T(8,128)(2,1)S(1)}, u32[]{:S(2)}, u32[]{:S(2)}) collective-permute-start(bf16[320,256]{1,0:T(8,128)(2,1)S(1)} %get-tuple-element.153), channel_id=1, source_target_pairs={{0,16},{4,20},{8,24},{12,28},{16,0},{20,4},{24,8},{28,12},{1,17},{... | collective-permute-start | bytes 491528 | tf_op jit(solution)/shard_map/ppermute | solution.py:56
  91.6 2.3 %collective-permute-done.25.refs_3_ = bf16[128,1280]{1,0:T(8,128)(2,1)S(1)} collective-permute-done((bf16[128,1280]{1,0:T(8,128)(2,1)S(1)}, bf16[128,1280]{1,0:T(8,128)(2,1)S(1)}, u32[]{:S(2)}, u32[]{:S(2)}) %collective-permute-start.25) | collective-permute-done | bytes 327712 | tf_op jit(solution)/shard_map/ppermute | solution.py:56
  93.9 1.0 last_sum.3
  94.9 1.2 %last_sum.4 = (f32[320,1024]{1,0:T(8,128)}, f32[8,128]{1,0:T(8,128)S(1)}) custom-call(f32[8,128]{1,0:T(8,128)S(1)} %get-tuple-element.144.refs_0_, f32[320,256]{1,0:T(8,128)S(1)} %get-tuple-element.124.refs_1_, f32[320,256]{1,0:T(8,128)S(1)} %get-tuple-element.128.refs_1_.refs_2_, f32[320,256]{1,0:T(8,128)S(1)} %get-tuple-element.132.refs_1_.refs_3_, ...), custom_call_target="tpu_custom_call" | custom-call | flops 1024 | bytes 1024 | tf_op jit(solution)/shard_map/last_sum/pallas_call | solution.py:409
  96.0 3.6 %collective-permute-done.30.refs_2_ = bf16[320,256]{1,0:T(8,128)(2,1)S(1)} collective-permute-done((bf16[320,256]{1,0:T(8,128)(2,1)S(1)}, bf16[320,256]{1,0:T(8,128)(2,1)S(1)}, u32[]{:S(2)}, u32[]{:S(2)}) %collective-permute-start.30) | collective-permute-done | bytes 163872 | tf_op jit(solution)/shard_map/ppermute | solution.py:56
  99.6 0.7 last_sum.5
  (62 shorter events, 3.3 us)
Async XLA Ops:
  0.6 17.9 %collective-permute-start = (bf16[128,2560]{1,0:T(8,128)(2,1)}, bf16[128,2560]{1,0:T(8,128)(2,1)S(1)}, u32[]{:S(2)}, u32[]{:S(2)}) collective-permute-start(bf16[128,2560]{1,0:T(8,128)(2,1)} %refs_1_.4), channel_id=1, source_target_pairs={{0,2},{1,3},{2,0},{3,1},{4,6},{5,7},{6,4},{7,5},{8,10},{9,11},{10,... | collective-permute-start | bytes 1966088 | tf_op jit(solution)/shard_map/ppermute | solution.py:56
  3.6 4.4 %collective-permute-start.2 = (bf16[128,2560]{1,0:T(8,128)(2,1)}, bf16[128,2560]{1,0:T(8,128)(2,1)S(1)}, u32[]{:S(2)}, u32[]{:S(2)}) collective-permute-start(bf16[128,2560]{1,0:T(8,128)(2,1)} %refs_1_.4), channel_id=1, source_target_pairs={{0,1},{1,0},{2,3},{3,2},{4,5},{5,4},{6,7},{7,6},{8,9},{9,8},{10,11... | collective-permute-start | bytes 1966088 | tf_op jit(solution)/shard_map/ppermute | solution.py:56
  3.6 1.1 %copy-start = (bf16[128,2560]{1,0:T(8,128)(2,1)S(1)}, bf16[128,2560]{1,0:T(8,128)(2,1)}, u32[]{:S(2)}) copy-start(bf16[128,2560]{1,0:T(8,128)(2,1)} %refs_1_.4) | copy-start | bytes 1966084
  4.8 3.2 %copy-start.8 = (bf16[128,4096]{1,0:T(8,128)(2,1)S(1)}, bf16[128,4096]{1,0:T(8,128)(2,1)}, u32[]{:S(2)}) copy-start(bf16[128,4096]{1,0:T(8,128)(2,1)} %param.14) | copy-start | bytes 3145732
  5.0 10.2 %collective-permute-start.1 = (bf16[1280,128]{1,0:T(8,128)(2,1)S(1)}, bf16[1280,128]{1,0:T(8,128)(2,1)S(1)}, u32[]{:S(2)}, u32[]{:S(2)}) collective-permute-start(bf16[1280,128]{1,0:T(8,128)(2,1)S(1)} %get-tuple-element.80), channel_id=1, source_target_pairs={{0,8},{4,12},{8,0},{12,4},{16,24},{20,28},{24,16},{28,20},{1,9},{5... | collective-permute-start | bytes 983048 | tf_op jit(solution)/shard_map/ppermute | solution.py:56
  6.6 1.4 %copy-start.1 = (bf16[128,2560]{1,0:T(8,128)(2,1)S(1)}, bf16[128,2560]{1,0:T(8,128)(2,1)}, u32[]{:S(2)}) copy-start(bf16[128,2560]{1,0:T(8,128)(2,1)} %refs_1_.4) | copy-start | bytes 1966084
  6.6 1.4 %copy-start.2 = (f32[128]{0:T(128)S(1)}, f32[128]{0:T(128)}, u32[]{:S(2)}) copy-start(f32[128]{0:T(128)} %param.12) | copy-start | bytes 1540
  6.7 1.4 %copy-start.5 = (bf16[2560,128]{1,0:T(8,128)(2,1)S(1)}, bf16[2560,128]{1,0:T(8,128)(2,1)}, u32[]{:S(2)}) copy-start(bf16[2560,128]{1,0:T(8,128)(2,1)} %refs_19_.3) | copy-start | bytes 1966084
  6.7 1.5 %copy-start.6 = (bf16[2560,128]{1,0:T(8,128)(2,1)S(1)}, bf16[2560,128]{1,0:T(8,128)(2,1)}, u32[]{:S(2)}) copy-start(bf16[2560,128]{1,0:T(8,128)(2,1)} %refs_20_.1) | copy-start | bytes 1966084
  6.7 1.5 %copy-start.7 = (f32[128]{0:T(128)S(1)}, f32[128]{0:T(128)}, u32[]{:S(2)}) copy-start(f32[128]{0:T(128)} %param.13) | copy-start | bytes 1540
  8.2 2.5 %copy-start.3 = (bf16[2560,1024]{1,0:T(8,128)(2,1)S(1)}, bf16[2560,1024]{1,0:T(8,128)(2,1)}, u32[]{:S(2)}) copy-start(bf16[2560,1024]{1,0:T(8,128)(2,1)} %refs_18_.3) | copy-start | bytes 15728644
  10.6 13.2 %copy-start.4 = (bf16[2560,1024]{1,0:T(8,128)(2,1)S(1)}, bf16[2560,1024]{1,0:T(8,128)(2,1)}, u32[]{:S(2)}) copy-start(bf16[2560,1024]{1,0:T(8,128)(2,1)} %refs_18_.3) | copy-start | bytes 15728644
  18.6 3.4 %collective-permute-start.3 = (bf16[128,2560]{1,0:T(8,128)(2,1)S(1)}, bf16[128,2560]{1,0:T(8,128)(2,1)S(1)}, u32[]{:S(2)}, u32[]{:S(2)}) collective-permute-start(bf16[128,2560]{1,0:T(8,128)(2,1)S(1)} %collective-permute-done.refs_1_), channel_id=1, source_target_pairs={{0,1},{1,0},{2,3},{3,2},{4,5},{5,4},{6,7},{7,6},{8,9},{9,8},{10,11... | collective-permute-start | bytes 1966088 | tf_op jit(solution)/shard_map/ppermute | solution.py:56
  19.2 8.3 %collective-permute-start.4 = (bf16[128,512]{1,0:T(8,128)(2,1)S(1)}, bf16[128,512]{1,0:T(8,128)(2,1)S(1)}, u32[]{:S(2)}, u32[]{:S(2)}) collective-permute-start(bf16[128,512]{1,0:T(8,128)(2,1)S(1)} %get-tuple-element.93), channel_id=1, source_target_pairs={{0,2},{1,3},{2,0},{3,1},{4,6},{5,7},{6,4},{7,5},{8,10},{9,11},{10,... | collective-permute-start | bytes 393224 | tf_op jit(solution)/shard_map/ppermute | solution.py:56
  21.0 8.1 %collective-permute-start.5 = (bf16[128,512]{1,0:T(8,128)(2,1)S(1)}, bf16[128,512]{1,0:T(8,128)(2,1)S(1)}, u32[]{:S(2)}, u32[]{:S(2)}) collective-permute-start(bf16[128,512]{1,0:T(8,128)(2,1)S(1)} %get-tuple-element.94), channel_id=1, source_target_pairs={{0,3},{1,2},{2,1},{3,0},{4,7},{5,6},{6,5},{7,4},{8,11},{9,10},{10,... | collective-permute-start | bytes 393224 | tf_op jit(solution)/shard_map/ppermute | solution.py:56
  21.2 8.4 %collective-permute-start.6 = (bf16[128,512]{1,0:T(8,128)(2,1)S(1)}, bf16[128,512]{1,0:T(8,128)(2,1)S(1)}, u32[]{:S(2)}, u32[]{:S(2)}) collective-permute-start(bf16[128,512]{1,0:T(8,128)(2,1)S(1)} %get-tuple-element.99), channel_id=1, source_target_pairs={{0,1},{1,0},{2,3},{3,2},{4,5},{5,4},{6,7},{7,6},{8,9},{9,8},{10,11... | collective-permute-start | bytes 393224 | tf_op jit(solution)/shard_map/ppermute | solution.py:56
  21.4 14.6 %collective-permute-start.8 = (bf16[128,512]{1,0:T(8,128)(2,1)S(1)}, bf16[128,512]{1,0:T(8,128)(2,1)S(1)}, u32[]{:S(2)}, u32[]{:S(2)}) collective-permute-start(bf16[128,512]{1,0:T(8,128)(2,1)S(1)} %get-tuple-element.102), channel_id=1, source_target_pairs={{0,1},{1,0},{2,3},{3,2},{4,5},{5,4},{6,7},{7,6},{8,9},{9,8},{10,11... | collective-permute-start | bytes 393224 | tf_op jit(solution)/shard_map/ppermute | solution.py:56
  22.0 11.7 %collective-permute-start.11 = (bf16[1280,128]{1,0:T(8,128)(2,1)S(1)}, bf16[1280,128]{1,0:T(8,128)(2,1)S(1)}, u32[]{:S(2)}, u32[]{:S(2)}) collective-permute-start(bf16[1280,128]{1,0:T(8,128)(2,1)S(1)} %get-tuple-element.106), channel_id=1, source_target_pairs={{0,8},{4,12},{8,0},{12,4},{16,24},{20,28},{24,16},{28,20},{1,9},{5... | collective-permute-start | bytes 983048 | tf_op jit(solution)/shard_map/ppermute | solution.py:56
  27.6 9.1 %collective-permute-start.9 = (bf16[128,512]{1,0:T(8,128)(2,1)S(1)}, bf16[128,512]{1,0:T(8,128)(2,1)S(1)}, u32[]{:S(2)}, u32[]{:S(2)}) collective-permute-start(bf16[128,512]{1,0:T(8,128)(2,1)S(1)} %get-tuple-element.103), channel_id=1, source_target_pairs={{0,2},{1,3},{2,0},{3,1},{4,6},{5,7},{6,4},{7,5},{8,10},{9,11},{10,... | collective-permute-start | bytes 393224 | tf_op jit(solution)/shard_map/ppermute | solution.py:56
  29.1 8.0 %collective-permute-start.10 = (bf16[128,512]{1,0:T(8,128)(2,1)S(1)}, bf16[128,512]{1,0:T(8,128)(2,1)S(1)}, u32[]{:S(2)}, u32[]{:S(2)}) collective-permute-start(bf16[128,512]{1,0:T(8,128)(2,1)S(1)} %get-tuple-element.104), channel_id=1, source_target_pairs={{0,3},{1,2},{2,1},{3,0},{4,7},{5,6},{6,5},{7,4},{8,11},{9,10},{10,... | collective-permute-start | bytes 393224 | tf_op jit(solution)/shard_map/ppermute | solution.py:56
  32.0 9.2 %collective-permute-start.7 = (bf16[512,256]{1,0:T(8,128)(2,1)S(1)}, bf16[512,256]{1,0:T(8,128)(2,1)S(1)}, u32[]{:S(2)}, u32[]{:S(2)}) collective-permute-start(bf16[512,256]{1,0:T(8,128)(2,1)S(1)} %get-tuple-element.100.refs_10_.refs_13_.refs_14_), channel_id=1, source_target_pairs={{0,8},{4,12},{8,0},{12,4},{16,24},{20,28},{24,16},{28,20},{1,9},{5... | collective-permute-start | bytes 786440 | tf_op jit(solution)/shard_map/ppermute | solution.py:56
  33.6 11.6 %collective-permute-start.12 = (bf16[1280,128]{1,0:T(8,128)(2,1)S(1)}, bf16[1280,128]{1,0:T(8,128)(2,1)S(1)}, u32[]{:S(2)}, u32[]{:S(2)}) collective-permute-start(bf16[1280,128]{1,0:T(8,128)(2,1)S(1)} %collective-permute-done.1.refs_6_.refs_7_.refs_8_), channel_id=1, source_target_pairs={{0,1},{1,0},{2,3},{3,2},{4,5},{5,4},{6,7},{7,6},{8,9},{9,8},{10,11... | collective-permute-start | bytes 983048 | tf_op jit(solution)/shard_map/ppermute | solution.py:56
  36.0 9.2 %collective-permute-start.13 = (bf16[1280,128]{1,0:T(8,128)(2,1)S(1)}, bf16[1280,128]{1,0:T(8,128)(2,1)S(1)}, u32[]{:S(2)}, u32[]{:S(2)}) collective-permute-start(bf16[1280,128]{1,0:T(8,128)(2,1)S(1)} %collective-permute-done.11.refs_8_.refs_9_.refs_10_), channel_id=1, source_target_pairs={{0,1},{1,0},{2,3},{3,2},{4,5},{5,4},{6,7},{7,6},{8,9},{9,8},{10,11... | collective-permute-start | bytes 983048 | tf_op jit(solution)/shard_map/ppermute | solution.py:56
  36.6 11.1 %collective-permute-start.14 = (bf16[512,256]{1,0:T(8,128)(2,1)S(1)}, bf16[512,256]{1,0:T(8,128)(2,1)S(1)}, u32[]{:S(2)}, u32[]{:S(2)}) collective-permute-start(bf16[512,256]{1,0:T(8,128)(2,1)S(1)} %get-tuple-element.119.refs_10_.refs_14_.refs_15_), channel_id=1, source_target_pairs={{0,8},{4,12},{8,0},{12,4},{16,24},{20,28},{24,16},{28,20},{1,9},{5... | collective-permute-start | bytes 786440 | tf_op jit(solution)/shard_map/ppermute | solution.py:56
  43.6 13.8 %collective-permute-start.16 = (bf16[512,256]{1,0:T(8,128)(2,1)S(1)}, bf16[512,256]{1,0:T(8,128)(2,1)S(1)}, u32[]{:S(2)}, u32[]{:S(2)}) collective-permute-start(bf16[512,256]{1,0:T(8,128)(2,1)S(1)} %get-tuple-element.125.refs_11_.refs_15_.refs_16_), channel_id=1, source_target_pairs={{0,8},{4,12},{8,0},{12,4},{16,24},{20,28},{24,16},{28,20},{1,9},{5... | collective-permute-start | bytes 786440 | tf_op jit(solution)/shard_map/ppermute | solution.py:56
  46.1 8.5 %collective-permute-start.15 = (bf16[640,256]{1,0:T(8,128)(2,1)S(1)}, bf16[640,256]{1,0:T(8,128)(2,1)S(1)}, u32[]{:S(2)}, u32[]{:S(2)}) collective-permute-start(bf16[640,256]{1,0:T(8,128)(2,1)S(1)} %get-tuple-element.123), channel_id=1, source_target_pairs={{0,4},{4,0},{8,12},{12,8},{16,20},{20,16},{24,28},{28,24},{1,5},{5... | collective-permute-start | bytes 983048 | tf_op jit(solution)/shard_map/ppermute | solution.py:56
  50.6 17.9 %collective-permute-start.19 = (bf16[512,512]{1,0:T(8,128)(2,1)S(1)}, bf16[512,512]{1,0:T(8,128)(2,1)S(1)}, u32[]{:S(2)}, u32[]{:S(2)}) collective-permute-start(bf16[512,512]{1,0:T(8,128)(2,1)S(1)} %attention.7.refs_0_.refs_16_.refs_12_.refs_17_), channel_id=1, source_target_pairs={{0,8},{4,12},{8,0},{12,4},{16,24},{20,28},{24,16},{28,20},{1,9},{5... | collective-permute-start | bytes 1572872 | tf_op jit(solution)/shard_map/ppermute | solution.py:56
  52.2 10.6 %collective-permute-start.17 = (bf16[640,256]{1,0:T(8,128)(2,1)S(1)}, bf16[640,256]{1,0:T(8,128)(2,1)S(1)}, u32[]{:S(2)}, u32[]{:S(2)}) collective-permute-start(bf16[640,256]{1,0:T(8,128)(2,1)S(1)} %get-tuple-element.127), channel_id=1, source_target_pairs={{0,4},{4,0},{8,12},{12,8},{16,20},{20,16},{24,28},{28,24},{1,5},{5... | collective-permute-start | bytes 983048 | tf_op jit(solution)/shard_map/ppermute | solution.py:56
  54.7 12.5 %collective-permute-start.18 = (bf16[320,256]{1,0:T(8,128)(2,1)S(1)}, bf16[320,256]{1,0:T(8,128)(2,1)S(1)}, u32[]{:S(2)}, u32[]{:S(2)}) collective-permute-start(bf16[320,256]{1,0:T(8,128)(2,1)S(1)} %get-tuple-element.129), channel_id=1, source_target_pairs={{0,16},{4,20},{8,24},{12,28},{16,0},{20,4},{24,8},{28,12},{1,17},{... | collective-permute-start | bytes 491528 | tf_op jit(solution)/shard_map/ppermute | solution.py:56
  61.2 12.5 %collective-permute-start.20 = (bf16[640,256]{1,0:T(8,128)(2,1)S(1)}, bf16[640,256]{1,0:T(8,128)(2,1)S(1)}, u32[]{:S(2)}, u32[]{:S(2)}) collective-permute-start(bf16[640,256]{1,0:T(8,128)(2,1)S(1)} %get-tuple-element.131), channel_id=1, source_target_pairs={{0,4},{4,0},{8,12},{12,8},{16,20},{20,16},{24,28},{28,24},{1,5},{5... | collective-permute-start | bytes 983048 | tf_op jit(solution)/shard_map/ppermute | solution.py:56
  62.8 13.2 %collective-permute-start.21 = (bf16[320,256]{1,0:T(8,128)(2,1)S(1)}, bf16[320,256]{1,0:T(8,128)(2,1)S(1)}, u32[]{:S(2)}, u32[]{:S(2)}) collective-permute-start(bf16[320,256]{1,0:T(8,128)(2,1)S(1)} %get-tuple-element.133), channel_id=1, source_target_pairs={{0,16},{4,20},{8,24},{12,28},{16,0},{20,4},{24,8},{28,12},{1,17},{... | collective-permute-start | bytes 491528 | tf_op jit(solution)/shard_map/ppermute | solution.py:56
  65.6 11.8 %collective-permute-start.22 = (bf16[256,1280]{1,0:T(8,128)(2,1)S(1)}, bf16[256,1280]{1,0:T(8,128)(2,1)S(1)}, u32[]{:S(2)}, u32[]{:S(2)}) collective-permute-start(bf16[256,1280]{1,0:T(8,128)(2,1)S(1)} %get-tuple-element.136), channel_id=1, source_target_pairs={{0,1},{1,0},{2,3},{3,2},{4,5},{5,4},{6,7},{7,6},{8,9},{9,8},{10,11... | collective-permute-start | bytes 1966088 | tf_op jit(solution)/shard_map/ppermute | solution.py:56
  72.1 6.3 %collective-permute-start.23 = (bf16[256,1280]{1,0:T(8,128)(2,1)S(1)}, bf16[256,1280]{1,0:T(8,128)(2,1)S(1)}, u32[]{:S(2)}, u32[]{:S(2)}) collective-permute-start(bf16[256,1280]{1,0:T(8,128)(2,1)S(1)} %get-tuple-element.139), channel_id=1, source_target_pairs={{0,1},{1,0},{2,3},{3,2},{4,5},{5,4},{6,7},{7,6},{8,9},{9,8},{10,11... | collective-permute-start | bytes 1966088 | tf_op jit(solution)/shard_map/ppermute | solution.py:56
  72.2 10.6 %collective-permute-start.26 = (bf16[640,256]{1,0:T(8,128)(2,1)S(1)}, bf16[640,256]{1,0:T(8,128)(2,1)S(1)}, u32[]{:S(2)}, u32[]{:S(2)}) collective-permute-start(bf16[640,256]{1,0:T(8,128)(2,1)S(1)} %get-tuple-element.145), channel_id=1, source_target_pairs={{0,4},{4,0},{8,12},{12,8},{16,20},{20,16},{24,28},{28,24},{1,5},{5... | collective-permute-start | bytes 983048 | tf_op jit(solution)/shard_map/ppermute | solution.py:56
  73.7 11.3 %collective-permute-start.27 = (bf16[320,256]{1,0:T(8,128)(2,1)S(1)}, bf16[320,256]{1,0:T(8,128)(2,1)S(1)}, u32[]{:S(2)}, u32[]{:S(2)}) collective-permute-start(bf16[320,256]{1,0:T(8,128)(2,1)S(1)} %get-tuple-element.147), channel_id=1, source_target_pairs={{0,16},{4,20},{8,24},{12,28},{16,0},{20,4},{24,8},{28,12},{1,17},{... | collective-permute-start | bytes 491528 | tf_op jit(solution)/shard_map/ppermute | solution.py:56
  76.8 12.5 %collective-permute-start.29 = (bf16[640,256]{1,0:T(8,128)(2,1)S(1)}, bf16[640,256]{1,0:T(8,128)(2,1)S(1)}, u32[]{:S(2)}, u32[]{:S(2)}) collective-permute-start(bf16[640,256]{1,0:T(8,128)(2,1)S(1)} %get-tuple-element.151), channel_id=1, source_target_pairs={{0,4},{4,0},{8,12},{12,8},{16,20},{20,16},{24,28},{28,24},{1,5},{5... | collective-permute-start | bytes 983048 | tf_op jit(solution)/shard_map/ppermute | solution.py:56
  77.6 14.0 %collective-permute-start.24 = (bf16[128,1280]{1,0:T(8,128)(2,1)S(1)}, bf16[128,1280]{1,0:T(8,128)(2,1)S(1)}, u32[]{:S(2)}, u32[]{:S(2)}) collective-permute-start(bf16[128,1280]{1,0:T(8,128)(2,1)S(1)} %get-tuple-element.141), channel_id=1, source_target_pairs={{0,2},{1,3},{2,0},{3,1},{4,6},{5,7},{6,4},{7,5},{8,10},{9,11},{10,... | collective-permute-start | bytes 983048 | tf_op jit(solution)/shard_map/ppermute | solution.py:56
  78.5 15.4 %collective-permute-start.25 = (bf16[128,1280]{1,0:T(8,128)(2,1)S(1)}, bf16[128,1280]{1,0:T(8,128)(2,1)S(1)}, u32[]{:S(2)}, u32[]{:S(2)}) collective-permute-start(bf16[128,1280]{1,0:T(8,128)(2,1)S(1)} %get-tuple-element.142), channel_id=1, source_target_pairs={{0,2},{1,3},{2,0},{3,1},{4,6},{5,7},{6,4},{7,5},{8,10},{9,11},{10,... | collective-permute-start | bytes 983048 | tf_op jit(solution)/shard_map/ppermute | solution.py:56
  82.8 12.0 %collective-permute-start.28 = (bf16[320,256]{1,0:T(8,128)(2,1)S(1)}, bf16[320,256]{1,0:T(8,128)(2,1)S(1)}, u32[]{:S(2)}, u32[]{:S(2)}) collective-permute-start(bf16[320,256]{1,0:T(8,128)(2,1)S(1)} %get-tuple-element.148), channel_id=1, source_target_pairs={{0,16},{4,20},{8,24},{12,28},{16,0},{20,4},{24,8},{28,12},{1,17},{... | collective-permute-start | bytes 491528 | tf_op jit(solution)/shard_map/ppermute | solution.py:56
  89.4 10.2 %collective-permute-start.30 = (bf16[320,256]{1,0:T(8,128)(2,1)S(1)}, bf16[320,256]{1,0:T(8,128)(2,1)S(1)}, u32[]{:S(2)}, u32[]{:S(2)}) collective-permute-start(bf16[320,256]{1,0:T(8,128)(2,1)S(1)} %get-tuple-element.153), channel_id=1, source_target_pairs={{0,16},{4,20},{8,24},{12,28},{16,0},{20,4},{24,8},{28,12},{1,17},{... | collective-permute-start | bytes 491528 | tf_op jit(solution)/shard_map/ppermute | solution.py:56
